TPU v7x, 128 devices: a whole 4x4x4 slice. The times are simulated.
128 devices in a mesh: orb: 32 (over y, x, core), fit: 4 (over z).
Axes of the slice: x: 4, y: 4, z: 4, core: 2. Of those that a mesh axis runs over, the one named last changes fastest.
Arguments:
- blocks: bfloat16 [128, 512, 2048], P('orb', None, 'fit'), may hold values from -1 to 1
- occ_energy: float32 [128], replicated, may hold values from -1.2 to -0.3
- virt_energy: float32 [128, 512], replicated, may hold values from 0.2 to 4
- domains: int32 [128], replicated, may hold values from 128 to 512, as said below
- pairs: int32 [512, 2], P('orb'), may hold values from 0 to 127, as said below
Outputs:
- gamma: float32 [128, 512, 2048], P('orb', None, 'fit')
- density: float32 [128, 512, 512], P('orb', None, 'fit')
Inputs may be any that keep to these rules, and one draw needn't show every extreme that they name: `domains`: multiples of 128; some orbital has domain 512 and some has 128. Rows d * 16 to (d + 1) * 16 - 1 are the pairs of the d-th index of orb: their i lies in d * 4 to (d + 1) * 4 - 1. Within them, rows 2g and 2g + 1 have the same j and different i, and the 8 values j // 4 of these groups are all different. One index of orb is among these values for every index of orb.
All inputs are finite; a program needn't handle non-finite values.
Results may differ from a plain program's by a relative error of at most 0.02.
Values may be sent and summed in bfloat16 or wider, within the bound.
No kernel may reach another device: no remote copies, remote signals or barrier semaphores. Data moves between devices by JAX's collectives and lax.ppermute only.
A program may use at most 192 MiB of HBM per device.

v0:
```python
import jax
import jax.numpy as jnp
from jax import lax
from jax.sharding import PartitionSpec as P


def make_amplitudes(integrals, energy_rows, energy_right, occ_sum, dom_left, dom_right):
    row_count = integrals.shape[1]
    col_count = integrals.shape[2]
    row_pos = jnp.arange(row_count, dtype=jnp.int32)
    col_pos = jnp.arange(col_count, dtype=jnp.int32)
    keep = (row_pos[None, :, None] < dom_left[:, None, None]) & (
        col_pos[None, None, :] < dom_right[:, None, None]
    )
    denominators = energy_rows[:, :, None] + energy_right[:, None, :] - occ_sum[:, None, None]
    values = jnp.where(keep, -integrals / denominators, jnp.zeros((), jnp.float32))
    return values.astype(jnp.bfloat16)


def on_device(blocks, occ_energy, virt_energy, domains, pairs):
    peer_count = lax.axis_size("orb")
    my_index = lax.axis_index("orb")
    fit_count = lax.axis_size("fit")
    fit_index = lax.axis_index("fit")
    orb_count = blocks.shape[0]
    virt_count = blocks.shape[1]
    aux_count = blocks.shape[2]
    first_orb = pairs[:, 0]
    second_orb = pairs[:, 1]
    local_left = first_orb - my_index * orb_count
    owner_dev = second_orb // orb_count
    local_right = second_orb - owner_dev * orb_count
    peer_ids = jnp.arange(peer_count, dtype=jnp.int32)
    slot_match = owner_dev[None, :] == peer_ids[:, None]
    local_ids = jnp.arange(orb_count, dtype=jnp.int32)
    needed_here = jnp.max(jnp.where(slot_match, local_right[None, :], -1), axis=1)
    wanted = lax.all_to_all(needed_here, "orb", split_axis=0, concat_axis=0, tiled=True)
    pick_rows = wanted[:, None] == local_ids[None, :]
    send_blocks = jnp.einsum(
        "ok,kva->ova", pick_rows.astype(jnp.bfloat16), blocks, preferred_element_type=jnp.float32
    ).astype(jnp.bfloat16)
    recv_blocks = lax.all_to_all(send_blocks, "orb", split_axis=0, concat_axis=0, tiled=True)
    right_blocks = jnp.take(recv_blocks, owner_dev, axis=0)
    energy_right = jnp.take(virt_energy, second_orb, axis=0)
    left_blocks = jnp.take(blocks, local_left, axis=0)
    energy_left = jnp.take(virt_energy, first_orb, axis=0)
    occ_sum = jnp.take(occ_energy, first_orb) + jnp.take(occ_energy, second_orb)
    dom_left = jnp.take(domains, first_orb)
    dom_right = jnp.take(domains, second_orb)
    partial_value = jnp.einsum(
        "pva,pwa->pvw", left_blocks, right_blocks, preferred_element_type=jnp.float32
    ).astype(jnp.bfloat16)
    partial_value = lax.optimization_barrier(partial_value).astype(jnp.float32)
    integrals = lax.psum(partial_value.astype(jnp.bfloat16), "fit").astype(jnp.float32)
    amplitudes = make_amplitudes(integrals, energy_left, energy_right, occ_sum, dom_left, dom_right)
    owner_rows = (local_left[None, :] == local_ids[:, None]).astype(jnp.float32)
    own_terms = jnp.einsum(
        "pab,pbc->pac", amplitudes, right_blocks, preferred_element_type=jnp.float32
    )
    gamma_own = jnp.einsum("kp,pac->kac", owner_rows, own_terms, precision=lax.Precision.HIGHEST)
    back_terms = jnp.einsum(
        "pab,pac->pbc", amplitudes, left_blocks, preferred_element_type=jnp.float32
    )
    group_sums = back_terms.reshape(-1, 2, virt_count, aux_count).sum(axis=1).astype(jnp.bfloat16)
    group_owner = owner_dev.reshape(-1, 2)[:, 0]
    group_match = (group_owner[None, :] == peer_ids[:, None]).astype(jnp.bfloat16)
    send_back = jnp.einsum(
        "os,sbc->obc", group_match, group_sums, preferred_element_type=jnp.float32
    ).astype(jnp.bfloat16)
    returned = lax.all_to_all(send_back, "orb", split_axis=0, concat_axis=0, tiled=True)
    gamma = gamma_own + jnp.einsum(
        "ok,obc->kbc", pick_rows.astype(jnp.bfloat16), returned, preferred_element_type=jnp.float32
    )
    cols_fit = virt_count // fit_count
    amp_slice = lax.dynamic_slice_in_dim(amplitudes, fit_index * cols_fit, cols_fit, 1)
    dens_terms = jnp.einsum(
        "pab,pcb->pac", amplitudes, amp_slice, preferred_element_type=jnp.float32
    )
    density = jnp.einsum("kp,pac->kac", owner_rows, dens_terms, precision=lax.Precision.HIGHEST)
    return (gamma, density)


def solution(mesh):
    placed = (P("orb", None, "fit"), P(), P(), P(), P("orb", None))
    return jax.shard_map(
        on_device,
        mesh=mesh,
        in_specs=placed,
        out_specs=(P("orb", None, "fit"), P("orb", None, "fit")),
        check_vma=False,
    )
```

profile of v0, /device:TPU:1, one launch (start us, length us, event | category | flops | bytes accessed | tf_op | source)
XLA Modules:
  0.0 753.4 jit_solution(3847465387147543581)
XLA Ops:
  7.2 0.0 copy-start
  7.2 0.9 bitcast_subtract_fusion
  8.0 0.1 select_reduce_fusion
  8.1 0.1 copy.50
  8.2 15.3 %all_to_all.19 = s32[32,1,1]{2,1,0:T(1,128)S(1)} all-to-all(s32[32,1,1]{2,1,0:T(1,128)S(1)} %copy.50), channel_id=1, replica_groups=mesh['orb'=32,'fit'=4] {'orb'}, dimensions={0} | all-to-all | bytes 256 | tf_op jit(solution)/shard_map/all_to_all | solution.py:37
  23.5 0.7 reduce
  24.2 0.0 copy-done
  24.2 8.2 %convolution_convert_fusion.1 = bf16[32,512,512]{2,0,1:T(8,128)(2,1)} fusion(bf16[4,512,512]{2,1,0:T(8,128)(2,1)S(1)} %copy-done, s32[32]{0:T(128)S(1)} %reduce), kind=kOutput, calls=%fused_computation.15 | convolution fusion | flops 75497600 | bytes 18874496 | tf_op jit(solution)/shard_map/ok,kva->ova/dot_general | solution.py:39
  32.4 16.8 %copy.52 = bf16[32,512,512]{2,1,0:T(8,128)(2,1)} copy(bf16[32,512,512]{2,0,1:T(8,128)(2,1)} %convolution_convert_fusion.1) | data formatting | bytes 33554432 | tf_op jit(solution)/shard_map/convert_element_type | solution.py:41
  49.2 0.0 copy-start.5
  49.2 5.5 all-to-all-start.1
  54.7 0.6 all-reduce.2.cloned.1.call-start
  55.3 0.0 copy-done.5
  55.3 4.7 gather_fusion
  60.1 196.2 %all-to-all-done.1 = bf16[32,512,512]{2,1,0:T(8,128)(2,1)} async-done(((bf16[32,512,512]{2,1,0:T(8,128)(2,1)}), bf16[32,512,512]{2,1,0:T(8,128)(2,1)}, u32[]{:S(2)}, u32[]{:S(2)}) %all-to-all-start.1) | async-done | bytes 16777248 | tf_op jit(solution)/shard_map/all_to_all | solution.py:42
  256.2 10.5 %gather_fusion.1 = bf16[16,512,512]{2,1,0:T(8,128)(2,1)} fusion(bf16[32,512,512]{2,1,0:T(8,128)(2,1)} %all-to-all-done.1, s32[1024]{0:T(1024)S(1)} %pad_clamp_fusion), kind=kCustom, calls=%fused_computation.7 | custom fusion | bytes 16777280 | tf_op jit(solution)/shard_map/jit(_take)/gather | solution.py:43
  266.8 11.6 %convolution_convert_fusion.2 = bf16[16,512,512]{2,1,0:T(8,128)(2,1)} fusion(bf16[16,512,512]{2,1,0:T(8,128)(2,1)} %gather_fusion, pred[16]{0:T(512)(128)(4,1)S(1)} %get-tuple-element.30, bf16[16,512,512]{2,1,0:T(8,128)(2,1)} %gather_fusion.1, pred[16]{0:T(512)(128)(4,1)S(1)} %get-tuple-element.21), kind=kOutput, calls=%fused_computation.18 | convolution fusion | flops 4307550208 | bytes 25165856 | tf_op jit(solution)/shard_map/pva,pwa->pvw/dot_general | solution.py:50
  278.3 0.0 copy-start.2
  278.3 0.0 copy-start.4
  278.3 0.0 copy-start.3
  278.3 0.0 all-reduce.2.cloned.1.call-update
  278.4 0.6 copy-done.2
  279.0 0.7 gather_fusion.7
  279.6 0.7 gather_fusion.6
  280.3 0.0 copy-done.4
  280.3 0.6 gather_fusion.5
  280.9 0.6 gather_fusion.4
  281.5 0.0 copy-done.3
  281.5 0.7 gather_fusion.3
  282.1 0.7 gather_fusion.2
  282.8 0.1 squeeze.10
  282.9 0.1 slice_reduce_fusion
  283.1 0.1 iota_compare_fusion
  283.1 0.1 iota_compare_fusion.1
  283.2 0.1 broadcast_select_fusion.8
  283.3 164.8 %all-reduce.2.cloned.1.call-done = bf16[16,512,512]{2,1,0:T(8,128)(2,1)} async-done(((bf16[16,512,512]{2,1,0:T(8,128)(2,1)}), bf16[16,512,512]{2,1,0:T(8,128)(2,1)}) %all-reduce.2.cloned.1.call-update) | async-done | bytes 8388624 | tf_op jit(solution)/shard_map/psum | solution.py:54
  448.1 8.4 %select_convert_fusion = bf16[16,512,512]{2,1,0:T(8,128)(2,1)} fusion(bf16[16,512,512]{2,1,0:T(8,128)(2,1)} %all-reduce.2.cloned.1.call-done, f32[16]{0:T(128)S(1)} %select_add_fusion, f32[16,512]{1,0:T(8,128)S(1)} %get-tuple-element.32, f32[16,512]{1,0:T(8,128)S(1)} %get-tuple-element.33, pred[16,512]{1,0:T(8,128)(4,1)S(1)} %iota_compare_fusion, ...), kind=kLoop, calls=%fused_computation.13 | loop fusion | flops 33554432 | bytes 16859200 | tf_op jit(solution)/shard_map/convert_element_type | solution.py:17
  456.6 12.6 %bitcast_reduce_fusion = bf16[8,512,512]{2,1,0:T(8,128)(2,1)} fusion(bf16[16,512,512]{2,1,0:T(8,128)(2,1)} %select_convert_fusion, bf16[16,512,512]{2,1,0:T(8,128)(2,1)} %gather_fusion, pred[16]{0:T(512)(128)(4,1)S(1)} %get-tuple-element.30), kind=kOutput, calls=%fused_computation.8 | convolution fusion | flops 4301258752 | bytes 20971536 | tf_op jit(solution)/shard_map/pab,pac->pbc/dot_general | solution.py:61
  469.1 9.9 %convolution_convert_fusion = bf16[32,512,512]{2,0,1:T(8,128)(2,1)} fusion(bf16[8,512,512]{2,1,0:T(8,128)(2,1)} %bitcast_reduce_fusion, s32[8]{0:T(128)S(1)} %slice_reduce_fusion), kind=kOutput, calls=%fused_computation.14 | convolution fusion | flops 142606592 | bytes 20971552 | tf_op jit(solution)/shard_map/os,sbc->obc/dot_general | solution.py:67
  479.0 16.8 %copy.56 = bf16[32,512,512]{2,1,0:T(8,128)(2,1)} copy(bf16[32,512,512]{2,0,1:T(8,128)(2,1)} %convolution_convert_fusion) | data formatting | bytes 33554432 | tf_op jit(solution)/shard_map/convert_element_type | solution.py:69
  495.8 7.8 %all-to-all-start.2 = ((bf16[32,512,512]{2,1,0:T(8,128)(2,1)}), bf16[32,512,512]{2,1,0:T(8,128)(2,1)}, u32[]{:S(2)}, u32[]{:S(2)}) async-start(bf16[32,512,512]{2,1,0:T(8,128)(2,1)} %copy.56), calls=%async_computation.2 | async-start | bytes 33554432 | tf_op jit(solution)/shard_map/all_to_all | solution.py:70
  503.6 6.3 fusion.10
  509.9 3.9 fusion.4
  513.8 1.0 copy.60
  514.8 16.1 %fusion.8 = f32[16,512,512]{2,1,0:T(8,128)} fusion(bf16[16,512,512]{2,1,0:T(8,128)(2,1)} %select_convert_fusion, bf16[16,512,512]{2,1,0:T(8,128)(2,1)} %gather_fusion.1, pred[16]{0:T(512)(128)(4,1)S(1)} %get-tuple-element.21), kind=kOutput, calls=%fused_computation.23 | convolution fusion | flops 4299161600 | bytes 33554448 | tf_op jit(solution)/shard_map/pab,pbc->pac/dot_general | solution.py:57
  530.9 174.4 %all-to-all-done.2 = bf16[32,512,512]{2,1,0:T(8,128)(2,1)} async-done(((bf16[32,512,512]{2,1,0:T(8,128)(2,1)}), bf16[32,512,512]{2,1,0:T(8,128)(2,1)}, u32[]{:S(2)}, u32[]{:S(2)}) %all-to-all-start.2) | async-done | bytes 16777248 | tf_op jit(solution)/shard_map/all_to_all | solution.py:70
  705.4 15.4 %fusion = f32[4,512,512]{2,0,1:T(4,128)S(1)} fusion(bf16[32,512,512]{2,1,0:T(8,128)(2,1)} %all-to-all-done.2, s32[32]{0:T(128)S(1)} %reduce), kind=kOutput, calls=%fused_computation.9 | convolution fusion | flops 67108992 | bytes 20971648 | tf_op jit(solution)/shard_map/ok,obc->kbc/dot_general | solution.py:71
  720.7 0.0 copy-start.1
  720.7 22.3 %fusion.12 = f32[4,512,512]{2,0,1:T(4,128)S(1)} fusion(f32[4,512,512]{2,0,1:T(4,128)S(1)} %fusion, f32[16,512,512]{2,1,0:T(8,128)} %fusion.8, s32[16]{0:T(128)S(1)} %get-tuple-element.27), kind=kOutput, calls=%fused_computation.27 | convolution fusion | flops 202375232 | bytes 25165888 | tf_op jit(solution)/shard_map/kp,pac->kac/dot_general | solution.py:60
  743.0 3.3 copy.59
  746.3 0.0 copy-done.1
  (10 shorter events, 0.1 us)
Async XLA Ops:
  7.2 17.0 %copy-start = (bf16[4,512,512]{2,1,0:T(8,128)(2,1)S(1)}, bf16[4,512,512]{2,1,0:T(8,128)(2,1)}, u32[]{:S(2)}) copy-start(bf16[4,512,512]{2,1,0:T(8,128)(2,1)} %param.11) | copy-start | bytes 6291460
  49.2 6.1 copy-start.5
  49.2 207.0 %all-to-all-start.1 = ((bf16[32,512,512]{2,1,0:T(8,128)(2,1)}), bf16[32,512,512]{2,1,0:T(8,128)(2,1)}, u32[]{:S(2)}, u32[]{:S(2)}) async-start(bf16[32,512,512]{2,1,0:T(8,128)(2,1)} %copy.52), calls=%async_computation.1 | async-start | bytes 33554432 | tf_op jit(solution)/shard_map/all_to_all | solution.py:42
  54.7 393.4 %all-reduce.2.cloned.1.call-start = ((), (), s32[]{:S(2)}) async-start(), calls=%async_computation.3 | async-start | bytes 16777216 | tf_op jit(solution)/shard_map/psum | solution.py:54
  278.3 0.7 copy-start.2
  278.3 2.0 copy-start.4
  278.3 3.2 copy-start.3
  495.8 209.5 %all-to-all-start.2 = ((bf16[32,512,512]{2,1,0:T(8,128)(2,1)}), bf16[32,512,512]{2,1,0:T(8,128)(2,1)}, u32[]{:S(2)}, u32[]{:S(2)}) async-start(bf16[32,512,512]{2,1,0:T(8,128)(2,1)} %copy.56), calls=%async_computation.2 | async-start | bytes 33554432 | tf_op jit(solution)/shard_map/all_to_all | solution.py:70
  720.7 25.6 %copy-start.1 = (bf16[4,512,512]{2,1,0:T(8,128)(2,1)S(1)}, bf16[4,512,512]{2,1,0:T(8,128)(2,1)}, u32[]{:S(2)}) copy-start(bf16[4,512,512]{2,1,0:T(8,128)(2,1)} %param.11) | copy-start | bytes 6291460
Sparse Core Ops, SparseCore 0:
  278.5 169.6 all-reduce.1
where the time goes:
time: 768 us; the launch traced here: 753 us
  waiting for transfers between devices  535 us (70%)
  matrix products  106 us (14%)
  local copies, waits for them, and re-layouts  57.9 us (8%)
  blocking collectives  15.3 us (2%)
  between operations  14.5 us (2%)
  starting transfers between devices  13.8 us (2%)
  other arithmetic  10.4 us (1%)
    all_to_all x1, waiting for transfers between devices, on_device(): lax.all_to_all(send_blocks, 'orb', split_axis=0, concat_axis=0, tiled=True)  196 us
    all_to_all x1, waiting for transfers between devices, on_device(): lax.all_to_all(send_back, 'orb', split_axis=0, concat_axis=0, tiled=True)  174 us
    psum x1, waiting for transfers between devices, on_device(): lax.psum(partial_value.astype(jnp.bfloat16), 'fit').astype(jnp.float32)  165 us
    dot_general x1, matrix products, on_device(): jnp.einsum('kp,pac->kac', owner_rows, own_terms, precision=lax.Precision....  22.3 us
    convert_element_type x1, local copies, waits for them, and re-layouts, on_device(): send_back = jnp.einsum('os,sbc->obc', group_match, group_sums, preferred_...  16.8 us
    convert_element_type x1, local copies, waits for them, and re-layouts, on_device(): send_blocks = jnp.einsum('ok,kva->ova', pick_rows.astype(jnp.bfloat16), b...  16.8 us
    dot_general x1, matrix products, on_device(): jnp.einsum('pab,pbc->pac', amplitudes, right_blocks, preferred_element_ty...  16.1 us
    dot_general x1, matrix products, on_device(): jnp.einsum('ok,obc->kbc', pick_rows.astype(jnp.bfloat16), returned, prefe...  15.4 us
  transfers between devices with their start and end apart: 3, of which 3 were waited for; matrix products, arithmetic and copies ran while one was open for 5% of the time, Pallas kernels for 0%

commit v1 on v0

v1 whole, which is shorter than its diff:
```python
import jax
import jax.numpy as jnp
from jax import lax
from jax.experimental import pallas as pl
from jax.experimental.pallas import tpu as pltpu
from jax.sharding import PartitionSpec as P

TILE = 128
SUB = 16
CHUNKS = 2
F32 = jnp.float32
BF16 = jnp.bfloat16
VMEM_LIMIT = 56 * 1024 * 1024


def call(kernel, out_shape, args, *, scalars=0, scratch=(), flops=0, name=None):
    outs = out_shape if isinstance(out_shape, (tuple, list)) else (out_shape,)
    moved = sum(a.size * a.dtype.itemsize for a in args) + sum(
        o.size * jnp.dtype(o.dtype).itemsize for o in outs
    )
    in_specs = [pl.BlockSpec(memory_space=pltpu.SMEM)] * scalars + [
        pl.BlockSpec(memory_space=pltpu.VMEM)
    ] * (len(args) - scalars)
    specs = [pl.BlockSpec(memory_space=pltpu.VMEM)] * len(outs)
    return pl.pallas_call(
        kernel,
        out_shape=out_shape,
        in_specs=in_specs,
        out_specs=specs if isinstance(out_shape, (tuple, list)) else specs[0],
        scratch_shapes=list(scratch),
        compiler_params=pltpu.CompilerParams(vmem_limit_bytes=VMEM_LIMIT),
        cost_estimate=pl.CostEstimate(flops=flops, bytes_accessed=moved, transcendentals=0),
        name=name,
    )(*args)


def sds(shape, dtype):
    return jax.ShapeDtypeStruct(shape, dtype)


def pack_blocks(blocks, info, peers):
    orbs, virt, aux = blocks.shape
    tiles, cols = virt // TILE, aux // 128

    def kernel(blocks_ref, info_ref, out_ref):
        for m in range(peers):
            r, c = divmod(m, cols)
            for k in range(orbs):
                for t in range(tiles):
                    out_ref[m, k * tiles + t] = blocks_ref[
                        k, t * TILE + r * SUB : t * TILE + (r + 1) * SUB, c * 128 : (c + 1) * 128
                    ]
            out_ref[m, orbs * tiles] = info_ref[...]

    return call(kernel, sds((peers, orbs * tiles + 1, SUB, 128), BF16), (blocks, info), name="pack_blocks")


def pick_pieces(wanted, held, first, count, tiles, orbs):
    peers = held.shape[0]

    def kernel(wanted_ref, held_ref, out_ref):
        @pl.loop(0, peers)
        def _(d):
            for g in range(count):
                j = wanted_ref[d, first + g]
                out_ref[d, g * tiles : (g + 1) * tiles] = held_ref[
                    j // orbs, pl.ds((j % orbs) * tiles, tiles)
                ]

    return call(
        kernel, sds((peers, count * tiles, SUB, 128), BF16), (wanted, held), scalars=1, name="pick_pieces"
    )


def assemble_right(right_ref, pieces_ref, g, tiles, cols):
    peers = pieces_ref.shape[0]
    for t in range(tiles):
        for m in range(peers):
            r, c = divmod(m, cols)
            right_ref[t * TILE + r * SUB : t * TILE + (r + 1) * SUB, c * 128 : (c + 1) * 128] = pieces_ref[
                m, g * tiles + t
            ]


def partial_integrals(where, pairs_at, slots, pieces, blocks, room, fits):
    orbs, virt, aux = blocks.shape
    tiles, cols = virt // TILE, aux // 128
    groups = pieces.shape[1] // tiles
    rows = TILE // fits
    half = rows // 2
    wide = 2 * TILE

    def kernel(where_ref, left_ref, slot_ref, pieces_ref, blocks_ref, own_ref, up_ref, down_ref, up0_ref, down1_ref, right_ref, part_ref):
        f = where_ref[0]
        at = [pl.multiple_of(((f + k) % fits) * rows, rows) for k in range(fits)]

        @pl.loop(0, groups)
        def _(g):
            assemble_right(right_ref, pieces_ref, g, tiles, cols)
            for u in range(2):
                p = 2 * g + u
                for h in reversed(range(virt // wide)):
                    left = blocks_ref[left_ref[p], h * wide : (h + 1) * wide, :]
                    part_ref[...] = lax.dot_general(
                        right_ref[...], left, (((1,), (1,)), ((), ())), preferred_element_type=F32
                    ).astype(BF16)
                    for tb in reversed(range(tiles)):
                        for v in reversed(range(2)):
                            s = slot_ref[p, tb * tiles + 2 * h + v]
                            lanes = slice(v * TILE, (v + 1) * TILE)

                            def piece(k, offset, size):
                                return part_ref[pl.ds(tb * TILE + at[k] + offset, size), lanes]

                            own_ref[s] = piece(0, 0, rows)
                            up_ref[s, 0:half] = piece(2, 0, half)
                            up_ref[s, half:rows] = piece(1, half, half)
                            down_ref[s, 0:half] = piece(3, 0, half)
                            down_ref[s, half:rows] = piece(2, half, half)
                            up0_ref[s] = piece(1, 0, half)
                            down1_ref[s] = piece(3, half, half)

    full, part = sds((room, rows, TILE), BF16), sds((room, half, TILE), BF16)
    return call(
        kernel,
        [full, full, full, part, part],
        (where, pairs_at, slots, pieces, blocks),
        scalars=3,
        scratch=[pltpu.VMEM((virt, aux), BF16), pltpu.VMEM((virt, wide), BF16)],
        flops=4 * groups * virt * virt * aux,
        name="partial_integrals",
    )


def merge_halves(up, up0, down, down1):
    half = up0.shape[1]

    def kernel(up_ref, up0_ref, down_ref, down1_ref, more_up_ref, more_down_ref):
        more_up_ref[...] = (up_ref[:, 0:half].astype(F32) + up0_ref[...].astype(F32)).astype(BF16)
        more_down_ref[...] = (down_ref[:, half:].astype(F32) + down1_ref[...].astype(F32)).astype(BF16)

    out = sds(up0.shape, BF16)
    return call(kernel, [out, out], (up, up0, down, down1), name="merge_halves")


def make_amplitudes(slots, pairs_at, own, up, down, more_up, more_down, right_level, left_level, groups):
    room, rows, _ = own.shape
    half = rows // 2
    pair_tiles = slots.shape[1]
    tiles = right_level.shape[0] // groups

    def kernel(slot_ref, left_ref, own_ref, up_ref, down_ref, mup_ref, mdown_ref, rl_ref, ll_ref, z0_ref, z1_ref):
        @pl.loop(0, groups)
        def _(g):
            for u in range(2):
                p = 2 * g + u
                k = left_ref[p]
                for tile in reversed(range(pair_tiles)):
                    tb, ta = divmod(tile, tiles)
                    s = slot_ref[p, tile]
                    level = rl_ref[g * tiles + tb] + ll_ref[k * tiles + ta]
                    low = own_ref[s, 0:half].astype(F32) + down_ref[s, 0:half].astype(F32) + mup_ref[s].astype(F32)
                    high = own_ref[s, half:].astype(F32) + up_ref[s, half:].astype(F32) + mdown_ref[s].astype(F32)
                    z0_ref[s] = (-low / level[0:half]).astype(BF16)
                    z1_ref[s] = (-high / level[half:]).astype(BF16)

    out = sds((room, half, TILE), BF16)
    return call(
        kernel,
        [out, out],
        (slots, pairs_at, own, up, down, more_up, more_down, right_level, left_level),
        scalars=2,
        name="make_amplitudes",
    )


def assemble_amplitudes(amp_ref, amps, slot_ref, keep_ref, p, at, tiles, half):
    for tb in range(tiles):
        for ta in range(tiles):
            tile = tb * tiles + ta
            s = slot_ref[p, tile]
            keep = keep_ref[p, tile] > 0
            for k, pair in enumerate(amps):
                for h, ref in enumerate(pair):
                    value = ref[s]
                    amp_ref[pl.ds(tb * TILE + at[k] + h * half, half), ta * TILE : (ta + 1) * TILE] = jnp.where(
                        keep, value, jnp.zeros_like(value)
                    )


def returned_blocks(where, pairs_at, slots, keep, amps, blocks, peers, fits):
    orbs, virt, aux = blocks.shape
    tiles, cols = virt // TILE, aux // 128
    groups = slots.shape[0] // 2
    rows = TILE // fits
    half = rows // 2
    wide = 256

    def kernel(where_ref, left_ref, slot_ref, keep_ref, *refs):
        parts = refs[: 2 * fits]
        blocks_ref, out_ref, amp0_ref, amp1_ref = refs[2 * fits :]
        f = where_ref[0]
        at = [pl.multiple_of(((f + k) % fits) * rows, rows) for k in range(fits)]
        amps = [parts[2 * k : 2 * k + 2] for k in range(fits)]

        @pl.loop(0, groups)
        def _(g):
            assemble_amplitudes(amp0_ref, amps, slot_ref, keep_ref, 2 * g, at, tiles, half)
            assemble_amplitudes(amp1_ref, amps, slot_ref, keep_ref, 2 * g + 1, at, tiles, half)
            k0, k1 = left_ref[2 * g], left_ref[2 * g + 1]
            for h in range(aux // wide):
                lanes = slice(h * wide, (h + 1) * wide)
                back = (
                    jnp.dot(amp0_ref[...], blocks_ref[k0, :, lanes], preferred_element_type=F32)
                    + jnp.dot(amp1_ref[...], blocks_ref[k1, :, lanes], preferred_element_type=F32)
                ).astype(BF16)
                for t in range(tiles):
                    for r in range(TILE // SUB):
                        for c in range(wide // 128):
                            out_ref[r * cols + h * (wide // 128) + c, g * tiles + t] = back[
                                t * TILE + r * SUB : t * TILE + (r + 1) * SUB, c * 128 : (c + 1) * 128
                            ]

    return call(
        kernel,
        sds((peers, groups * tiles, SUB, 128), BF16),
        (where, pairs_at, slots, keep, *amps, blocks),
        scalars=4,
        scratch=[pltpu.VMEM((virt, virt), BF16)] * 2,
        flops=4 * groups * virt * virt * aux,
        name="returned_blocks",
    )


def own_terms(where, pairs_at, slots, keep, amps, pieces, orbs, virt, aux, fits):
    tiles, cols = virt // TILE, aux // 128
    chunks = len(pieces)
    groups = pieces[0].shape[1] // tiles
    rows = TILE // fits
    half = rows // 2

    def kernel(where_ref, left_ref, *refs):
        slot_refs, keep_refs = refs[:chunks], refs[chunks : 2 * chunks]
        refs = refs[2 * chunks :]
        amp_refs = refs[: 2 * fits * chunks]
        refs = refs[2 * fits * chunks :]
        piece_refs = refs[:chunks]
        gamma_ref, dens_ref, right_ref, amp_ref, turned_ref = refs[chunks:]
        f = where_ref[0]
        at = [pl.multiple_of(((f + k) % fits) * rows, rows) for k in range(fits)]
        mine = pl.ds(pl.multiple_of(f * (virt // fits), virt // fits), virt // fits)
        gamma_ref[...] = jnp.zeros_like(gamma_ref)
        dens_ref[...] = jnp.zeros_like(dens_ref)
        for n in range(chunks):
            flat = amp_refs[2 * fits * n : 2 * fits * (n + 1)]
            parts = [flat[2 * k : 2 * k + 2] for k in range(fits)]

            @pl.loop(0, groups)
            def _(g):
                assemble_right(right_ref, piece_refs[n], g, tiles, cols)
                for u in range(2):
                    p = 2 * g + u
                    k = left_ref[2 * groups * n + p]
                    assemble_amplitudes(amp_ref, parts, slot_refs[n], keep_refs[n], p, at, tiles, half)
                    turned_ref[...] = amp_ref[...].T
                    for h in range(2):
                        lanes = slice(h * (aux // 2), (h + 1) * (aux // 2))
                        gamma_ref[k, :, lanes] += jnp.dot(
                            turned_ref[...], right_ref[:, lanes], preferred_element_type=F32
                        )
                    dens_ref[k] += lax.dot_general(
                        turned_ref[...], turned_ref[mine, :], (((1,), (1,)), ((), ())), preferred_element_type=F32
                    )

    return call(
        kernel,
        [sds((orbs, virt, aux), F32), sds((orbs, virt, virt // fits), F32)],
        (where, pairs_at, *slots, *keep, *[a for part in amps for a in part], *pieces),
        scalars=2 + 2 * chunks,
        scratch=[pltpu.VMEM((virt, aux), BF16), pltpu.VMEM((virt, virt), BF16), pltpu.VMEM((virt, virt), BF16)],
        flops=5 * chunks * groups * virt * virt * aux,
        name="own_terms",
    )


def sum_returned(wanted, returned, orbs, tiles):
    peers = wanted.shape[0]
    count = returned[0].shape[1] // tiles

    def kernel(wanted_ref, *refs):
        parts, out_ref, total_ref = refs[: len(returned)], refs[-2], refs[-1]
        total_ref[...] = jnp.zeros_like(total_ref)
        for n, ref in enumerate(parts):

            @pl.loop(0, peers)
            def _(d):
                for g in range(count):
                    j = wanted_ref[d, n * count + g]
                    spot = pl.ds((j % orbs) * tiles, tiles)
                    total_ref[j // orbs, spot] += ref[d, g * tiles : (g + 1) * tiles].astype(F32)

        out_ref[...] = total_ref[...].astype(BF16)

    shape = (peers, orbs * tiles, SUB, 128)
    return call(
        kernel, sds(shape, BF16), (wanted, *returned), scalars=1, scratch=[pltpu.VMEM(shape, F32)], name="sum_returned"
    )


def add_returned(gamma_own, sums):
    orbs, virt, aux = gamma_own.shape
    tiles, cols = virt // TILE, aux // 128
    peers = sums.shape[0]

    def kernel(own_ref, sums_ref, out_ref):
        for t in range(tiles):
            for m in range(peers):
                r, c = divmod(m, cols)
                rows = slice(t * TILE + r * SUB, t * TILE + (r + 1) * SUB)
                lanes = slice(c * 128, (c + 1) * 128)
                out_ref[0, rows, lanes] = own_ref[0, rows, lanes] + sums_ref[m, t].astype(F32)

    return pl.pallas_call(
        kernel,
        grid=(orbs,),
        out_shape=sds((orbs, virt, aux), F32),
        in_specs=[
            pl.BlockSpec((1, virt, aux), lambda k: (k, 0, 0)),
            pl.BlockSpec((peers, tiles, SUB, 128), lambda k: (0, k, 0, 0)),
        ],
        out_specs=pl.BlockSpec((1, virt, aux), lambda k: (k, 0, 0)),
        compiler_params=pltpu.CompilerParams(vmem_limit_bytes=VMEM_LIMIT),
        cost_estimate=pl.CostEstimate(flops=0, bytes_accessed=10 * orbs * virt * aux, transcendentals=0),
        name="add_returned",
    )(gamma_own, sums)


def on_device(blocks, occ_energy, virt_energy, domains, pairs):
    peers = lax.axis_size("orb")
    fits = lax.axis_size("fit")
    my_index = lax.axis_index("orb")
    f = lax.axis_index("fit")
    orbs, virt, aux = blocks.shape
    tiles = virt // TILE
    pair_count = pairs.shape[0]
    group_count = pair_count // 2
    per = group_count // CHUNKS
    rows = TILE // fits

    left_orb = pairs[:, 0]
    pairs_at = (left_orb - my_index * orbs).astype(jnp.int32)
    right_orb = pairs[::2, 1]
    where = f.astype(jnp.int32).reshape(1)

    info = jnp.zeros((SUB, 128), BF16).at[0, :group_count].set(right_orb.astype(BF16))
    held = lax.all_to_all(pack_blocks(blocks, info, peers), "orb", split_axis=0, concat_axis=0, tiled=True)
    wanted = held[:, orbs * tiles, 0, :group_count].astype(jnp.int32)

    right_rows = jnp.take(virt_energy, right_orb, axis=0) - jnp.take(occ_energy, right_orb)[:, None]
    right_rows = lax.dynamic_slice_in_dim(right_rows.reshape(group_count * tiles, TILE), f * rows, rows, axis=1)
    right_level = jnp.broadcast_to(right_rows[:, :, None], (group_count * tiles, rows, TILE))
    my_orbs = my_index * orbs + jnp.arange(orbs, dtype=jnp.int32)
    left_rows = jnp.take(virt_energy, my_orbs, axis=0) - jnp.take(occ_energy, my_orbs)[:, None]
    left_level = left_rows.reshape(orbs * tiles, 1, TILE)

    span_left = jnp.take(domains, left_orb) // TILE
    span_right = jnp.take(domains, jnp.repeat(right_orb, 2)) // TILE
    tile_ids = jnp.arange(tiles, dtype=jnp.int32)
    keep = (
        (tile_ids[None, :, None] < span_right[:, None, None]) & (tile_ids[None, None, :] < span_left[:, None, None])
    ).astype(jnp.int32).reshape(pair_count, tiles * tiles)
    chunk_pairs = 2 * per
    room = chunk_pairs * tiles * tiles
    slots = jnp.arange(room, dtype=jnp.int32).reshape(chunk_pairs, tiles * tiles)

    up = [(k, (k + 1) % fits) for k in range(fits)]
    down = [(k, (k - 1) % fits) for k in range(fits)]

    pieces = [
        lax.all_to_all(
            pick_pieces(wanted, held, n * per, per, tiles, orbs), "orb", split_axis=0, concat_axis=0, tiled=True
        )
        for n in range(CHUNKS)
    ]
    all_amps, keeps, returned = [], [], []
    for n in range(CHUNKS):
        at = pairs_at[n * chunk_pairs : (n + 1) * chunk_pairs]
        kept = keep[n * chunk_pairs : (n + 1) * chunk_pairs]
        own, go_up, go_down, up0, down1 = partial_integrals(where, at, slots, pieces[n], blocks, room, fits)
        came_up = lax.ppermute(go_up, "fit", up)
        came_down = lax.ppermute(go_down, "fit", down)
        more_up, more_down = merge_halves(came_up, up0, came_down, down1)
        more_up = lax.ppermute(more_up, "fit", up)
        more_down = lax.ppermute(more_down, "fit", down)
        z0, z1 = make_amplitudes(
            slots, at, own, came_up, came_down, more_up, more_down,
            right_level[n * per * tiles : (n + 1) * per * tiles], left_level, per,
        )
        below0 = lax.ppermute(z0, "fit", up)
        above1 = lax.ppermute(z1, "fit", down)
        below1 = lax.ppermute(z1, "fit", up)
        above0 = lax.ppermute(z0, "fit", down)
        across0 = lax.ppermute(below0, "fit", up)
        across1 = lax.ppermute(above1, "fit", down)
        amps = [z0, z1, above0, above1, across0, across1, below0, below1]
        back = returned_blocks(where, at, slots, kept, amps, blocks, peers, fits)
        returned.append(lax.all_to_all(back, "orb", split_axis=0, concat_axis=0, tiled=True))
        all_amps.append(amps)
        keeps.append(kept)
    gamma_own, density = own_terms(
        where, pairs_at, [slots] * CHUNKS, keeps, all_amps, pieces, orbs, virt, aux, fits
    )
    sums = sum_returned(wanted, returned, orbs, tiles)
    sums = lax.all_to_all(sums, "orb", split_axis=0, concat_axis=0, tiled=True)
    return add_returned(gamma_own, sums), density


def solution(mesh):
    placed = (P("orb", None, "fit"), P(), P(), P(), P("orb", None))
    return jax.shard_map(
        on_device,
        mesh=mesh,
        in_specs=placed,
        out_specs=(P("orb", None, "fit"), P("orb", None, "fit")),
        check_vma=False,
    )
```

time: 768 us -> 378 us (0.49); the launches traced: 753 us -> 377 us
  waiting for transfers between devices: 535 us -> 141 us
  matrix products: 106 us -> 0 us
  Pallas kernels: 0 us -> 88.3 us
  blocking collectives: 15.3 us -> 76.1 us
  local copies, waits for them, and re-layouts: 57.9 us -> 14.7 us
  starting transfers between devices: 13.8 us -> 52.9 us
  between operations: 14.5 us -> 0.94 us
  other arithmetic: 10.4 us -> 2.14 us
    all_to_all x2 -> x4, waiting for transfers between devices: 371 us -> 31.1 us  [the longest x2 21.9 us: on_device(): lax.all_to_all(pick_pieces(wanted, held, n * per, per, tiles, orbs), 'orb...]
    psum x1 -> x0, waiting for transfers between devices: 165 us -> none  [on_device(): lax.psum(partial_value.astype(jnp.bfloat16), 'fit').astype(jnp.float32)]
    ppermute x0 -> x20, waiting for transfers between devices: none -> 110 us  [the longest x2 22.6 us: on_device(): below1 = lax.ppermute(z1, 'fit', up)]
    dot_general x9 -> x0, matrix products: 106 us -> none  [the longest x1 22.3 us: on_device(): jnp.einsum('kp,pac->kac', owner_rows, own_terms, precision=lax.Precision....]
    pallas_call x0 -> x14, Pallas kernels: none -> 88.3 us  [the longest x13 83.2 us: call(): pl.pallas_call(kernel, out_shape=out_shape, in_specs=in_specs, out_specs=...]
    all_to_all x1 -> x2, blocking collectives: 15.3 us -> 76.1 us  [the longest x1 38.7 us: on_device(): lax.all_to_all(pack_blocks(blocks, info, peers), 'orb', split_axis=0, con...]
    convert_element_type x2 -> x0, local copies, waits for them, and re-layouts: 33.6 us -> none  [the longest x1 16.8 us: on_device(): send_back = jnp.einsum('os,sbc->obc', group_match, group_sums, preferred_...]
    ppermute x0 -> x20, starting transfers between devices: none -> 26.8 us  [the longest x2 5.79 us: on_device(): across1 = lax.ppermute(above1, 'fit', down)]
  transfers between devices with their start and end apart: 3 -> 24, of which waited for: 3 -> 12; matrix products, arithmetic and copies ran while one was open for 5% -> 3% of each run, Pallas kernels for 0% -> 18%
where the time goes in v1:
time: 378 us; the launch traced here: 377 us
  waiting for transfers between devices  141 us (37%)
  Pallas kernels  88.3 us (23%)
  blocking collectives  76.1 us (20%)
  starting transfers between devices  52.9 us (14%)
  local copies, waits for them, and re-layouts  14.7 us (4%)
    pallas_call x13, Pallas kernels, call(): pl.pallas_call(kernel, out_shape=out_shape, in_specs=in_specs, out_specs=...  83.2 us
    all_to_all x1, blocking collectives, on_device(): lax.all_to_all(pack_blocks(blocks, info, peers), 'orb', split_axis=0, con...  38.7 us
    all_to_all x1, blocking collectives, on_device(): lax.all_to_all(back, 'orb', split_axis=0, concat_axis=0, tiled=True)  37.4 us
    ppermute x2, waiting for transfers between devices, on_device(): below1 = lax.ppermute(z1, 'fit', up)  22.6 us
    ppermute x2, waiting for transfers between devices, on_device(): across0 = lax.ppermute(below0, 'fit', up)  22.5 us
    ppermute x2, waiting for transfers between devices, on_device(): more_up = lax.ppermute(more_up, 'fit', up)  22.3 us
    all_to_all x2, waiting for transfers between devices, on_device(): lax.all_to_all(pick_pieces(wanted, held, n * per, per, tiles, orbs), 'orb...  21.9 us
    ppermute x2, waiting for transfers between devices, on_device(): came_up = lax.ppermute(go_up, 'fit', up)  20.3 us
  transfers between devices with their start and end apart: 24, of which 12 were waited for; matrix products, arithmetic and copies ran while one was open for 3% of the time, Pallas kernels for 18%

profile of v1, /device:TPU:1, one launch (start us, length us, event | category | flops | bytes accessed | tf_op | source)
XLA Modules:
  0.0 376.6 jit_solution(14281062623163025058)
XLA Ops:
  0.6 0.8 slice.53
  1.5 0.6 scatter.4.info_ref
  2.1 3.3 pack_blocks.1
  5.4 38.7 %all_to_all.30.held_ref = bf16[32,17,16,128]{3,2,1,0:T(8,128)(2,1)S(1)} all-to-all(bf16[32,17,16,128]{3,2,1,0:T(8,128)(2,1)} %pack_blocks.1), channel_id=1, replica_groups=mesh['orb'=32,'fit'=4] {'orb'}, dimensions={0} | all-to-all | bytes 4456448 | tf_op jit(solution)/shard_map/all_to_all | solution.py:356
  44.1 0.7 fusion.1.wanted_ref
  44.8 0.7 copy-done.3
  45.5 4.1 %pick_pieces.2 = bf16[32,16,16,128]{3,2,1,0:T(8,128)(2,1)} custom-call(s32[32,8]{1,0:T(8,128)} %fusion.1.wanted_ref, bf16[32,17,16,128]{3,2,1,0:T(8,128)(2,1)} %copy-done.3), custom_call_target="tpu_custom_call" | custom-call | bytes 4326400 | tf_op jit(solution)/shard_map/pick_pieces/pallas_call | solution.py:25
  49.6 4.2 %all-to-all-start.1 = ((bf16[32,16,16,128]{3,2,1,0:T(8,128)(2,1)}), bf16[32,16,16,128]{3,2,1,0:T(8,128)(2,1)S(1)}, u32[]{:S(2)}, u32[]{:S(2)}) async-start(bf16[32,16,16,128]{3,2,1,0:T(8,128)(2,1)} %pick_pieces.2), calls=%async_computation.1 | async-start | bytes 4194304 | tf_op jit(solution)/shard_map/all_to_all | solution.py:380
  53.8 0.7 gather_fusion.5
  54.5 0.6 multiply_add_fusion.slot_ref.refs_0_.refs_1_
  55.1 0.6 fusion.9
  55.7 4.1 %pick_pieces.3 = bf16[32,16,16,128]{3,2,1,0:T(8,128)(2,1)} custom-call(s32[32,8]{1,0:T(8,128)} %fusion.1.wanted_ref, bf16[32,17,16,128]{3,2,1,0:T(8,128)(2,1)} %copy-done.3), custom_call_target="tpu_custom_call" | custom-call | bytes 4326400 | tf_op jit(solution)/shard_map/pick_pieces/pallas_call | solution.py:25
  59.8 21.9 %all-to-all-done.1.pieces_ref.refs_20_ = bf16[32,16,16,128]{3,2,1,0:T(8,128)(2,1)S(1)} async-done(((bf16[32,16,16,128]{3,2,1,0:T(8,128)(2,1)}), bf16[32,16,16,128]{3,2,1,0:T(8,128)(2,1)S(1)}, u32[]{:S(2)}, u32[]{:S(2)}) %all-to-all-start.1) | async-done | bytes 2097184 | tf_op jit(solution)/shard_map/all_to_all | solution.py:380
  81.7 6.7 %all-to-all-start.2 = ((bf16[32,16,16,128]{3,2,1,0:T(8,128)(2,1)}), bf16[32,16,16,128]{3,2,1,0:T(8,128)(2,1)}, u32[]{:S(2)}, u32[]{:S(2)}) async-start(bf16[32,16,16,128]{3,2,1,0:T(8,128)(2,1)} %pick_pieces.3), calls=%async_computation.2 | async-start | bytes 4194304 | tf_op jit(solution)/shard_map/all_to_all | solution.py:380
  88.5 8.4 %partial_integrals.2 = (bf16[128,32,128]{2,1,0:T(8,128)(2,1)}, bf16[128,32,128]{2,1,0:T(8,128)(2,1)}, bf16[128,32,128]{2,1,0:T(8,128)(2,1)}, bf16[128,16,128]{2,1,0:T(8,128)(2,1)}, bf16[128,16,128]{2,1,0:T(8,128)(2,1)}) custom-call(s32[1]{0:T(128)} %bitcast.where_ref, s32[8]{0:T(128)} %get-tuple-element.62.left_ref, ...), custom_call_target="tpu_custom_call" | custom-call | flops 2147483648 | bytes 8389156 | tf_op jit(solution)/shard_map/partial_integrals/pallas_call | solution.py:25
  96.8 1.6 collective-permute-start
  98.5 2.1 collective-permute-start.1
  100.8 0.6 gather_fusion.1
  101.4 0.6 gather_fusion.3
  102.1 0.6 gather_fusion.2
  103.0 0.7 fusion.2.ll_ref
  103.7 20.3 %collective-permute-done.up_ref = bf16[128,32,128]{2,1,0:T(8,128)(2,1)S(1)} collective-permute-done((bf16[128,32,128]{2,1,0:T(8,128)(2,1)}, bf16[128,32,128]{2,1,0:T(8,128)(2,1)S(1)}, u32[]{:S(2)}, u32[]{:S(2)}) %collective-permute-start) | collective-permute-done | bytes 1048608 | tf_op jit(solution)/shard_map/ppermute | solution.py:390
  124.0 1.0 copy-done.6
  125.4 3.0 merge_halves.2
  128.4 2.7 collective-permute-start.3
  131.1 0.6 gather_fusion
  132.1 10.2 %collective-permute-done.2.mup_ref = bf16[128,16,128]{2,1,0:T(8,128)(2,1)S(1)} collective-permute-done((bf16[128,16,128]{2,1,0:T(8,128)(2,1)}, bf16[128,16,128]{2,1,0:T(8,128)(2,1)S(1)}, u32[]{:S(2)}, u32[]{:S(2)}) %collective-permute-start.2) | collective-permute-done | bytes 524320 | tf_op jit(solution)/shard_map/ppermute | solution.py:393
  142.3 1.0 broadcast_in_dim.58.rl_ref
  143.4 3.9 %make_amplitudes.2 = (bf16[128,16,128]{2,1,0:T(8,128)(2,1)}, bf16[128,16,128]{2,1,0:T(8,128)(2,1)}) custom-call(s32[8,16]{1,0:T(8,128)} %multiply_add_fusion.slot_ref.refs_0_.refs_1_, s32[8]{0:T(128)} %get-tuple-element.62.left_ref, bf16[128,32,128]{2,1,0:T(8,128)(2,1)} %get-tuple-element.35.own_ref, bf16[128,32,128]{2,1,0:T(8,128)(2,1)} %copy-done.6, ...), custom_call_target="tpu_custom_call" | custom-call | bytes 5513760 | tf_op jit(solution)/shard_map/make_amplitudes/pallas_call | solution.py:25
  147.3 2.2 collective-permute-start.4
  149.5 2.7 collective-permute-start.5
  152.2 0.7 gather_fusion.4
  152.9 8.5 %partial_integrals.3 = (bf16[128,32,128]{2,1,0:T(8,128)(2,1)}, bf16[128,32,128]{2,1,0:T(8,128)(2,1)}, bf16[128,32,128]{2,1,0:T(8,128)(2,1)}, bf16[128,16,128]{2,1,0:T(8,128)(2,1)}, bf16[128,16,128]{2,1,0:T(8,128)(2,1)}) custom-call(s32[1]{0:T(128)} %bitcast.where_ref, s32[8]{0:T(128)} %get-tuple-element.61.left_ref, ...), custom_call_target="tpu_custom_call" | custom-call | flops 2147483648 | bytes 8389156 | tf_op jit(solution)/shard_map/partial_integrals/pallas_call | solution.py:25
  161.4 2.7 collective-permute-start.11
  164.3 6.1 %collective-permute-done.5.refs_7_.refs_3_ = bf16[128,16,128]{2,1,0:T(8,128)(2,1)S(1)} collective-permute-done((bf16[128,16,128]{2,1,0:T(8,128)(2,1)}, bf16[128,16,128]{2,1,0:T(8,128)(2,1)S(1)}, u32[]{:S(2)}, u32[]{:S(2)}) %collective-permute-start.5) | collective-permute-done | bytes 524320 | tf_op jit(solution)/shard_map/ppermute | solution.py:400
  170.3 3.1 collective-permute-start.8
  173.5 0.7 copy.22.refs_2_.keep_ref
  174.2 21.6 %collective-permute-done.9.refs_11_.refs_7_ = bf16[128,16,128]{2,1,0:T(8,128)(2,1)} collective-permute-done((bf16[128,16,128]{2,1,0:T(8,128)(2,1)S(1)}, bf16[128,16,128]{2,1,0:T(8,128)(2,1)}, u32[]{:S(2)}, u32[]{:S(2)}) %collective-permute-start.9) | collective-permute-done | bytes 524320 | tf_op jit(solution)/shard_map/ppermute | solution.py:401
  195.8 11.2 %collective-permute-done.7.refs_8_.refs_4_ = bf16[128,16,128]{2,1,0:T(8,128)(2,1)} collective-permute-done((bf16[128,16,128]{2,1,0:T(8,128)(2,1)S(1)}, bf16[128,16,128]{2,1,0:T(8,128)(2,1)}, u32[]{:S(2)}, u32[]{:S(2)}) %collective-permute-start.7) | collective-permute-done | bytes 524320 | tf_op jit(solution)/shard_map/ppermute | solution.py:403
  207.1 8.0 %returned_blocks.2 = bf16[32,16,16,128]{3,2,1,0:T(8,128)(2,1)} custom-call(s32[1]{0:T(128)} %bitcast.where_ref, s32[8]{0:T(128)} %get-tuple-element.62.left_ref, s32[8,16]{1,0:T(8,128)} %multiply_add_fusion.slot_ref.refs_0_.refs_1_, s32[8,16]{1,0:T(8,128)} %copy.22.refs_2_.keep_ref, bf16[128,16,128]{2,1,0:T(8,128)(2,1)} %get-tuple-element.42.refs_4_.refs_0_, ...), custom_call_target="tpu_custom_call" | custom-call | flops 2147483648 | bytes 8389668 | tf_op jit(solution)/shard_map/returned_blocks/pallas_call | solution.py:25
  215.1 11.2 %all-to-all-start.3 = ((bf16[32,16,16,128]{3,2,1,0:T(8,128)(2,1)}), bf16[32,16,16,128]{3,2,1,0:T(8,128)(2,1)S(1)}, u32[]{:S(2)}, u32[]{:S(2)}) async-start(bf16[32,16,16,128]{3,2,1,0:T(8,128)(2,1)} %returned_blocks.2), calls=%async_computation.3 | async-start | bytes 4194304 | tf_op jit(solution)/shard_map/all_to_all | solution.py:407
  226.3 1.0 copy-done.8
  227.3 2.9 merge_halves.3
  230.2 2.7 collective-permute-start.13
  232.9 12.0 %collective-permute-done.12.mup_ref = bf16[128,16,128]{2,1,0:T(8,128)(2,1)S(1)} collective-permute-done((bf16[128,16,128]{2,1,0:T(8,128)(2,1)}, bf16[128,16,128]{2,1,0:T(8,128)(2,1)S(1)}, u32[]{:S(2)}, u32[]{:S(2)}) %collective-permute-start.12) | collective-permute-done | bytes 524320 | tf_op jit(solution)/shard_map/ppermute | solution.py:393
  244.9 1.0 broadcast_in_dim.63.rl_ref
  246.0 3.9 %make_amplitudes.3 = (bf16[128,16,128]{2,1,0:T(8,128)(2,1)}, bf16[128,16,128]{2,1,0:T(8,128)(2,1)}) custom-call(s32[8,16]{1,0:T(8,128)} %multiply_add_fusion.slot_ref.refs_0_.refs_1_, s32[8]{0:T(128)} %get-tuple-element.61.left_ref, bf16[128,32,128]{2,1,0:T(8,128)(2,1)} %get-tuple-element.44.own_ref, bf16[128,32,128]{2,1,0:T(8,128)(2,1)} %copy-done.8, ...), custom_call_target="tpu_custom_call" | custom-call | bytes 5513760 | tf_op jit(solution)/shard_map/make_amplitudes/pallas_call | solution.py:25
  250.0 2.7 collective-permute-start.15
  252.7 1.0 collective-permute-start.14
  253.7 0.5 collective-permute-start.19
  254.1 9.6 %collective-permute-done.16.refs_18_.refs_6_ = bf16[128,16,128]{2,1,0:T(8,128)(2,1)S(1)} collective-permute-done((bf16[128,16,128]{2,1,0:T(8,128)(2,1)}, bf16[128,16,128]{2,1,0:T(8,128)(2,1)S(1)}, u32[]{:S(2)}, u32[]{:S(2)}) %collective-permute-start.16) | collective-permute-done | bytes 524320 | tf_op jit(solution)/shard_map/ppermute | solution.py:399
  263.8 2.7 collective-permute-start.18
  266.5 0.7 copy.23.refs_3_.keep_ref
  267.1 7.0 %collective-permute-done.14.refs_14_.refs_2_ = bf16[128,16,128]{2,1,0:T(8,128)(2,1)} collective-permute-done((bf16[128,16,128]{2,1,0:T(8,128)(2,1)}, bf16[128,16,128]{2,1,0:T(8,128)(2,1)}, u32[]{:S(2)}, u32[]{:S(2)}) %collective-permute-start.14) | collective-permute-done | bytes 524320 | tf_op jit(solution)/shard_map/ppermute | solution.py:402
  274.1 1.0 collective-permute-done.19.refs_19_.refs_7_
  275.1 11.2 %collective-permute-done.17.refs_16_.refs_4_ = bf16[128,16,128]{2,1,0:T(8,128)(2,1)} collective-permute-done((bf16[128,16,128]{2,1,0:T(8,128)(2,1)S(1)}, bf16[128,16,128]{2,1,0:T(8,128)(2,1)}, u32[]{:S(2)}, u32[]{:S(2)}) %collective-permute-start.17) | collective-permute-done | bytes 524320 | tf_op jit(solution)/shard_map/ppermute | solution.py:403
  286.4 8.0 %returned_blocks.3 = bf16[32,16,16,128]{3,2,1,0:T(8,128)(2,1)} custom-call(s32[1]{0:T(128)} %bitcast.where_ref, s32[8]{0:T(128)} %get-tuple-element.61.left_ref, s32[8,16]{1,0:T(8,128)} %multiply_add_fusion.slot_ref.refs_0_.refs_1_, s32[8,16]{1,0:T(8,128)} %copy.23.refs_3_.keep_ref, bf16[128,16,128]{2,1,0:T(8,128)(2,1)} %get-tuple-element.51.refs_12_.refs_0_, ...), custom_call_target="tpu_custom_call" | custom-call | flops 2147483648 | bytes 8389668 | tf_op jit(solution)/shard_map/returned_blocks/pallas_call | solution.py:25
  294.4 37.4 %all_to_all.31.refs_1_ = bf16[32,16,16,128]{3,2,1,0:T(8,128)(2,1)} all-to-all(bf16[32,16,16,128]{3,2,1,0:T(8,128)(2,1)} %returned_blocks.3), channel_id=1, replica_groups=mesh['orb'=32,'fit'=4] {'orb'}, dimensions={0} | all-to-all | bytes 4194304 | tf_op jit(solution)/shard_map/all_to_all | solution.py:407
  331.8 6.3 %sum_returned.1 = bf16[32,16,16,128]{3,2,1,0:T(8,128)(2,1)} custom-call(s32[32,8]{1,0:T(8,128)} %fusion.1.wanted_ref, bf16[32,16,16,128]{3,2,1,0:T(8,128)(2,1)} %copy-done.4, bf16[32,16,16,128]{3,2,1,0:T(8,128)(2,1)} %all_to_all.31.refs_1_), custom_call_target="tpu_custom_call" | custom-call | bytes 6292480 | tf_op jit(solution)/shard_map/sum_returned/pallas_call | solution.py:25
  338.1 4.1 %all-to-all-start.5 = ((bf16[32,16,16,128]{3,2,1,0:T(8,128)(2,1)}), bf16[32,16,16,128]{3,2,1,0:T(8,128)(2,1)S(1)}, u32[]{:S(2)}, u32[]{:S(2)}) async-start(bf16[32,16,16,128]{3,2,1,0:T(8,128)(2,1)} %sum_returned.1), calls=%async_computation.5 | async-start | bytes 4194304 | tf_op jit(solution)/shard_map/all_to_all | solution.py:414
  342.1 18.7 %own_terms.1 = (f32[4,512,512]{2,1,0:T(8,128)}, f32[4,512,128]{2,1,0:T(8,128)}) custom-call(s32[1]{0:T(128)} %bitcast.where_ref, s32[16]{0:T(128)} %copy-done.20, s32[8,16]{1,0:T(8,128)} %multiply_add_fusion.slot_ref.refs_0_.refs_1_, s32[8,16]{1,0:T(8,128)} %multiply_add_fusion.slot_ref.refs_0_.refs_1_, s32[8,16]{1,0:T(8,128)} %copy.22.refs_2_.keep_ref, ...), custom_call_target="tpu_custom_call" | custom-call | flops 5368709120 | bytes 17827908 | tf_op jit(solution)/shard_map/own_terms/pallas_call | solution.py:25
  360.9 9.2 %all-to-all-done.5.sums_ref = bf16[32,16,16,128]{3,2,1,0:T(8,128)(2,1)S(1)} async-done(((bf16[32,16,16,128]{3,2,1,0:T(8,128)(2,1)}), bf16[32,16,16,128]{3,2,1,0:T(8,128)(2,1)S(1)}, u32[]{:S(2)}, u32[]{:S(2)}) %all-to-all-start.5) | async-done | bytes 2097184 | tf_op jit(solution)/shard_map/all_to_all | solution.py:414
  370.1 1.4 copy-done.5
  371.4 5.1 %add_returned.1 = f32[4,512,512]{2,1,0:T(8,128)} custom-call(f32[4,512,512]{2,1,0:T(8,128)} %get-tuple-element.53.own_ref, bf16[32,16,16,128]{3,2,1,0:T(8,128)(2,1)} %copy-done.5), custom_call_target="tpu_custom_call" | custom-call | bytes 10485760 | tf_op jit(solution)/shard_map/add_returned/pallas_call | solution.py:323
  (92 shorter events, 2.0 us)
Async XLA Ops:
  0.6 101.4 %copy-start = (f32[128,512]{1,0:T(8,128)S(1)}, f32[128,512]{1,0:T(8,128)}, u32[]{:S(2)}) copy-start(f32[128,512]{1,0:T(8,128)} %param.11) | copy-start | bytes 786436
  44.1 1.4 copy-start.3
  49.6 4.2 %copy-start.21 = (s32[16,2]{0,1:T(2,128)S(1)}, s32[16,2]{0,1:T(2,128)}, u32[]{:S(2)}) copy-start(s32[16,2]{0,1:T(2,128)} %param.13) | copy-start | bytes 388
  49.6 4.2 %copy-start.2 = (s32[128]{0:T(128)S(1)}, s32[128]{0:T(128)}, u32[]{:S(2)}) copy-start(s32[128]{0:T(128)} %param.12) | copy-start | bytes 1540
  49.6 32.1 %all-to-all-start.1 = ((bf16[32,16,16,128]{3,2,1,0:T(8,128)(2,1)}), bf16[32,16,16,128]{3,2,1,0:T(8,128)(2,1)S(1)}, u32[]{:S(2)}, u32[]{:S(2)}) async-start(bf16[32,16,16,128]{3,2,1,0:T(8,128)(2,1)} %pick_pieces.2), calls=%async_computation.1 | async-start | bytes 4194304 | tf_op jit(solution)/shard_map/all_to_all | solution.py:380
  55.1 4.7 %copy-start.20 = (s32[16]{0:T(128)}, s32[16]{0:T(128)S(1)}, u32[]{:S(2)}) copy-start(s32[16]{0:T(128)S(1)} %get-tuple-element.60.left_ref) | copy-start | bytes 196
  81.7 6.7 %copy-start.9 = (bf16[32,16,16,128]{3,2,1,0:T(8,128)(2,1)}, bf16[32,16,16,128]{3,2,1,0:T(8,128)(2,1)S(1)}, u32[]{:S(2)}) copy-start(bf16[32,16,16,128]{3,2,1,0:T(8,128)(2,1)S(1)} %all-to-all-done.1.pieces_ref.refs_20_) | copy-start | bytes 6291460
  81.7 71.2 %all-to-all-start.2 = ((bf16[32,16,16,128]{3,2,1,0:T(8,128)(2,1)}), bf16[32,16,16,128]{3,2,1,0:T(8,128)(2,1)}, u32[]{:S(2)}, u32[]{:S(2)}) async-start(bf16[32,16,16,128]{3,2,1,0:T(8,128)(2,1)} %pick_pieces.3), calls=%async_computation.2 | async-start | bytes 4194304 | tf_op jit(solution)/shard_map/all_to_all | solution.py:380
  88.5 12.3 %copy-start.1 = (f32[128]{0:T(128)S(1)}, f32[128]{0:T(128)}, u32[]{:S(2)}) copy-start(f32[128]{0:T(128)} %param.10) | copy-start | bytes 1540
  96.8 27.2 %collective-permute-start = (bf16[128,32,128]{2,1,0:T(8,128)(2,1)}, bf16[128,32,128]{2,1,0:T(8,128)(2,1)S(1)}, u32[]{:S(2)}, u32[]{:S(2)}) collective-permute-start(bf16[128,32,128]{2,1,0:T(8,128)(2,1)} %get-tuple-element.36), channel_id=1, source_target_pairs={{0,1},{1,2},{2,3},{3,0},{4,5},{5,6},{6,7},{7,4},{8,9},{9,10},{10,1... | collective-permute-start | bytes 3145736 | tf_op jit(solution)/shard_map/ppermute | solution.py:390
  98.5 25.5 %collective-permute-start.1 = (bf16[128,32,128]{2,1,0:T(8,128)(2,1)}, bf16[128,32,128]{2,1,0:T(8,128)(2,1)S(1)}, u32[]{:S(2)}, u32[]{:S(2)}) collective-permute-start(bf16[128,32,128]{2,1,0:T(8,128)(2,1)} %get-tuple-element.37), channel_id=1, source_target_pairs={{0,3},{1,0},{2,1},{3,2},{4,7},{5,4},{6,5},{7,6},{8,11},{9,8},{10,9... | collective-permute-start | bytes 3145736 | tf_op jit(solution)/shard_map/ppermute | solution.py:391
  124.0 1.0 copy-start.6
  124.0 1.4 copy-start.7
  128.4 13.9 %collective-permute-start.2 = (bf16[128,16,128]{2,1,0:T(8,128)(2,1)}, bf16[128,16,128]{2,1,0:T(8,128)(2,1)S(1)}, u32[]{:S(2)}, u32[]{:S(2)}) collective-permute-start(bf16[128,16,128]{2,1,0:T(8,128)(2,1)} %get-tuple-element.40), channel_id=1, source_target_pairs={{0,1},{1,2},{2,3},{3,0},{4,5},{5,6},{6,7},{7,4},{8,9},{9,10},{10,1... | collective-permute-start | bytes 1572872 | tf_op jit(solution)/shard_map/ppermute | solution.py:393
  128.4 13.9 %collective-permute-start.3 = (bf16[128,16,128]{2,1,0:T(8,128)(2,1)}, bf16[128,16,128]{2,1,0:T(8,128)(2,1)S(1)}, u32[]{:S(2)}, u32[]{:S(2)}) collective-permute-start(bf16[128,16,128]{2,1,0:T(8,128)(2,1)} %get-tuple-element.41), channel_id=1, source_target_pairs={{0,3},{1,0},{2,1},{3,2},{4,7},{5,4},{6,5},{7,6},{8,11},{9,8},{10,9... | collective-permute-start | bytes 1572872 | tf_op jit(solution)/shard_map/ppermute | solution.py:394
  142.3 1.0 copy-start.16
  142.3 1.1 copy-start.17
  147.3 16.8 %collective-permute-start.4 = (bf16[128,16,128]{2,1,0:T(8,128)(2,1)}, bf16[128,16,128]{2,1,0:T(8,128)(2,1)S(1)}, u32[]{:S(2)}, u32[]{:S(2)}) collective-permute-start(bf16[128,16,128]{2,1,0:T(8,128)(2,1)} %get-tuple-element.42.refs_4_.refs_0_), channel_id=1, source_target_pairs={{0,3},{1,0},{2,1},{3,2},{4,7},{5,4},{6,5},{7,6},{8,11},{9,8},{10,9... | collective-permute-start | bytes 1572872 | tf_op jit(solution)/shard_map/ppermute | solution.py:402
  149.5 14.6 %collective-permute-start.6 = (bf16[128,16,128]{2,1,0:T(8,128)(2,1)}, bf16[128,16,128]{2,1,0:T(8,128)(2,1)S(1)}, u32[]{:S(2)}, u32[]{:S(2)}) collective-permute-start(bf16[128,16,128]{2,1,0:T(8,128)(2,1)} %get-tuple-element.42.refs_4_.refs_0_), channel_id=1, source_target_pairs={{0,1},{1,2},{2,3},{3,0},{4,5},{5,6},{6,7},{7,4},{8,9},{9,10},{10,1... | collective-permute-start | bytes 1572872 | tf_op jit(solution)/shard_map/ppermute | solution.py:399
  149.5 20.8 %collective-permute-start.5 = (bf16[128,16,128]{2,1,0:T(8,128)(2,1)}, bf16[128,16,128]{2,1,0:T(8,128)(2,1)S(1)}, u32[]{:S(2)}, u32[]{:S(2)}) collective-permute-start(bf16[128,16,128]{2,1,0:T(8,128)(2,1)} %get-tuple-element.43.refs_5_.refs_1_), channel_id=1, source_target_pairs={{0,3},{1,0},{2,1},{3,2},{4,7},{5,4},{6,5},{7,6},{8,11},{9,8},{10,9... | collective-permute-start | bytes 1572872 | tf_op jit(solution)/shard_map/ppermute | solution.py:400
  152.9 11.2 %copy-start.10 = (bf16[128,16,128]{2,1,0:T(8,128)(2,1)S(1)}, bf16[128,16,128]{2,1,0:T(8,128)(2,1)}, u32[]{:S(2)}) copy-start(bf16[128,16,128]{2,1,0:T(8,128)(2,1)} %get-tuple-element.43.refs_5_.refs_1_) | copy-start | bytes 1572868
  161.4 64.9 %collective-permute-start.10 = (bf16[128,32,128]{2,1,0:T(8,128)(2,1)}, bf16[128,32,128]{2,1,0:T(8,128)(2,1)S(1)}, u32[]{:S(2)}, u32[]{:S(2)}) collective-permute-start(bf16[128,32,128]{2,1,0:T(8,128)(2,1)} %get-tuple-element.45), channel_id=1, source_target_pairs={{0,1},{1,2},{2,3},{3,0},{4,5},{5,6},{6,7},{7,4},{8,9},{9,10},{10,1... | collective-permute-start | bytes 3145736 | tf_op jit(solution)/shard_map/ppermute | solution.py:390
  161.4 64.9 %collective-permute-start.11 = (bf16[128,32,128]{2,1,0:T(8,128)(2,1)}, bf16[128,32,128]{2,1,0:T(8,128)(2,1)}, u32[]{:S(2)}, u32[]{:S(2)}) collective-permute-start(bf16[128,32,128]{2,1,0:T(8,128)(2,1)} %get-tuple-element.46), channel_id=1, source_target_pairs={{0,3},{1,0},{2,1},{3,2},{4,7},{5,4},{6,5},{7,6},{8,11},{9,8},{10,9... | collective-permute-start | bytes 3145736 | tf_op jit(solution)/shard_map/ppermute | solution.py:391
  164.1 43.0 %copy-start.11 = (bf16[128,16,128]{2,1,0:T(8,128)(2,1)}, bf16[128,16,128]{2,1,0:T(8,128)(2,1)S(1)}, u32[]{:S(2)}) copy-start(bf16[128,16,128]{2,1,0:T(8,128)(2,1)S(1)} %collective-permute-done.4.refs_6_.refs_2_) | copy-start | bytes 1572868
  164.1 31.7 %collective-permute-start.9 = (bf16[128,16,128]{2,1,0:T(8,128)(2,1)S(1)}, bf16[128,16,128]{2,1,0:T(8,128)(2,1)}, u32[]{:S(2)}, u32[]{:S(2)}) collective-permute-start(bf16[128,16,128]{2,1,0:T(8,128)(2,1)S(1)} %copy-done.10), channel_id=1, source_target_pairs={{0,1},{1,2},{2,3},{3,0},{4,5},{5,6},{6,7},{7,4},{8,9},{9,10},{10,1... | collective-permute-start | bytes 1572872 | tf_op jit(solution)/shard_map/ppermute | solution.py:401
  164.2 42.9 %copy-start.12 = (bf16[128,16,128]{2,1,0:T(8,128)(2,1)}, bf16[128,16,128]{2,1,0:T(8,128)(2,1)S(1)}, u32[]{:S(2)}) copy-start(bf16[128,16,128]{2,1,0:T(8,128)(2,1)S(1)} %collective-permute-done.6.refs_10_.refs_6_) | copy-start | bytes 1572868
  164.2 42.9 %collective-permute-start.7 = (bf16[128,16,128]{2,1,0:T(8,128)(2,1)S(1)}, bf16[128,16,128]{2,1,0:T(8,128)(2,1)}, u32[]{:S(2)}, u32[]{:S(2)}) collective-permute-start(bf16[128,16,128]{2,1,0:T(8,128)(2,1)S(1)} %collective-permute-done.6.refs_10_.refs_6_), channel_id=1, source_target_pairs={{0,1},{1,2},{2,3},{3,0},{4,5},{5,6},{6,7},{7,4},{8,9},{9,10},{10,1... | collective-permute-start | bytes 1572872 | tf_op jit(solution)/shard_map/ppermute | solution.py:403
  170.3 36.7 %copy-start.13 = (bf16[128,16,128]{2,1,0:T(8,128)(2,1)}, bf16[128,16,128]{2,1,0:T(8,128)(2,1)S(1)}, u32[]{:S(2)}) copy-start(bf16[128,16,128]{2,1,0:T(8,128)(2,1)S(1)} %collective-permute-done.5.refs_7_.refs_3_) | copy-start | bytes 1572868
  170.3 36.7 %collective-permute-start.8 = (bf16[128,16,128]{2,1,0:T(8,128)(2,1)S(1)}, bf16[128,16,128]{2,1,0:T(8,128)(2,1)}, u32[]{:S(2)}, u32[]{:S(2)}) collective-permute-start(bf16[128,16,128]{2,1,0:T(8,128)(2,1)S(1)} %collective-permute-done.5.refs_7_.refs_3_), channel_id=1, source_target_pairs={{0,3},{1,0},{2,1},{3,2},{4,7},{5,4},{6,5},{7,6},{8,11},{9,8},{10,9... | collective-permute-start | bytes 1572872 | tf_op jit(solution)/shard_map/ppermute | solution.py:404
  215.1 79.3 %all-to-all-start.3 = ((bf16[32,16,16,128]{3,2,1,0:T(8,128)(2,1)}), bf16[32,16,16,128]{3,2,1,0:T(8,128)(2,1)S(1)}, u32[]{:S(2)}, u32[]{:S(2)}) async-start(bf16[32,16,16,128]{3,2,1,0:T(8,128)(2,1)} %returned_blocks.2), calls=%async_computation.3 | async-start | bytes 4194304 | tf_op jit(solution)/shard_map/all_to_all | solution.py:407
  226.3 1.0 copy-start.8
  230.2 14.7 %collective-permute-start.12 = (bf16[128,16,128]{2,1,0:T(8,128)(2,1)}, bf16[128,16,128]{2,1,0:T(8,128)(2,1)S(1)}, u32[]{:S(2)}, u32[]{:S(2)}) collective-permute-start(bf16[128,16,128]{2,1,0:T(8,128)(2,1)} %get-tuple-element.49), channel_id=1, source_target_pairs={{0,1},{1,2},{2,3},{3,0},{4,5},{5,6},{6,7},{7,4},{8,9},{9,10},{10,1... | collective-permute-start | bytes 1572872 | tf_op jit(solution)/shard_map/ppermute | solution.py:393
  230.2 14.7 %collective-permute-start.13 = (bf16[128,16,128]{2,1,0:T(8,128)(2,1)}, bf16[128,16,128]{2,1,0:T(8,128)(2,1)S(1)}, u32[]{:S(2)}, u32[]{:S(2)}) collective-permute-start(bf16[128,16,128]{2,1,0:T(8,128)(2,1)} %get-tuple-element.50), channel_id=1, source_target_pairs={{0,3},{1,0},{2,1},{3,2},{4,7},{5,4},{6,5},{7,6},{8,11},{9,8},{10,9... | collective-permute-start | bytes 1572872 | tf_op jit(solution)/shard_map/ppermute | solution.py:394
  244.9 1.0 copy-start.18
  244.9 1.1 copy-start.19
  250.0 13.8 %collective-permute-start.16 = (bf16[128,16,128]{2,1,0:T(8,128)(2,1)}, bf16[128,16,128]{2,1,0:T(8,128)(2,1)S(1)}, u32[]{:S(2)}, u32[]{:S(2)}) collective-permute-start(bf16[128,16,128]{2,1,0:T(8,128)(2,1)} %get-tuple-element.51.refs_12_.refs_0_), channel_id=1, source_target_pairs={{0,1},{1,2},{2,3},{3,0},{4,5},{5,6},{6,7},{7,4},{8,9},{9,10},{10,1... | collective-permute-start | bytes 1572872 | tf_op jit(solution)/shard_map/ppermute | solution.py:399
  250.0 13.8 %collective-permute-start.15 = (bf16[128,16,128]{2,1,0:T(8,128)(2,1)}, bf16[128,16,128]{2,1,0:T(8,128)(2,1)S(1)}, u32[]{:S(2)}, u32[]{:S(2)}) collective-permute-start(bf16[128,16,128]{2,1,0:T(8,128)(2,1)} %get-tuple-element.52.refs_13_.refs_1_), channel_id=1, source_target_pairs={{0,3},{1,0},{2,1},{3,2},{4,7},{5,4},{6,5},{7,6},{8,11},{9,8},{10,9... | collective-permute-start | bytes 1572872 | tf_op jit(solution)/shard_map/ppermute | solution.py:400
  252.7 21.4 %collective-permute-start.14 = (bf16[128,16,128]{2,1,0:T(8,128)(2,1)}, bf16[128,16,128]{2,1,0:T(8,128)(2,1)}, u32[]{:S(2)}, u32[]{:S(2)}) collective-permute-start(bf16[128,16,128]{2,1,0:T(8,128)(2,1)} %get-tuple-element.51.refs_12_.refs_0_), channel_id=1, source_target_pairs={{0,3},{1,0},{2,1},{3,2},{4,7},{5,4},{6,5},{7,6},{8,11},{9,8},{10,9... | collective-permute-start | bytes 1572872 | tf_op jit(solution)/shard_map/ppermute | solution.py:402
  253.7 21.5 %collective-permute-start.19 = (bf16[128,16,128]{2,1,0:T(8,128)(2,1)}, bf16[128,16,128]{2,1,0:T(8,128)(2,1)}, u32[]{:S(2)}, u32[]{:S(2)}) collective-permute-start(bf16[128,16,128]{2,1,0:T(8,128)(2,1)} %get-tuple-element.52.refs_13_.refs_1_), channel_id=1, source_target_pairs={{0,1},{1,2},{2,3},{3,0},{4,5},{5,6},{6,7},{7,4},{8,9},{9,10},{10,1... | collective-permute-start | bytes 1572872 | tf_op jit(solution)/shard_map/ppermute | solution.py:401
  263.8 22.6 %copy-start.14 = (bf16[128,16,128]{2,1,0:T(8,128)(2,1)}, bf16[128,16,128]{2,1,0:T(8,128)(2,1)S(1)}, u32[]{:S(2)}) copy-start(bf16[128,16,128]{2,1,0:T(8,128)(2,1)S(1)} %collective-permute-done.16.refs_18_.refs_6_) | copy-start | bytes 1572868
  263.8 22.6 %collective-permute-start.17 = (bf16[128,16,128]{2,1,0:T(8,128)(2,1)S(1)}, bf16[128,16,128]{2,1,0:T(8,128)(2,1)}, u32[]{:S(2)}, u32[]{:S(2)}) collective-permute-start(bf16[128,16,128]{2,1,0:T(8,128)(2,1)S(1)} %collective-permute-done.16.refs_18_.refs_6_), channel_id=1, source_target_pairs={{0,1},{1,2},{2,3},{3,0},{4,5},{5,6},{6,7},{7,4},{8,9},{9,10},{10,1... | collective-permute-start | bytes 1572872 | tf_op jit(solution)/shard_map/ppermute | solution.py:403
  263.8 22.6 %copy-start.15 = (bf16[128,16,128]{2,1,0:T(8,128)(2,1)}, bf16[128,16,128]{2,1,0:T(8,128)(2,1)S(1)}, u32[]{:S(2)}) copy-start(bf16[128,16,128]{2,1,0:T(8,128)(2,1)S(1)} %collective-permute-done.15.refs_15_.refs_3_) | copy-start | bytes 1572868
  263.8 22.6 %collective-permute-start.18 = (bf16[128,16,128]{2,1,0:T(8,128)(2,1)S(1)}, bf16[128,16,128]{2,1,0:T(8,128)(2,1)}, u32[]{:S(2)}, u32[]{:S(2)}) collective-permute-start(bf16[128,16,128]{2,1,0:T(8,128)(2,1)S(1)} %collective-permute-done.15.refs_15_.refs_3_), channel_id=1, source_target_pairs={{0,3},{1,0},{2,1},{3,2},{4,7},{5,4},{6,5},{7,6},{8,11},{9,8},{10,9... | collective-permute-start | bytes 1572872 | tf_op jit(solution)/shard_map/ppermute | solution.py:404
  294.4 37.4 %copy-start.4 = (bf16[32,16,16,128]{3,2,1,0:T(8,128)(2,1)}, bf16[32,16,16,128]{3,2,1,0:T(8,128)(2,1)S(1)}, u32[]{:S(2)}) copy-start(bf16[32,16,16,128]{3,2,1,0:T(8,128)(2,1)S(1)} %all-to-all-done.3.refs_0_) | copy-start | bytes 6291460
  338.1 32.0 %all-to-all-start.5 = ((bf16[32,16,16,128]{3,2,1,0:T(8,128)(2,1)}), bf16[32,16,16,128]{3,2,1,0:T(8,128)(2,1)S(1)}, u32[]{:S(2)}, u32[]{:S(2)}) async-start(bf16[32,16,16,128]{3,2,1,0:T(8,128)(2,1)} %sum_returned.1), calls=%async_computation.5 | async-start | bytes 4194304 | tf_op jit(solution)/shard_map/all_to_all | solution.py:414
  370.1 1.4 copy-start.5

commit v2 on v0

v2 whole, which is shorter than its diff:
```python
import jax
import jax.numpy as jnp
from jax import lax
from jax.experimental import pallas as pl
from jax.experimental.pallas import tpu as pltpu
from jax.sharding import PartitionSpec as P

TILE = 128
SUB = 16
WIDE = 256
F32 = jnp.float32
BF16 = jnp.bfloat16
MIB = 1024 * 1024


ORB, FIT, BACK, MINE, NEXT = 0, 1, 2, 6, 10

SMEM = pl.BlockSpec(memory_space=pltpu.SMEM)
ANY = pl.BlockSpec(memory_space=pl.ANY)


def sds(shape, dtype):
    return jax.ShapeDtypeStruct(shape, dtype)


def whole(shape):
    return pl.BlockSpec(shape, lambda n: (0,) * len(shape))


def call(kernel, grid, in_specs, out_specs, out_shape, args, scratch=(), memory=56, name=None):
    return pl.pallas_call(
        kernel,
        grid=(grid,),
        in_specs=in_specs,
        out_specs=out_specs,
        out_shape=out_shape,
        scratch_shapes=list(scratch),
        compiler_params=pltpu.CompilerParams(vmem_limit_bytes=memory * MIB),
        cost_estimate=pl.CostEstimate(flops=0, bytes_accessed=1024, transcendentals=0),
        name=name,
    )(*args)


def device_of(m, fits, cols):
    return m // (fits * cols), m // cols % fits, m % cols


def pack_blocks(place, info, blocks, peers, fits):
    orbs, virt, aux = blocks.shape
    cols = aux // 128
    rows = TILE // fits

    def kernel(place_ref, info_ref, blocks_ref, out_ref):
        @pl.when(pl.program_id(0) < orbs)
        def _():
            for m in range(peers):
                h, turned, c = device_of(m, fits, cols)
                tile = place_ref[BACK + turned] * TILE
                for z in range(fits):
                    at = pl.multiple_of(tile + z * rows + h * SUB, SUB)
                    out_ref[m * fits + z, 0] = blocks_ref[0, pl.ds(at, SUB), c * 128 : (c + 1) * 128]

        @pl.when(pl.program_id(0) == orbs)
        def _():
            for m in range(peers * fits):
                out_ref[m, 0] = info_ref[...]

    return call(
        kernel,
        orbs + 1,
        [SMEM, whole(info.shape), pl.BlockSpec((1, virt, aux), lambda k: (jnp.minimum(k, orbs - 1), 0, 0))],
        pl.BlockSpec((peers * fits, 1, SUB, 128), lambda k: (0, k, 0, 0)),
        sds((peers * fits, orbs + 1, SUB, 128), BF16),
        (place, info, blocks),
        name="pack_blocks",
    )


def pick_pieces(place, wanted, held, fits, after):
    peers, count = wanted.shape
    orbs = held.shape[1] - 1
    block = peers // 4

    def kernel(place_ref, wanted_ref, held_ref, *refs):
        out_ref = refs[-1]
        parts = [place_ref[NEXT + s] for s in range(fits)]
        first = pl.program_id(0) * block

        @pl.loop(0, block)
        def _(d):
            for g in range(count):
                j = wanted_ref[first + d, g]
                source, k = lax.div(j, orbs) * fits, lax.rem(j, orbs)
                for s in range(fits):
                    out_ref[d, g * fits + s] = held_ref[source + parts[s], k]

    return call(
        kernel,
        4,
        [SMEM, SMEM, whole(held.shape)] + [ANY] * len(after),
        pl.BlockSpec((block, count * fits, SUB, 128), lambda n: (n, 0, 0, 0)),
        sds((peers, count * fits, SUB, 128), BF16),
        (place, wanted, held, *after),
        name="pick_pieces",
    )


def pair_terms(place, plan, left_levels, right_levels, pieces, lefts, fits):
    orbs, virt, aux = lefts[0].shape
    peers, count = pieces.shape[0], pieces.shape[1] // fits
    tiles, cols = virt // TILE, aux // 128
    rows = TILE // fits
    taken = tiles * rows
    wide = virt // fits
    half = orbs // 2
    names = ("left", "nleft", "nright")

    def kernel(place_ref, left_ref, nleft_ref, nright_ref, low_ref, high_ref, pieces_ref, *refs):
        sources, refs = refs[: len(lefts)], refs[len(lefts) :]
        out_ref, own_ref, *parts = refs[: 2 * fits]
        lefts_ref, rows_ref, turned_ref, amp_ref, all_ref, square_ref, sems = refs[2 * fits :]
        n = pl.program_id(0)
        targets = [lefts_ref.at[0]]
        for s in range(1, fits):
            targets += [lefts_ref.at[s, 0:half], lefts_ref.at[s, half:orbs]]
        copies = [pltpu.make_async_copy(a, b, sems.at[k]) for k, (a, b) in enumerate(zip(sources, targets))]

        @pl.when(n == 0)
        def _():
            for copy in copies:
                copy.start()
            all_ref[...] = jnp.zeros_like(all_ref)

        @pl.when(n < count)
        def _():
            g = n
            for m in range(peers):
                h, turned, c = device_of(m, fits, cols)
                for s in range(fits):
                    at = pl.multiple_of(place_ref[BACK + (turned - s) % fits] * rows + h * SUB, SUB)
                    rows_ref[g, pl.ds(at, SUB), s * aux + c * 128 : s * aux + (c + 1) * 128] = pieces_ref[m, s]

            @pl.when(n == 0)
            def _():
                for copy in copies:
                    copy.wait()

            turned_ref[...] = rows_ref[g].T
            row_id = lax.broadcasted_iota(jnp.int32, (WIDE, taken), 0)
            col_id = lax.broadcasted_iota(jnp.int32, (WIDE, taken), 1)
            for u in range(2):
                p = 2 * g + u
                k = left_ref[p]
                for start in range(0, virt, WIDE):
                    at = slice(start, start + WIDE)
                    total = jnp.zeros((WIDE, taken), F32)
                    for s in range(fits):
                        total += (
                            jnp.dot(
                                lefts_ref[s, k, at, :],
                                turned_ref[s * aux : (s + 1) * aux, :],
                                preferred_element_type=F32,
                            )
                            .astype(BF16)
                            .astype(F32)
                        )
                    keep = (row_id < nleft_ref[p] * TILE - start) & (col_id < nright_ref[g] * rows)
                    amp = jnp.where(keep, -total / (low_ref[k, at, :] + high_ref[g]), 0.0).astype(BF16)
                    all_ref[k, at, pl.ds(pl.multiple_of(g * taken, taken), taken)] = amp
                    amp_ref[u, :, at] = amp.T
            k0, k1 = left_ref[2 * g], left_ref[2 * g + 1]
            for s in range(fits):
                for start in range(0, aux, WIDE):
                    lanes = slice(start, start + WIDE)
                    back = (
                        jnp.dot(amp_ref[0], lefts_ref[s, k0, :, lanes], preferred_element_type=F32)
                        + jnp.dot(amp_ref[1], lefts_ref[s, k1, :, lanes], preferred_element_type=F32)
                    ).astype(BF16)
                    for t in range(tiles):
                        turned = place_ref[NEXT + (s + t) % fits]
                        for h in range(rows // SUB):
                            for c in range(WIDE // 128):
                                out_ref[(h * fits + turned) * cols + start // 128 + c, t] = back[
                                    t * rows + h * SUB : t * rows + (h + 1) * SUB, c * 128 : (c + 1) * 128
                                ]

        for low in range(2):

            @pl.when((n >= count + low * half) & (n < count + (low + 1) * half))
            def _(low=low):
                k = n - count
                square_ref[...] = lax.dot_general(
                    all_ref[k], all_ref[k], (((1,), (1,)), ((), ())), preferred_element_type=F32
                ).astype(BF16)
                for s, target in enumerate([own_ref, *[parts[2 * s + low] for s in range(fits - 1)]]):
                    for start in range(0, aux, WIDE):
                        at = slice(s * aux + start, s * aux + start + WIDE)
                        right = rows_ref[:, :, at].reshape(count * taken, WIDE)
                        target[0, :, start : start + WIDE] = jnp.dot(
                            all_ref[k], right, preferred_element_type=F32
                        ).astype(BF16)
                    mine = pl.ds(pl.multiple_of(place_ref[NEXT + s] * wide, wide), wide)
                    target[0, :, aux : aux + wide] = square_ref[:, mine]

    block = (1, virt, aux + wide)
    places = [
        pl.BlockSpec(block, lambda n: (jnp.clip(n - count, 0, half - 1), 0, 0)),
        pl.BlockSpec(block, lambda n: (jnp.clip(n - count - half, 0, half - 1), 0, 0)),
    ]
    return call(
        kernel,
        count + orbs,
        [SMEM] * 4
        + [
            whole(left_levels.shape),
            whole(right_levels.shape),
            pl.BlockSpec((peers, fits, SUB, 128), lambda n: (0, jnp.minimum(n, count - 1), 0, 0)),
        ]
        + [ANY] * len(lefts),
        [
            pl.BlockSpec((peers, tiles, SUB, 128), lambda n: (0, jnp.minimum(n, count - 1), 0, 0)),
            pl.BlockSpec(block, lambda n: (jnp.maximum(n - count, 0), 0, 0)),
        ]
        + places * (fits - 1),
        [sds((peers, count * tiles, SUB, 128), BF16), sds((orbs, virt, aux + wide), BF16)]
        + [sds((half, virt, aux + wide), BF16)] * (2 * (fits - 1)),
        (place, *[plan[n] for n in names], left_levels, right_levels, pieces, *lefts),
        scratch=[
            pltpu.VMEM((fits, orbs, virt, aux), BF16),
            pltpu.VMEM((count, taken, fits * aux), BF16),
            pltpu.VMEM((fits * aux, taken), BF16),
            pltpu.VMEM((2, taken, virt), BF16),
            pltpu.VMEM((orbs, virt, count * taken), BF16),
            pltpu.VMEM((virt, virt), BF16),
            pltpu.SemaphoreType.DMA((len(lefts),)),
        ],
        name="pair_terms",
    )


def merge(mine, came, straight):
    half, virt, width = came[0].shape

    def kernel(a_ref, b_ref, c_ref, d_ref, e_ref, f_ref, up_ref, down_ref):
        n = pl.program_id(0)

        @pl.when(n < half)
        def _():
            up_ref[...] = (a_ref[...].astype(F32) + c_ref[...].astype(F32)).astype(BF16)
            down_ref[...] = f_ref[...]

        @pl.when(n >= half)
        def _():
            up_ref[...] = e_ref[...]
            down_ref[...] = (b_ref[...].astype(F32) + d_ref[...].astype(F32)).astype(BF16)

    block = (1, virt, width)
    first = pl.BlockSpec(block, lambda n: (jnp.minimum(n, half - 1), 0, 0))
    second = pl.BlockSpec(block, lambda n: (jnp.maximum(n - half, 0), 0, 0))
    every = pl.BlockSpec(block, lambda n: (n, 0, 0))
    return call(
        kernel,
        2 * half,
        [first, second, first, second, second, first],
        [every] * 2,
        [sds((2 * half, virt, width), BF16)] * 2,
        (*mine, *came, *straight),
        name="merge",
    )


def sum_returned(place, wanted, returned, orbs, fits, after):
    peers, count = wanted.shape
    tiles = fits
    steps = 4
    block = peers // steps

    def kernel(place_ref, wanted_ref, part_ref, *refs):
        out_ref, total_ref = refs[len(after) :]
        n = pl.program_id(0)

        @pl.when(n == 0)
        def _():
            total_ref[...] = jnp.zeros_like(total_ref)

        @pl.loop(0, block)
        def _(d):
            for g in range(count):
                spot = pl.ds(wanted_ref[n * block + d, g] * tiles, tiles)
                total_ref[spot] += part_ref[d, g * tiles : (g + 1) * tiles].astype(F32)

        @pl.when(n == steps - 1)
        def _():
            tile = [place_ref[MINE + q] for q in range(fits)]

            @pl.loop(0, peers)
            def _(o):
                for q in range(fits):
                    for k in range(orbs):
                        out_ref[o * fits + q, k] = total_ref[(o * orbs + k) * tiles + tile[q]].astype(BF16)

    out = (peers * fits, orbs, SUB, 128)
    return call(
        kernel,
        steps,
        [SMEM, SMEM, pl.BlockSpec((block, count * tiles, SUB, 128), lambda n: (n, 0, 0, 0))] + [ANY] * len(after),
        whole(out),
        sds(out, BF16),
        (place, wanted, returned, *after),
        scratch=[pltpu.VMEM((peers * orbs * tiles, SUB, 128), F32)],
        name="sum_returned",
    )


def add_all(place, own, below, above, sums, fits):
    orbs, virt, width = own.shape
    wide = virt // fits
    aux = width - wide
    cols = aux // 128
    rows = TILE // fits
    peers = sums.shape[0] // fits

    def kernel(place_ref, own_ref, below_ref, above_ref, sums_ref, gamma_ref, dens_ref):
        total = own_ref[0].astype(F32) + below_ref[0].astype(F32) + above_ref[0].astype(F32)
        gamma_ref[0] = total[:, 0:aux]
        dens_ref[0] = total[:, aux:width]
        for m in range(peers):
            h, turned, c = device_of(m, fits, cols)
            tile = place_ref[BACK + turned] * TILE
            lanes = slice(c * 128, (c + 1) * 128)
            for z in range(fits):
                at = pl.ds(pl.multiple_of(tile + z * rows + h * SUB, SUB), SUB)
                gamma_ref[0, at, lanes] += sums_ref[m * fits + z, 0].astype(F32)

    block = pl.BlockSpec((1, virt, width), lambda k: (k, 0, 0))
    return call(
        kernel,
        orbs,
        [SMEM, block, block, block, pl.BlockSpec((peers * fits, 1, SUB, 128), lambda k: (0, k, 0, 0))],
        [pl.BlockSpec((1, virt, aux), lambda k: (k, 0, 0)), pl.BlockSpec((1, virt, wide), lambda k: (k, 0, 0))],
        [sds((orbs, virt, aux), F32), sds((orbs, virt, wide), F32)],
        (place, own, below, above, sums),
        name="add_all",
    )


def on_device(blocks, occ_energy, virt_energy, domains, pairs):
    peers = lax.axis_size("orb")
    fits = lax.axis_size("fit")
    orbs, virt, aux = blocks.shape
    cols = aux // 128
    orb, fit = lax.axis_index("orb"), lax.axis_index("fit")
    steps = jnp.arange(fits, dtype=jnp.int32)
    place = jnp.concatenate(
        [jnp.stack([orb, fit]), (steps - fit) % fits, (orb // cols - steps) % fits, (fit + steps) % fits]
    ).astype(jnp.int32)

    def shift(x, k):
        return lax.ppermute(x, "fit", [(n, (n + k) % fits) for n in range(fits)])

    def to_orb(x):
        return lax.all_to_all(x, "orb", split_axis=0, concat_axis=0, tiled=True)

    def to_all(x):
        return lax.all_to_all(x, ("orb", "fit"), split_axis=0, concat_axis=0, tiled=True)

    low, high = blocks[: orbs // 2], blocks[orbs // 2 :]
    last0, next1 = shift(low, 1), shift(high, fits - 1)
    far0, far1 = shift(last0, 1), shift(next1, fits - 1)
    low, high, _, _ = lax.optimization_barrier((low, high, last0, next1))
    last1, next0 = shift(high, 1), shift(low, fits - 1)
    lefts = [blocks, next0, next1, far0, far1, last0, last1]
    right = pairs[::2, 1]
    groups = right.shape[0]
    info = jnp.zeros((SUB, 128), BF16).at[0, :groups].set(right.astype(BF16))
    held = to_all(pack_blocks(place, info, blocks, peers, fits))
    wanted = held[::fits, orbs, 0, :groups].astype(jnp.int32)
    spans = domains // TILE
    plan = dict(
        left=pairs[:, 0] - orb.astype(jnp.int32) * orbs,
        nleft=jnp.take(spans, pairs[:, 0]),
        nright=jnp.take(spans, right),
    )
    local = orb.astype(jnp.int32) * orbs + jnp.arange(orbs, dtype=jnp.int32)
    left_levels = (jnp.take(virt_energy, local, axis=0) - jnp.take(occ_energy, local)[:, None])[:, :, None]
    right_levels = jnp.take(virt_energy, right, axis=0) - jnp.take(occ_energy, right)[:, None]
    right_levels = lax.dynamic_slice_in_dim(
        right_levels.reshape(groups, -1, TILE), fit * (TILE // fits), TILE // fits, axis=2
    ).reshape(groups, 1, virt // fits)

    pieces = to_orb(pick_pieces(place, wanted, held, fits, after=[]))
    back, own, next0, next1, far0, far1, last0, last1 = pair_terms(
        place, plan, left_levels, right_levels, pieces, lefts, fits
    )
    returned = to_orb(back)
    far0, far1 = shift(far0, 1), shift(far1, fits - 1)
    rise, fall = merge((next0, last1), (far0, far1), (next1, last0))
    below, above = shift(rise, 1), shift(fall, fits - 1)
    total = to_all(sum_returned(place, wanted, returned, orbs, fits, after=[rise]))
    return tuple(add_all(place, own, below, above, total, fits))


def solution(mesh):
    placed = (P("orb", None, "fit"), P(), P(), P(), P("orb", None))
    return jax.shard_map(
        on_device,
        mesh=mesh,
        in_specs=placed,
        out_specs=(P("orb", None, "fit"), P("orb", None, "fit")),
        check_vma=False,
    )
```

time: 768 us -> 325 us (0.42); the launches traced: 753 us -> 324 us
  waiting for transfers between devices: 535 us -> 159 us
  matrix products: 106 us -> 0 us
  Pallas kernels: 0 us -> 68.1 us
  local copies, waits for them, and re-layouts: 57.9 us -> 13.9 us
  blocking collectives: 15.3 us -> 47.6 us
  starting transfers between devices: 13.8 us -> 30.8 us
  between operations: 14.5 us -> 1.02 us
    all_to_all x2 -> x3, waiting for transfers between devices: 371 us -> 11.7 us  [the longest x2 8.8 us: to_orb(): return lax.all_to_all(x, 'orb', split_axis=0, concat_axis=0, tiled=True)]
    psum x1 -> x0, waiting for transfers between devices: 165 us -> none  [on_device(): lax.psum(partial_value.astype(jnp.bfloat16), 'fit').astype(jnp.float32)]
    ppermute x0 -> x10, waiting for transfers between devices: none -> 147 us  [shift(): return lax.ppermute(x, 'fit', [(n, (n + k) % fits) for n in range(fits)])]
    dot_general x9 -> x0, matrix products: 106 us -> none  [the longest x1 22.3 us: on_device(): jnp.einsum('kp,pac->kac', owner_rows, own_terms, precision=lax.Precision....]
    pallas_call x0 -> x6, Pallas kernels: none -> 68.1 us  [call(): pl.pallas_call(kernel, grid=(grid,), in_specs=in_specs, out_specs=out_spe...]
    convert_element_type x2 -> x0, local copies, waits for them, and re-layouts: 33.6 us -> none  [the longest x1 16.8 us: on_device(): send_back = jnp.einsum('os,sbc->obc', group_match, group_sums, preferred_...]
    all_to_all x1, blocking collectives: 15.3 us -> 47.6 us  [to_all(): lax.all_to_all(x, ('orb', 'fit'), split_axis=0, concat_axis=0, tiled=True)]
    gather x8 -> x7, local copies, waits for them, and re-layouts: 19 us -> 4.07 us  [the longest x2 0.93 us: on_device(): jnp.take(virt_energy, local, axis=0) - jnp.take(occ_energy, local)[:, None]]
  transfers between devices with their start and end apart: 3 -> 13, of which waited for: 3 -> 8; matrix products, arithmetic and copies ran while one was open for 5% -> 3% of each run, Pallas kernels for 0% -> 4%
where the time goes in v2:
time: 325 us; the launch traced here: 324 us
  waiting for transfers between devices  159 us (49%)
  Pallas kernels  68.1 us (21%)
  blocking collectives  47.6 us (15%)
  starting transfers between devices  30.8 us (9%)
  local copies, waits for them, and re-layouts  13.9 us (4%)
  other arithmetic  3.64 us (1%)
    ppermute x10, waiting for transfers between devices, shift(): return lax.ppermute(x, 'fit', [(n, (n + k) % fits) for n in range(fits)])  147 us
    pallas_call x6, Pallas kernels, call(): pl.pallas_call(kernel, grid=(grid,), in_specs=in_specs, out_specs=out_spe...  68.1 us
    all_to_all x1, blocking collectives, to_all(): lax.all_to_all(x, ('orb', 'fit'), split_axis=0, concat_axis=0, tiled=True)  47.6 us
    all_to_all x2, starting transfers between devices, to_orb(): return lax.all_to_all(x, 'orb', split_axis=0, concat_axis=0, tiled=True)  14.7 us
    ppermute x10, starting transfers between devices, shift(): return lax.ppermute(x, 'fit', [(n, (n + k) % fits) for n in range(fits)])  9.13 us
    all_to_all x2, waiting for transfers between devices, to_orb(): return lax.all_to_all(x, 'orb', split_axis=0, concat_axis=0, tiled=True)  8.8 us
    all_to_all x1, starting transfers between devices, to_all(): lax.all_to_all(x, ('orb', 'fit'), split_axis=0, concat_axis=0, tiled=True)  6.96 us
  transfers between devices with their start and end apart: 13, of which 8 were waited for; matrix products, arithmetic and copies ran while one was open for 3% of the time, Pallas kernels for 4%

profile of v2, /device:TPU:1, one launch (start us, length us, event | category | flops | bytes accessed | tf_op | source)
XLA Modules:
  0.0 323.9 jit_solution(15040291955204176215)
XLA Ops:
  0.6 0.0 copy-start
  0.7 0.8 slice.33
  1.5 0.6 scatter.4.info_ref
  2.1 0.6 concatenate.5.place_ref
  2.7 4.4 %pack_blocks.1 = bf16[128,5,16,128]{3,2,1,0:T(8,128)(2,1)} custom-call(s32[14]{0:T(128)} %concatenate.5.place_ref, bf16[16,128]{1,0:T(8,128)(2,1)} %scatter.4.info_ref, bf16[4,512,512]{2,1,0:T(8,128)(2,1)} %refs_0_.1), custom_call_target="tpu_custom_call" | custom-call | bytes 1024 | tf_op jit(solution)/shard_map/pack_blocks/pallas_call | solution.py:31
  7.1 47.6 %all_to_all.20.held_ref = bf16[128,5,16,128]{3,2,1,0:T(8,128)(2,1)S(1)} all-to-all(bf16[128,5,16,128]{3,2,1,0:T(8,128)(2,1)} %pack_blocks.1), channel_id=1, replica_groups=mesh['orb'=32,'fit'=4] {'orb','fit'}, dimensions={0} | all-to-all | bytes 5242880 | tf_op jit(solution)/shard_map/all_to_all | solution.py:365
  54.8 0.7 fusion.1.wanted_ref
  55.4 0.8 copy-done.4
  56.2 5.5 %pick_pieces.1 = bf16[32,32,16,128]{3,2,1,0:T(8,128)(2,1)} custom-call(s32[14]{0:T(128)} %concatenate.5.place_ref, s32[32,8]{1,0:T(8,128)} %fusion.1.wanted_ref, bf16[128,5,16,128]{3,2,1,0:T(8,128)(2,1)} %copy-done.4), custom_call_target="tpu_custom_call" | custom-call | bytes 1024 | tf_op jit(solution)/shard_map/pick_pieces/pallas_call | solution.py:31
  61.8 4.9 %all-to-all-start.1 = ((bf16[32,32,16,128]{3,2,1,0:T(8,128)(2,1)}), bf16[32,32,16,128]{3,2,1,0:T(8,128)(2,1)}, u32[]{:S(2)}, u32[]{:S(2)}) async-start(bf16[32,32,16,128]{3,2,1,0:T(8,128)(2,1)} %pick_pieces.1), calls=%async_computation.1 | async-start | bytes 8388608 | tf_op jit(solution)/shard_map/all_to_all | solution.py:362
  66.7 0.0 copy-start.2
  66.7 0.0 copy-start.15
  66.7 0.0 copy-start.12
  66.7 1.1 fusion.9
  67.8 0.9 collective-permute-start.1
  68.8 0.5 collective-permute-start
  69.3 0.6 gather_fusion.3
  70.0 0.6 gather_fusion.5
  70.6 0.0 copy-done
  70.6 0.6 gather_fusion.2
  71.2 0.6 gather_fusion.4
  71.8 0.6 gather_fusion.1
  72.4 0.5 fusion.8
  72.9 0.7 gather_fusion
  73.6 0.1 constant_dynamic-slice_fusion
  73.7 0.1 fusion
  73.8 0.7 reshape.148.high_ref
  74.5 0.4 copy.14
  74.8 17.4 %collective-permute-done.1.refs_2_ = bf16[2,512,512]{2,1,0:T(8,128)(2,1)S(1)} collective-permute-done((bf16[2,512,512]{2,1,0:T(8,128)(2,1)S(1)}, bf16[2,512,512]{2,1,0:T(8,128)(2,1)S(1)}, u32[]{:S(2)}, u32[]{:S(2)}) %collective-permute-start.1) | collective-permute-done | bytes 1048608 | tf_op jit(solution)/shard_map/ppermute | solution.py:359
  92.2 2.0 collective-permute-done.refs_5_
  94.3 0.1 collective-permute-start.2
  94.4 1.4 collective-permute-start.5
  95.8 1.3 collective-permute-start.4
  97.1 0.2 collective-permute-start.3
  97.3 0.6 broadcast_select_fusion.1.nright_ref
  97.8 0.6 bitcast_select_fusion.nleft_ref
  98.4 1.1 select_subtract_fusion.low_ref
  99.6 40.6 %collective-permute-done.4.refs_4_ = bf16[2,512,512]{2,1,0:T(8,128)(2,1)S(1)} collective-permute-done((bf16[2,512,512]{2,1,0:T(8,128)(2,1)S(1)}, bf16[2,512,512]{2,1,0:T(8,128)(2,1)S(1)}, u32[]{:S(2)}, u32[]{:S(2)}) %collective-permute-start.4) | collective-permute-done | bytes 1048608 | tf_op jit(solution)/shard_map/ppermute | solution.py:359
  140.1 0.0 collective-permute-done.2.refs_1_
  140.2 0.0 collective-permute-done.5.refs_6_
  140.2 1.0 copy-done.11
  141.1 0.4 copy-done.9
  141.5 1.0 copy-done.10
  142.5 0.0 collective-permute-done.3.refs_3_
  142.5 0.0 all-to-all-done.1.pieces_ref
  142.5 38.4 %pair_terms.1 = (bf16[32,32,16,128]{3,2,1,0:T(8,128)(2,1)}, bf16[4,512,640]{2,1,0:T(8,128)(2,1)}, bf16[2,512,640]{2,1,0:T(8,128)(2,1)}, bf16[2,512,640]{2,1,0:T(...) custom-call(s32[14]{0:T(128)} %concatenate.5.place_ref, ...), custom_call_target="tpu_custom_call" | custom-call | bytes 1024 | tf_op jit(solution)/shard_map/pair_terms/pallas_call | solution.py:31
  180.9 9.8 %all-to-all-start.2 = ((bf16[32,32,16,128]{3,2,1,0:T(8,128)(2,1)}), bf16[32,32,16,128]{3,2,1,0:T(8,128)(2,1)}, u32[]{:S(2)}, u32[]{:S(2)}) async-start(bf16[32,32,16,128]{3,2,1,0:T(8,128)(2,1)} %get-tuple-element.37), calls=%async_computation.2 | async-start | bytes 8388608 | tf_op jit(solution)/shard_map/all_to_all | solution.py:362
  190.7 0.1 collective-permute-start.6
  190.8 2.7 collective-permute-start.7
  193.5 28.7 %collective-permute-done.6.c_ref = bf16[2,512,640]{2,1,0:T(8,128)(2,1)S(1)} collective-permute-done((bf16[2,512,640]{2,1,0:T(8,128)(2,1)S(1)}, bf16[2,512,640]{2,1,0:T(8,128)(2,1)S(1)}, u32[]{:S(2)}, u32[]{:S(2)}) %collective-permute-start.6) | collective-permute-done | bytes 1310752 | tf_op jit(solution)/shard_map/ppermute | solution.py:359
  222.2 0.0 collective-permute-done.7.d_ref
  222.2 1.1 copy-done.6
  223.2 0.4 copy-done.7
  223.6 6.6 %merge.1 = (bf16[4,512,640]{2,1,0:T(8,128)(2,1)}, bf16[4,512,640]{2,1,0:T(8,128)(2,1)}) custom-call(bf16[2,512,640]{2,1,0:T(8,128)(2,1)} %get-tuple-element.29.a_ref, bf16[2,512,640]{2,1,0:T(8,128)(2,1)} %get-tuple-element.30.b_ref, bf16[2,512,640]{2,1,0:T(8,128)(2,1)} %copy-done.6, bf16[2,512,640]{2,1,0:T(8,128)(2,1)} %copy-done.7, ...), custom_call_target="tpu_custom_call" | custom-call | bytes 1024 | tf_op jit(solution)/shard_map/merge/pallas_call | solution.py:31
  230.2 2.0 collective-permute-start.9
  232.2 0.0 collective-permute-start.8
  232.2 8.8 %all-to-all-done.2.part_ref = bf16[32,32,16,128]{3,2,1,0:T(8,128)(2,1)} async-done(((bf16[32,32,16,128]{3,2,1,0:T(8,128)(2,1)}), bf16[32,32,16,128]{3,2,1,0:T(8,128)(2,1)}, u32[]{:S(2)}, u32[]{:S(2)}) %all-to-all-start.2) | async-done | bytes 4194336 | tf_op jit(solution)/shard_map/all_to_all | solution.py:362
  241.0 5.6 %sum_returned.1 = bf16[128,4,16,128]{3,2,1,0:T(8,128)(2,1)} custom-call(s32[14]{0:T(128)} %concatenate.5.place_ref, s32[32,8]{1,0:T(8,128)} %fusion.1.wanted_ref, bf16[32,32,16,128]{3,2,1,0:T(8,128)(2,1)} %all-to-all-done.2.part_ref, bf16[4,512,640]{2,1,0:T(8,128)(2,1)} %get-tuple-element.35.refs_0_), custom_call_target="tpu_custom_call" | custom-call | bytes 1024 | tf_op jit(solution)/shard_map/sum_returned/pallas_call | solution.py:31
  246.6 7.0 %all-to-all-start.3 = ((bf16[128,4,16,128]{3,2,1,0:T(8,128)(2,1)}), bf16[128,4,16,128]{3,2,1,0:T(8,128)(2,1)S(1)}, u32[]{:S(2)}, u32[]{:S(2)}) async-start(bf16[128,4,16,128]{3,2,1,0:T(8,128)(2,1)} %sum_returned.1), calls=%async_computation.3 | async-start | bytes 4194304 | tf_op jit(solution)/shard_map/all_to_all | solution.py:365
  253.5 55.4 %collective-permute-done.9.above_ref = bf16[4,512,640]{2,1,0:T(8,128)(2,1)} collective-permute-done((bf16[4,512,640]{2,1,0:T(8,128)(2,1)}, bf16[4,512,640]{2,1,0:T(8,128)(2,1)}, u32[]{:S(2)}, u32[]{:S(2)}) %collective-permute-start.9) | collective-permute-done | bytes 2621472 | tf_op jit(solution)/shard_map/ppermute | solution.py:359
  308.9 2.9 collective-permute-done.8.below_ref
  311.8 2.9 all-to-all-done.3.sums_ref
  314.8 1.4 copy-done.5
  316.1 7.6 %add_all.1 = (f32[4,512,512]{2,1,0:T(8,128)}, f32[4,512,128]{2,1,0:T(8,128)}) custom-call(s32[14]{0:T(128)} %concatenate.5.place_ref, bf16[4,512,640]{2,1,0:T(8,128)(2,1)} %get-tuple-element.28.own_ref, bf16[4,512,640]{2,1,0:T(8,128)(2,1)} %collective-permute-done.8.below_ref, bf16[4,512,640]{2,1,0:T(8,128)(2,1)} %collective-permute-done.9.above_ref, ...), custom_call_target="tpu_custom_call" | custom-call | bytes 1024 | tf_op jit(solution)/shard_map/add_all/pallas_call | solution.py:31
  (32 shorter events, 0.1 us)
Async XLA Ops:
  0.6 70.0 %copy-start = (f32[128,512]{1,0:T(8,128)S(1)}, f32[128,512]{1,0:T(8,128)}, u32[]{:S(2)}) copy-start(f32[128,512]{1,0:T(8,128)} %param.9) | copy-start | bytes 786436
  54.8 1.5 copy-start.4
  61.8 4.9 %copy-start.3 = (bf16[4,512,512]{2,1,0:T(8,128)(2,1)S(1)}, bf16[4,512,512]{2,1,0:T(8,128)(2,1)}, u32[]{:S(2)}) copy-start(bf16[4,512,512]{2,1,0:T(8,128)(2,1)} %refs_0_.1) | copy-start | bytes 6291460
  61.8 80.7 %all-to-all-start.1 = ((bf16[32,32,16,128]{3,2,1,0:T(8,128)(2,1)}), bf16[32,32,16,128]{3,2,1,0:T(8,128)(2,1)}, u32[]{:S(2)}, u32[]{:S(2)}) async-start(bf16[32,32,16,128]{3,2,1,0:T(8,128)(2,1)} %pick_pieces.1), calls=%async_computation.1 | async-start | bytes 8388608 | tf_op jit(solution)/shard_map/all_to_all | solution.py:362
  66.7 2.6 copy-start.2
  66.7 5.1 %copy-start.15 = (s32[128]{0:T(128)S(1)}, s32[128]{0:T(128)}, u32[]{:S(2)}) copy-start(s32[128]{0:T(128)} %param.10) | copy-start | bytes 1540
  66.7 5.7 %copy-start.12 = (s32[16,2]{0,1:T(2,128)S(1)}, s32[16,2]{0,1:T(2,128)}, u32[]{:S(2)}) copy-start(s32[16,2]{0,1:T(2,128)} %param.11) | copy-start | bytes 388
  67.8 24.4 %collective-permute-start.1 = (bf16[2,512,512]{2,1,0:T(8,128)(2,1)S(1)}, bf16[2,512,512]{2,1,0:T(8,128)(2,1)S(1)}, u32[]{:S(2)}, u32[]{:S(2)}) collective-permute-start(bf16[2,512,512]{2,1,0:T(8,128)(2,1)S(1)} %get-tuple-element.27), channel_id=1, source_target_pairs={{0,3},{1,0},{2,1},{3,2},{4,7},{5,4},{6,5},{7,6},{8,11},{9,8},{10,9... | collective-permute-start | bytes 3145736 | tf_op jit(solution)/shard_map/ppermute | solution.py:359
  68.8 25.5 %collective-permute-start = (bf16[2,512,512]{2,1,0:T(8,128)(2,1)}, bf16[2,512,512]{2,1,0:T(8,128)(2,1)}, u32[]{:S(2)}, u32[]{:S(2)}) collective-permute-start(bf16[2,512,512]{2,1,0:T(8,128)(2,1)} %get-tuple-element.26), channel_id=1, source_target_pairs={{0,1},{1,2},{2,3},{3,0},{4,5},{5,6},{6,7},{7,4},{8,9},{9,10},{10,1... | collective-permute-start | bytes 3145736 | tf_op jit(solution)/shard_map/ppermute | solution.py:359
  92.2 50.2 %copy-start.8 = (bf16[2,512,512]{2,1,0:T(8,128)(2,1)}, bf16[2,512,512]{2,1,0:T(8,128)(2,1)S(1)}, u32[]{:S(2)}) copy-start(bf16[2,512,512]{2,1,0:T(8,128)(2,1)S(1)} %collective-permute-done.1.refs_2_) | copy-start | bytes 3145732
  94.3 45.9 %collective-permute-start.2 = (bf16[2,512,512]{2,1,0:T(8,128)(2,1)}, bf16[2,512,512]{2,1,0:T(8,128)(2,1)S(1)}, u32[]{:S(2)}, u32[]{:S(2)}) collective-permute-start(bf16[2,512,512]{2,1,0:T(8,128)(2,1)} %get-tuple-element.26), channel_id=1, source_target_pairs={{0,3},{1,0},{2,1},{3,2},{4,7},{5,4},{6,5},{7,6},{8,11},{9,8},{10,9... | collective-permute-start | bytes 3145736 | tf_op jit(solution)/shard_map/ppermute | solution.py:359
  94.4 45.8 %collective-permute-start.5 = (bf16[2,512,512]{2,1,0:T(8,128)(2,1)S(1)}, bf16[2,512,512]{2,1,0:T(8,128)(2,1)S(1)}, u32[]{:S(2)}, u32[]{:S(2)}) collective-permute-start(bf16[2,512,512]{2,1,0:T(8,128)(2,1)S(1)} %get-tuple-element.27), channel_id=1, source_target_pairs={{0,1},{1,2},{2,3},{3,0},{4,5},{5,6},{6,7},{7,4},{8,9},{9,10},{10,1... | collective-permute-start | bytes 3145736 | tf_op jit(solution)/shard_map/ppermute | solution.py:359
  95.8 44.4 %collective-permute-start.4 = (bf16[2,512,512]{2,1,0:T(8,128)(2,1)S(1)}, bf16[2,512,512]{2,1,0:T(8,128)(2,1)S(1)}, u32[]{:S(2)}, u32[]{:S(2)}) collective-permute-start(bf16[2,512,512]{2,1,0:T(8,128)(2,1)S(1)} %collective-permute-done.1.refs_2_), channel_id=1, source_target_pairs={{0,3},{1,0},{2,1},{3,2},{4,7},{5,4},{6,5},{7,6},{8,11},{9,8},{10,9... | collective-permute-start | bytes 3145736 | tf_op jit(solution)/shard_map/ppermute | solution.py:359
  97.1 45.4 %collective-permute-start.3 = (bf16[2,512,512]{2,1,0:T(8,128)(2,1)}, bf16[2,512,512]{2,1,0:T(8,128)(2,1)}, u32[]{:S(2)}, u32[]{:S(2)}) collective-permute-start(bf16[2,512,512]{2,1,0:T(8,128)(2,1)} %collective-permute-done.refs_5_), channel_id=1, source_target_pairs={{0,1},{1,2},{2,3},{3,0},{4,5},{5,6},{6,7},{7,4},{8,9},{9,10},{10,1... | collective-permute-start | bytes 3145736 | tf_op jit(solution)/shard_map/ppermute | solution.py:359
  140.1 1.0 copy-start.11
  140.1 1.3 copy-start.9
  141.5 1.0 copy-start.10
  180.9 9.8 %copy-start.14 = (bf16[2,512,640]{2,1,0:T(8,128)(2,1)S(1)}, bf16[2,512,640]{2,1,0:T(8,128)(2,1)}, u32[]{:S(2)}) copy-start(bf16[2,512,640]{2,1,0:T(8,128)(2,1)} %get-tuple-element.31) | copy-start | bytes 3932164
  180.9 9.9 %copy-start.13 = (bf16[2,512,640]{2,1,0:T(8,128)(2,1)S(1)}, bf16[2,512,640]{2,1,0:T(8,128)(2,1)}, u32[]{:S(2)}) copy-start(bf16[2,512,640]{2,1,0:T(8,128)(2,1)} %get-tuple-element.32) | copy-start | bytes 3932164
  180.9 60.1 %all-to-all-start.2 = ((bf16[32,32,16,128]{3,2,1,0:T(8,128)(2,1)}), bf16[32,32,16,128]{3,2,1,0:T(8,128)(2,1)}, u32[]{:S(2)}, u32[]{:S(2)}) async-start(bf16[32,32,16,128]{3,2,1,0:T(8,128)(2,1)} %get-tuple-element.37), calls=%async_computation.2 | async-start | bytes 8388608 | tf_op jit(solution)/shard_map/all_to_all | solution.py:362
  190.7 31.4 %collective-permute-start.6 = (bf16[2,512,640]{2,1,0:T(8,128)(2,1)S(1)}, bf16[2,512,640]{2,1,0:T(8,128)(2,1)S(1)}, u32[]{:S(2)}, u32[]{:S(2)}) collective-permute-start(bf16[2,512,640]{2,1,0:T(8,128)(2,1)S(1)} %copy-done.14), channel_id=1, source_target_pairs={{0,1},{1,2},{2,3},{3,0},{4,5},{5,6},{6,7},{7,4},{8,9},{9,10},{10,1... | collective-permute-start | bytes 3932168 | tf_op jit(solution)/shard_map/ppermute | solution.py:359
  190.8 31.4 %collective-permute-start.7 = (bf16[2,512,640]{2,1,0:T(8,128)(2,1)S(1)}, bf16[2,512,640]{2,1,0:T(8,128)(2,1)S(1)}, u32[]{:S(2)}, u32[]{:S(2)}) collective-permute-start(bf16[2,512,640]{2,1,0:T(8,128)(2,1)S(1)} %copy-done.13), channel_id=1, source_target_pairs={{0,3},{1,0},{2,1},{3,2},{4,7},{5,4},{6,5},{7,6},{8,11},{9,8},{10,9... | collective-permute-start | bytes 3932168 | tf_op jit(solution)/shard_map/ppermute | solution.py:359
  222.2 1.1 copy-start.6
  222.2 1.5 copy-start.7
  230.2 78.7 %collective-permute-start.9 = (bf16[4,512,640]{2,1,0:T(8,128)(2,1)}, bf16[4,512,640]{2,1,0:T(8,128)(2,1)}, u32[]{:S(2)}, u32[]{:S(2)}) collective-permute-start(bf16[4,512,640]{2,1,0:T(8,128)(2,1)} %get-tuple-element.36), channel_id=1, source_target_pairs={{0,3},{1,0},{2,1},{3,2},{4,7},{5,4},{6,5},{7,6},{8,11},{9,8},{10,9... | collective-permute-start | bytes 7864328 | tf_op jit(solution)/shard_map/ppermute | solution.py:359
  232.2 79.7 %collective-permute-start.8 = (bf16[4,512,640]{2,1,0:T(8,128)(2,1)}, bf16[4,512,640]{2,1,0:T(8,128)(2,1)}, u32[]{:S(2)}, u32[]{:S(2)}) collective-permute-start(bf16[4,512,640]{2,1,0:T(8,128)(2,1)} %get-tuple-element.35.refs_0_), channel_id=1, source_target_pairs={{0,1},{1,2},{2,3},{3,0},{4,5},{5,6},{6,7},{7,4},{8,9},{9,10},{10,1... | collective-permute-start | bytes 7864328 | tf_op jit(solution)/shard_map/ppermute | solution.py:359
  246.6 68.2 %all-to-all-start.3 = ((bf16[128,4,16,128]{3,2,1,0:T(8,128)(2,1)}), bf16[128,4,16,128]{3,2,1,0:T(8,128)(2,1)S(1)}, u32[]{:S(2)}, u32[]{:S(2)}) async-start(bf16[128,4,16,128]{3,2,1,0:T(8,128)(2,1)} %sum_returned.1), calls=%async_computation.3 | async-start | bytes 4194304 | tf_op jit(solution)/shard_map/all_to_all | solution.py:365
  314.8 1.4 copy-start.5
  314.8 9.0 %copy-start.1 = (f32[128,512]{1,0:T(8,128)S(1)}, f32[128,512]{1,0:T(8,128)}, u32[]{:S(2)}) copy-start(f32[128,512]{1,0:T(8,128)} %param.9) | copy-start | bytes 786436

commit v3 on v2

--- a/solution.py
+++ b/solution.py
@@ -8,6 +8,7 @@
 TILE = 128
 SUB = 16
 WIDE = 256
+DIGITS = ((2, 1), (4, 2), (4, 8))
 F32 = jnp.float32
 BF16 = jnp.bfloat16
 MIB = 1024 * 1024
@@ -27,7 +28,7 @@
     return pl.BlockSpec(shape, lambda n: (0,) * len(shape))
 
 
-def call(kernel, grid, in_specs, out_specs, out_shape, args, scratch=(), memory=56, name=None):
+def call(kernel, grid, in_specs, out_specs, out_shape, args, scratch=(), memory=56, aliases=None, name=None):
     return pl.pallas_call(
         kernel,
         grid=(grid,),
@@ -37,6 +38,7 @@
         scratch_shapes=list(scratch),
         compiler_params=pltpu.CompilerParams(vmem_limit_bytes=memory * MIB),
         cost_estimate=pl.CostEstimate(flops=0, bytes_accessed=1024, transcendentals=0),
+        input_output_aliases=aliases or {},
         name=name,
     )(*args)
 
@@ -45,40 +47,43 @@
     return m // (fits * cols), m // cols % fits, m % cols
 
 
-def pack_blocks(place, info, blocks, peers, fits):
+def list_row(me, d):
+    return sum(((me // stride - d // stride) & (count - 1)) * stride for count, stride in DIGITS)
+
+
+def pack_blocks(place, blocks, peers, fits):
     orbs, virt, aux = blocks.shape
     cols = aux // 128
     rows = TILE // fits
-
-    def kernel(place_ref, info_ref, blocks_ref, out_ref):
-        @pl.when(pl.program_id(0) < orbs)
-        def _():
-            for m in range(peers):
-                h, turned, c = device_of(m, fits, cols)
-                tile = place_ref[BACK + turned] * TILE
-                for z in range(fits):
-                    at = pl.multiple_of(tile + z * rows + h * SUB, SUB)
-                    out_ref[m * fits + z, 0] = blocks_ref[0, pl.ds(at, SUB), c * 128 : (c + 1) * 128]
-
-        @pl.when(pl.program_id(0) == orbs)
-        def _():
-            for m in range(peers * fits):
-                out_ref[m, 0] = info_ref[...]
-
-    return call(
-        kernel,
-        orbs + 1,
-        [SMEM, whole(info.shape), pl.BlockSpec((1, virt, aux), lambda k: (jnp.minimum(k, orbs - 1), 0, 0))],
-        pl.BlockSpec((peers * fits, 1, SUB, 128), lambda k: (0, k, 0, 0)),
-        sds((peers * fits, orbs + 1, SUB, 128), BF16),
-        (place, info, blocks),
+    steps = 4
+    block = peers // steps
+
+    def kernel(place_ref, blocks_ref, out_ref):
+        @pl.loop(0, block)
+        def _(n):
+            m = pl.program_id(0) * block + n
+            h, turned, c = m // (fits * cols), m // cols % fits, m % cols
+            tile = place_ref[BACK + turned] * TILE
+            lanes = pl.ds(pl.multiple_of(c * 128, 128), 128)
+            for z in range(fits):
+                at = pl.ds(pl.multiple_of(tile + z * rows + h * SUB, SUB), SUB)
+                for k in range(orbs):
+                    out_ref[n * fits + z, k] = blocks_ref[k, at, lanes]
+
+    return call(
+        kernel,
+        steps,
+        [SMEM, whole(blocks.shape)],
+        pl.BlockSpec((block * fits, orbs, SUB, 128), lambda n: (n, 0, 0, 0)),
+        sds((peers * fits, orbs, SUB, 128), BF16),
+        (place, blocks),
         name="pack_blocks",
     )
 
 
 def pick_pieces(place, wanted, held, fits, after):
     peers, count = wanted.shape
-    orbs = held.shape[1] - 1
+    orbs = held.shape[1]
     block = peers // 4
 
     def kernel(place_ref, wanted_ref, held_ref, *refs):
@@ -88,8 +93,9 @@
 
         @pl.loop(0, block)
         def _(d):
+            row = list_row(place_ref[ORB], first + d)
             for g in range(count):
-                j = wanted_ref[first + d, g]
+                j = wanted_ref[row, g]
                 source, k = lax.div(j, orbs) * fits, lax.rem(j, orbs)
                 for s in range(fits):
                     out_ref[d, g * fits + s] = held_ref[source + parts[s], k]
@@ -106,7 +112,7 @@
 
 
 def pair_terms(place, plan, left_levels, right_levels, pieces, lefts, fits):
-    orbs, virt, aux = lefts[0].shape
+    orbs, virt, aux = lefts[0][0].shape
     peers, count = pieces.shape[0], pieces.shape[1] // fits
     tiles, cols = virt // TILE, aux // 128
     rows = TILE // fits
@@ -117,13 +123,13 @@
 
     def kernel(place_ref, left_ref, nleft_ref, nright_ref, low_ref, high_ref, pieces_ref, *refs):
         sources, refs = refs[: len(lefts)], refs[len(lefts) :]
-        out_ref, own_ref, *parts = refs[: 2 * fits]
-        lefts_ref, rows_ref, turned_ref, amp_ref, all_ref, square_ref, sems = refs[2 * fits :]
+        out_ref, all_out_ref, rows_out_ref, *far_refs = refs[:5]
+        lefts_ref, rows_ref, turned_ref, amp_ref, all_ref, sems = refs[5:]
         n = pl.program_id(0)
-        targets = [lefts_ref.at[0]]
-        for s in range(1, fits):
-            targets += [lefts_ref.at[s, 0:half], lefts_ref.at[s, half:orbs]]
-        copies = [pltpu.make_async_copy(a, b, sems.at[k]) for k, (a, b) in enumerate(zip(sources, targets))]
+        copies = [
+            pltpu.make_async_copy(source, lefts_ref.at[s, first : first + array.shape[0]], sems.at[k])
+            for k, (source, (array, s, first)) in enumerate(zip(sources, lefts))
+        ]
 
         @pl.when(n == 0)
         def _():
@@ -145,6 +151,7 @@
                 for copy in copies:
                     copy.wait()
 
+            rows_out_ref[0] = rows_ref[g]
             turned_ref[...] = rows_ref[g].T
             row_id = lax.broadcasted_iota(jnp.int32, (WIDE, taken), 0)
             col_id = lax.broadcasted_iota(jnp.int32, (WIDE, taken), 1)
@@ -189,18 +196,8 @@
             @pl.when((n >= count + low * half) & (n < count + (low + 1) * half))
             def _(low=low):
                 k = n - count
-                square_ref[...] = lax.dot_general(
-                    all_ref[k], all_ref[k], (((1,), (1,)), ((), ())), preferred_element_type=F32
-                ).astype(BF16)
-                for s, target in enumerate([own_ref, *[parts[2 * s + low] for s in range(fits - 1)]]):
-                    for start in range(0, aux, WIDE):
-                        at = slice(s * aux + start, s * aux + start + WIDE)
-                        right = rows_ref[:, :, at].reshape(count * taken, WIDE)
-                        target[0, :, start : start + WIDE] = jnp.dot(
-                            all_ref[k], right, preferred_element_type=F32
-                        ).astype(BF16)
-                    mine = pl.ds(pl.multiple_of(place_ref[NEXT + s] * wide, wide), wide)
-                    target[0, :, aux : aux + wide] = square_ref[:, mine]
+                all_out_ref[0] = all_ref[k]
+                sum_part(place_ref, all_ref.at[k], rows_ref, fits // 2, far_refs[low])
 
     block = (1, virt, aux + wide)
     places = [
@@ -219,52 +216,85 @@
         + [ANY] * len(lefts),
         [
             pl.BlockSpec((peers, tiles, SUB, 128), lambda n: (0, jnp.minimum(n, count - 1), 0, 0)),
-            pl.BlockSpec(block, lambda n: (jnp.maximum(n - count, 0), 0, 0)),
         ]
-        + places * (fits - 1),
-        [sds((peers, count * tiles, SUB, 128), BF16), sds((orbs, virt, aux + wide), BF16)]
-        + [sds((half, virt, aux + wide), BF16)] * (2 * (fits - 1)),
-        (place, *[plan[n] for n in names], left_levels, right_levels, pieces, *lefts),
+        + [
+            pl.BlockSpec((1, virt, count * taken), lambda n: (jnp.maximum(n - count, 0), 0, 0)),
+            pl.BlockSpec((1, taken, fits * aux), lambda n: (jnp.minimum(n, count - 1), 0, 0)),
+        ]
+        + places,
+        [
+            sds((peers, count * tiles, SUB, 128), BF16),
+            sds((orbs, virt, count * taken), BF16),
+            sds((count, taken, fits * aux), BF16),
+        ]
+        + [sds((half, virt, aux + wide), BF16)] * 2,
+        (place, *[plan[n] for n in names], left_levels, right_levels, pieces, *[array for array, _, _ in lefts]),
         scratch=[
             pltpu.VMEM((fits, orbs, virt, aux), BF16),
             pltpu.VMEM((count, taken, fits * aux), BF16),
             pltpu.VMEM((fits * aux, taken), BF16),
             pltpu.VMEM((2, taken, virt), BF16),
             pltpu.VMEM((orbs, virt, count * taken), BF16),
-            pltpu.VMEM((virt, virt), BF16),
             pltpu.SemaphoreType.DMA((len(lefts),)),
         ],
         name="pair_terms",
     )
 
 
-def merge(mine, came, straight):
-    half, virt, width = came[0].shape
-
-    def kernel(a_ref, b_ref, c_ref, d_ref, e_ref, f_ref, up_ref, down_ref):
-        n = pl.program_id(0)
-
-        @pl.when(n < half)
-        def _():
-            up_ref[...] = (a_ref[...].astype(F32) + c_ref[...].astype(F32)).astype(BF16)
-            down_ref[...] = f_ref[...]
-
-        @pl.when(n >= half)
-        def _():
-            up_ref[...] = e_ref[...]
-            down_ref[...] = (b_ref[...].astype(F32) + d_ref[...].astype(F32)).astype(BF16)
+def sum_part(place_ref, all_ref, rows_ref, s, out_ref):
+    virt, depth = all_ref.shape
+    aux = out_ref.shape[2] * rows_ref.shape[2] // (rows_ref.shape[2] + virt)
+    wide = out_ref.shape[2] - aux
+    for start in range(0, aux, WIDE):
+        right = rows_ref[:, :, s * aux + start : s * aux + start + WIDE].reshape(depth, WIDE)
+        out_ref[0, :, start : start + WIDE] = jnp.dot(
+            all_ref[...], right, preferred_element_type=F32
+        ).astype(BF16)
+    mine = pl.ds(pl.multiple_of(place_ref[NEXT + s] * wide, wide), wide)
+    out_ref[0, :, aux : aux + wide] = lax.dot_general(
+        all_ref[...], all_ref[mine, :], (((1,), (1,)), ((), ())), preferred_element_type=F32
+    ).astype(BF16)
+
+
+def near_terms(place, amps, rows, fits):
+    orbs, virt, depth = amps.shape
+    aux = rows.shape[2] // fits
+    block = (1, virt, aux + virt // fits)
+
+    def kernel(place_ref, all_ref, rows_ref, *out_refs):
+        for s, out_ref in zip((0, 1, fits - 1), out_refs):
+            sum_part(place_ref, all_ref.at[0], rows_ref, s, out_ref)
+
+    return call(
+        kernel,
+        orbs,
+        [SMEM, pl.BlockSpec((1, virt, depth), lambda k: (k, 0, 0)), whole(rows.shape)],
+        [pl.BlockSpec(block, lambda k: (k, 0, 0))] * 3,
+        [sds((orbs, *block[1:]), BF16)] * 3,
+        (place, amps, rows),
+        name="near_terms",
+    )
+
+
+def merge(rise, fall, far):
+    orbs, virt, width = rise.shape
+    half = orbs // 2
+
+    def kernel(a_ref, b_ref, c_ref, d_ref, up_ref, down_ref):
+        up_ref[...] = (a_ref[...].astype(F32) + c_ref[...].astype(F32)).astype(BF16)
+        down_ref[...] = (b_ref[...].astype(F32) + d_ref[...].astype(F32)).astype(BF16)
 
     block = (1, virt, width)
-    first = pl.BlockSpec(block, lambda n: (jnp.minimum(n, half - 1), 0, 0))
-    second = pl.BlockSpec(block, lambda n: (jnp.maximum(n - half, 0), 0, 0))
-    every = pl.BlockSpec(block, lambda n: (n, 0, 0))
-    return call(
-        kernel,
-        2 * half,
-        [first, second, first, second, second, first],
-        [every] * 2,
-        [sds((2 * half, virt, width), BF16)] * 2,
-        (*mine, *came, *straight),
+    low = pl.BlockSpec(block, lambda n: (n, 0, 0))
+    high = pl.BlockSpec(block, lambda n: (n + half, 0, 0))
+    return call(
+        kernel,
+        half,
+        [low, high, low, low],
+        [low, high],
+        [sds(rise.shape, BF16)] * 2,
+        (rise, fall, *far),
+        aliases={0: 0, 1: 1},
         name="merge",
     )
 
@@ -285,8 +315,9 @@
 
         @pl.loop(0, block)
         def _(d):
+            row = list_row(place_ref[ORB], n * block + d)
             for g in range(count):
-                spot = pl.ds(wanted_ref[n * block + d, g] * tiles, tiles)
+                spot = pl.ds(wanted_ref[row, g] * tiles, tiles)
                 total_ref[spot] += part_ref[d, g * tiles : (g + 1) * tiles].astype(F32)
 
         @pl.when(n == steps - 1)
@@ -321,6 +352,7 @@
     peers = sums.shape[0] // fits
 
     def kernel(place_ref, own_ref, below_ref, above_ref, sums_ref, gamma_ref, dens_ref):
+        k = pl.program_id(0)
         total = own_ref[0].astype(F32) + below_ref[0].astype(F32) + above_ref[0].astype(F32)
         gamma_ref[0] = total[:, 0:aux]
         dens_ref[0] = total[:, aux:width]
@@ -330,13 +362,13 @@
             lanes = slice(c * 128, (c + 1) * 128)
             for z in range(fits):
                 at = pl.ds(pl.multiple_of(tile + z * rows + h * SUB, SUB), SUB)
-                gamma_ref[0, at, lanes] += sums_ref[m * fits + z, 0].astype(F32)
+                gamma_ref[0, at, lanes] += sums_ref[m * fits + z, k].astype(F32)
 
     block = pl.BlockSpec((1, virt, width), lambda k: (k, 0, 0))
     return call(
         kernel,
         orbs,
-        [SMEM, block, block, block, pl.BlockSpec((peers * fits, 1, SUB, 128), lambda k: (0, k, 0, 0))],
+        [SMEM, block, block, block, whole(sums.shape)],
         [pl.BlockSpec((1, virt, aux), lambda k: (k, 0, 0)), pl.BlockSpec((1, virt, wide), lambda k: (k, 0, 0))],
         [sds((orbs, virt, aux), F32), sds((orbs, virt, wide), F32)],
         (place, own, below, above, sums),
@@ -364,17 +396,22 @@
     def to_all(x):
         return lax.all_to_all(x, ("orb", "fit"), split_axis=0, concat_axis=0, tiled=True)
 
-    low, high = blocks[: orbs // 2], blocks[orbs // 2 :]
-    last0, next1 = shift(low, 1), shift(high, fits - 1)
-    far0, far1 = shift(last0, 1), shift(next1, fits - 1)
-    low, high, _, _ = lax.optimization_barrier((low, high, last0, next1))
-    last1, next0 = shift(high, 1), shift(low, fits - 1)
-    lefts = [blocks, next0, next1, far0, far1, last0, last1]
+    half = orbs // 2
+    one = [blocks[k : k + 1] for k in range(orbs)]
+    last0, next3 = shift(one[0], 1), shift(one[3], fits - 1)
     right = pairs[::2, 1]
     groups = right.shape[0]
-    info = jnp.zeros((SUB, 128), BF16).at[0, :groups].set(right.astype(BF16))
-    held = to_all(pack_blocks(place, info, blocks, peers, fits))
-    wanted = held[::fits, orbs, 0, :groups].astype(jnp.int32)
+    held = to_all(pack_blocks(place, blocks, peers, fits))
+    wanted = jnp.pad(right[None], ((0, 0), (0, 128 - groups)))
+    for count, stride in DIGITS:
+        wanted = jnp.concatenate(
+            [wanted]
+            + [
+                lax.ppermute(wanted, "orb", [(n, n + ((n // stride + k) % count - n // stride % count) * stride) for n in range(peers)])
+                for k in range(1, count)
+            ]
+        )
+    wanted = wanted[:, :groups]
     spans = domains // TILE
     plan = dict(
         left=pairs[:, 0] - orb.astype(jnp.int32) * orbs,
@@ -388,13 +425,20 @@
         right_levels.reshape(groups, -1, TILE), fit * (TILE // fits), TILE // fits, axis=2
     ).reshape(groups, 1, virt // fits)
 
-    pieces = to_orb(pick_pieces(place, wanted, held, fits, after=[]))
-    back, own, next0, next1, far0, far1, last0, last1 = pair_terms(
-        place, plan, left_levels, right_levels, pieces, lefts, fits
-    )
+    pieces = to_orb(pick_pieces(place, wanted, held, fits, after=[last0, next3]))
+    last1, next2 = shift(one[1], 1), shift(one[2], fits - 1)
+    far0, far3 = shift(last0, 1), shift(next3, fits - 1)
+    low, high, last1, next2 = lax.optimization_barrier((blocks[:half], blocks[half:], last1, next2))
+    last2, next0 = shift(high, 1), shift(low, fits - 1)
+    far1, far2 = shift(last1, 1), shift(next2, fits - 1)
+    lefts = [(blocks, 0, 0), (next0, 1, 0), (next2, 1, 2), (next3, 1, 3)]
+    lefts += [(last0, 3, 0), (last1, 3, 1), (last2, 3, 2)]
+    lefts += [(far0, 2, 0), (far1, 2, 1), (far2, 2, 2), (far3, 2, 3)]
+    back, amps, rows, *far = pair_terms(place, plan, left_levels, right_levels, pieces, lefts, fits)
+    far = [shift(far[0], 1), shift(far[1], fits - 1)]
     returned = to_orb(back)
-    far0, far1 = shift(far0, 1), shift(far1, fits - 1)
-    rise, fall = merge((next0, last1), (far0, far1), (next1, last0))
+    own, rise, fall = near_terms(place, amps, rows, fits)
+    rise, fall = merge(rise, fall, far)
     below, above = shift(rise, 1), shift(fall, fits - 1)
     total = to_all(sum_returned(place, wanted, returned, orbs, fits, after=[rise]))
     return tuple(add_all(place, own, below, above, total, fits))

time: 325 us -> 303 us (0.932)
  blocking collectives: 47.6 us -> 0 us
  starting transfers between devices: 30.8 us -> 58.2 us
  waiting for transfers between devices: 159 us -> 152 us
  Pallas kernels: 68.1 us -> 72.1 us
    all_to_all x1 -> x0, blocking collectives: 47.6 us -> none  [to_all(): lax.all_to_all(x, ('orb', 'fit'), split_axis=0, concat_axis=0, tiled=True)]
    ppermute x10 -> x14, waiting for transfers between devices: 147 us -> 118 us  [shift(): return lax.ppermute(x, 'fit', [(n, (n + k) % fits) for n in range(fits)])]
    ppermute x0 -> x7, waiting for transfers between devices: none -> 19.5 us  [on_device(): lax.ppermute(wanted, 'orb', [(n, n + ((n // stride + k) % count - n // st...]
    all_to_all x1 -> x2, starting transfers between devices: 6.96 us -> 18.9 us  [to_all(): lax.all_to_all(x, ('orb', 'fit'), split_axis=0, concat_axis=0, tiled=True)]
    ppermute x0 -> x7, starting transfers between devices: none -> 7.93 us  [on_device(): lax.ppermute(wanted, 'orb', [(n, n + ((n // stride + k) % count - n // st...]
    ppermute x10 -> x14, starting transfers between devices: 9.13 us -> 14 us  [shift(): return lax.ppermute(x, 'fit', [(n, (n + k) % fits) for n in range(fits)])]
    pallas_call x6 -> x7, Pallas kernels: 68.1 us -> 72.1 us  [call(): pl.pallas_call(kernel, grid=(grid,), in_specs=in_specs, out_specs=out_spe...]
  transfers between devices with their start and end apart: 13 -> 25, of which waited for: 8 -> 16; matrix products, arithmetic and copies ran while one was open for 3% -> 4% of each run, Pallas kernels for 4% -> 8%
where the time goes in v3:
time: 303 us; the launch traced here: 302 us
  waiting for transfers between devices  152 us (50%)
  Pallas kernels  72.1 us (24%)
  starting transfers between devices  58.2 us (19%)
  local copies, waits for them, and re-layouts  16.3 us (5%)
    ppermute x14, waiting for transfers between devices, shift(): return lax.ppermute(x, 'fit', [(n, (n + k) % fits) for n in range(fits)])  118 us
    pallas_call x7, Pallas kernels, call(): pl.pallas_call(kernel, grid=(grid,), in_specs=in_specs, out_specs=out_spe...  72.1 us
    ppermute x7, waiting for transfers between devices, on_device(): lax.ppermute(wanted, 'orb', [(n, n + ((n // stride + k) % count - n // st...  19.5 us
    all_to_all x2, starting transfers between devices, to_all(): lax.all_to_all(x, ('orb', 'fit'), split_axis=0, concat_axis=0, tiled=True)  18.9 us
    all_to_all x2, starting transfers between devices, to_orb(): return lax.all_to_all(x, 'orb', split_axis=0, concat_axis=0, tiled=True)  17.3 us
    ppermute x14, starting transfers between devices, shift(): return lax.ppermute(x, 'fit', [(n, (n + k) % fits) for n in range(fits)])  14 us
    all_to_all x2, waiting for transfers between devices, to_orb(): return lax.all_to_all(x, 'orb', split_axis=0, concat_axis=0, tiled=True)  11.6 us
    ppermute x7, starting transfers between devices, on_device(): lax.ppermute(wanted, 'orb', [(n, n + ((n // stride + k) % count - n // st...  7.93 us
  transfers between devices with their start and end apart: 25, of which 16 were waited for; matrix products, arithmetic and copies ran while one was open for 4% of the time, Pallas kernels for 8%

profile of v3, /device:TPU:1, one launch (start us, length us, event | category | flops | bytes accessed | tf_op | source)
XLA Modules:
  0.0 302.5 jit_solution(10927580848456125287)
XLA Ops:
  0.7 0.7 concatenate.14.place_ref
  1.4 4.1 %pack_blocks.1 = bf16[128,4,16,128]{3,2,1,0:T(8,128)(2,1)} custom-call(s32[14]{0:T(128)} %concatenate.14.place_ref, bf16[4,512,512]{2,1,0:T(8,128)(2,1)} %refs_0_.1), custom_call_target="tpu_custom_call" | custom-call | bytes 1024 | tf_op jit(solution)/shard_map/pack_blocks/pallas_call | solution.py:32
  5.5 12.0 %all-to-all-start = ((bf16[128,4,16,128]{3,2,1,0:T(8,128)(2,1)}), bf16[128,4,16,128]{3,2,1,0:T(8,128)(2,1)}, u32[]{:S(2)}, u32[]{:S(2)}) async-start(bf16[128,4,16,128]{3,2,1,0:T(8,128)(2,1)} %pack_blocks.1), calls=%async_computation | async-start | bytes 4194304 | tf_op jit(solution)/shard_map/all_to_all | solution.py:397
  17.4 1.4 fusion.8
  18.8 3.3 %collective-permute-start.8 = (bf16[1,512,512]{2,1,0:T(8,128)(2,1)}, bf16[1,512,512]{2,1,0:T(8,128)(2,1)S(1)}, u32[]{:S(2)}, u32[]{:S(2)}) collective-permute-start(bf16[1,512,512]{2,1,0:T(8,128)(2,1)} %get-tuple-element.34), channel_id=1, source_target_pairs={{0,3},{1,0},{2,1},{3,2},{4,7},{5,4},{6,5},{7,6},{8,11},{9,8},{10,9... | collective-permute-start | bytes 1572872 | tf_op jit(solution)/shard_map/ppermute | solution.py:391
  22.2 0.7 collective-permute-start
  22.9 0.8 collective-permute-done
  23.7 2.4 collective-permute-start.3
  26.2 0.5 collective-permute-start.2
  26.7 0.6 collective-permute-start.1
  27.3 13.8 %collective-permute-done.3 = s32[2,128]{1,0:T(2,128)S(1)} collective-permute-done((s32[2,128]{1,0:T(2,128)S(1)}, s32[2,128]{1,0:T(2,128)S(1)}, u32[]{:S(2)}, u32[]{:S(2)}) %collective-permute-start.3) | collective-permute-done | bytes 1056 | tf_op jit(solution)/shard_map/ppermute | solution.py:410
  41.0 1.5 collective-permute-done.2
  42.6 2.5 collective-permute-start.6
  45.1 0.5 collective-permute-start.5
  45.6 0.6 collective-permute-start.4
  46.2 2.9 collective-permute-done.5
  49.1 0.5 collective-permute-done.4
  49.6 2.4 concatenate.17
  52.0 1.1 collective-permute-done.8.refs_1_.refs_3_
  53.1 2.0 collective-permute-done.7.refs_0_.refs_4_
  55.1 0.8 copy-done.7
  55.9 5.8 %pick_pieces.1 = bf16[32,32,16,128]{3,2,1,0:T(8,128)(2,1)} custom-call(s32[14]{0:T(128)} %concatenate.14.place_ref, s32[32,8]{1,0:T(8,128)} %bitcast.24, bf16[128,4,16,128]{3,2,1,0:T(8,128)(2,1)} %all-to-all-done.held_ref, bf16[1,512,512]{2,1,0:T(8,128)(2,1)} %copy-done.7, bf16[1,512,512]{2,1,0:T(8,128)(2,1)} %copy-done.5), custom_call_target="tpu_custom_call" | custom-call | bytes 1024 | tf_op jit(solution)/shard_map/pick_pieces/pallas_call | solution.py:32
  61.7 7.0 %all-to-all-start.1 = ((bf16[32,32,16,128]{3,2,1,0:T(8,128)(2,1)}), bf16[32,32,16,128]{3,2,1,0:T(8,128)(2,1)}, u32[]{:S(2)}, u32[]{:S(2)}) async-start(bf16[32,32,16,128]{3,2,1,0:T(8,128)(2,1)} %pick_pieces.1), calls=%async_computation.1 | async-start | bytes 8388608 | tf_op jit(solution)/shard_map/all_to_all | solution.py:394
  69.0 1.2 collective-permute-start.9
  70.3 0.6 gather_fusion.5
  71.0 0.6 gather_fusion.1
  71.6 0.6 gather_fusion.3
  72.3 0.6 gather_fusion.4
  72.8 0.6 broadcast_select_fusion.1.nright_ref
  73.4 0.5 fusion.7
  74.0 1.5 fusion.9
  75.5 1.4 collective-permute-start.16
  77.0 5.3 %collective-permute-done.10.refs_2_ = bf16[1,512,512]{2,1,0:T(8,128)(2,1)} collective-permute-done((bf16[1,512,512]{2,1,0:T(8,128)(2,1)}, bf16[1,512,512]{2,1,0:T(8,128)(2,1)}, u32[]{:S(2)}, u32[]{:S(2)}) %collective-permute-start.10) | collective-permute-done | bytes 524320 | tf_op jit(solution)/shard_map/ppermute | solution.py:391
  82.3 1.1 collective-permute-done.9.refs_5_
  83.7 1.1 collective-permute-start.12
  85.0 1.6 collective-permute-start.15
  86.6 7.0 %collective-permute-done.16.refs_10_ = bf16[1,512,512]{2,1,0:T(8,128)(2,1)S(1)} collective-permute-done((bf16[1,512,512]{2,1,0:T(8,128)(2,1)S(1)}, bf16[1,512,512]{2,1,0:T(8,128)(2,1)S(1)}, u32[]{:S(2)}, u32[]{:S(2)}) %collective-permute-start.16) | collective-permute-done | bytes 524320 | tf_op jit(solution)/shard_map/ppermute | solution.py:391
  93.7 0.7 copy-done.12
  94.3 0.6 gather_fusion.2
  94.9 0.7 gather_fusion
  95.6 0.7 reshape.110.high_ref
  96.2 0.4 copy.10
  96.6 0.6 bitcast_select_fusion.nleft_ref
  97.2 1.1 select_subtract_fusion.low_ref
  98.3 31.8 %collective-permute-done.13.refs_7_ = bf16[1,512,512]{2,1,0:T(8,128)(2,1)S(1)} collective-permute-done((bf16[1,512,512]{2,1,0:T(8,128)(2,1)S(1)}, bf16[1,512,512]{2,1,0:T(8,128)(2,1)S(1)}, u32[]{:S(2)}, u32[]{:S(2)}) %collective-permute-start.13) | collective-permute-done | bytes 524320 | tf_op jit(solution)/shard_map/ppermute | solution.py:391
  130.2 0.8 copy-done.13
  130.9 0.4 copy-done.11
  131.3 30.1 %pair_terms.1 = (bf16[32,32,16,128]{3,2,1,0:T(8,128)(2,1)}, bf16[4,512,1024]{2,1,0:T(8,128)(2,1)}, bf16[8,128,2048]{2,1,0:T(8,128)(2,1)}, bf16[2,512,640]{2,1,0:T(8,128)(2,1)}, bf16[2,512,640]{2,1,0:T(8,128)(2,1)}) custom-call(s32[14]{0:T(128)} %concatenate.14.place_ref, s32[16]{0:T(128)} %get-tuple-element.39.left_ref, s32[16]{0:T(128)} %bitcast_select_fusion.nleft_ref, ...), custom_call_target="tpu_custom_call" | custom-call | bytes 1024 | tf_op jit(solution)/shard_map/pair_terms/pallas_call | solution.py:32
  161.4 10.3 %all-to-all-start.2 = ((bf16[32,32,16,128]{3,2,1,0:T(8,128)(2,1)}), bf16[32,32,16,128]{3,2,1,0:T(8,128)(2,1)}, u32[]{:S(2)}, u32[]{:S(2)}) async-start(bf16[32,32,16,128]{3,2,1,0:T(8,128)(2,1)} %get-tuple-element.29), calls=%async_computation.2 | async-start | bytes 8388608 | tf_op jit(solution)/shard_map/all_to_all | solution.py:394
  171.8 2.7 collective-permute-start.18
  174.4 14.2 %near_terms.1 = (bf16[4,512,640]{2,1,0:T(8,128)(2,1)}, bf16[4,512,640]{2,1,0:T(8,128)(2,1)}, bf16[4,512,640]{2,1,0:T(8,128)(2,1)}) custom-call(s32[14]{0:T(128)} %concatenate.14.place_ref, bf16[4,512,1024]{2,1,0:T(8,128)(2,1)} %get-tuple-element.20.all_ref, bf16[8,128,2048]{2,1,0:T(8,128)(2,1)} %get-tuple-element.21.rows_ref), custom_call_target="tpu_custom_call" | custom-call | bytes 1024 | tf_op jit(solution)/shard_map/near_terms/pallas_call | solution.py:32
  188.6 14.5 %collective-permute-done.17.c_ref = bf16[2,512,640]{2,1,0:T(8,128)(2,1)S(1)} collective-permute-done((bf16[2,512,640]{2,1,0:T(8,128)(2,1)S(1)}, bf16[2,512,640]{2,1,0:T(8,128)(2,1)S(1)}, u32[]{:S(2)}, u32[]{:S(2)}) %collective-permute-start.17) | collective-permute-done | bytes 1310752 | tf_op jit(solution)/shard_map/ppermute | solution.py:391
  203.1 1.1 copy-done.9
  204.2 0.5 copy-done.10
  204.7 3.7 %merge.1 = (bf16[4,512,640]{2,1,0:T(8,128)(2,1)}, bf16[4,512,640]{2,1,0:T(8,128)(2,1)}) custom-call(bf16[4,512,640]{2,1,0:T(8,128)(2,1)} %get-tuple-element.23.a_ref, bf16[4,512,640]{2,1,0:T(8,128)(2,1)} %get-tuple-element.24.b_ref, bf16[2,512,640]{2,1,0:T(8,128)(2,1)} %copy-done.9, ...), custom_call_target="tpu_custom_call", output_to_operand_aliasing={{0}: (0, {}), {1}: (1, {})} | custom-call | bytes 1024 | tf_op jit(solution)/shard_map/merge/pallas_call | solution.py:32
  208.4 1.9 collective-permute-start.20
  210.3 11.6 %all-to-all-done.2.part_ref = bf16[32,32,16,128]{3,2,1,0:T(8,128)(2,1)} async-done(((bf16[32,32,16,128]{3,2,1,0:T(8,128)(2,1)}), bf16[32,32,16,128]{3,2,1,0:T(8,128)(2,1)}, u32[]{:S(2)}, u32[]{:S(2)}) %all-to-all-start.2) | async-done | bytes 4194336 | tf_op jit(solution)/shard_map/all_to_all | solution.py:394
  221.9 6.0 %sum_returned.1 = bf16[128,4,16,128]{3,2,1,0:T(8,128)(2,1)} custom-call(s32[14]{0:T(128)} %concatenate.14.place_ref, s32[32,8]{1,0:T(8,128)} %bitcast.25, bf16[32,32,16,128]{3,2,1,0:T(8,128)(2,1)} %all-to-all-done.2.part_ref, bf16[4,512,640]{2,1,0:T(8,128)(2,1)} %get-tuple-element.27.refs_0_), custom_call_target="tpu_custom_call" | custom-call | bytes 1024 | tf_op jit(solution)/shard_map/sum_returned/pallas_call | solution.py:32
  228.0 7.0 %all-to-all-start.3 = ((bf16[128,4,16,128]{3,2,1,0:T(8,128)(2,1)}), bf16[128,4,16,128]{3,2,1,0:T(8,128)(2,1)S(1)}, u32[]{:S(2)}, u32[]{:S(2)}) async-start(bf16[128,4,16,128]{3,2,1,0:T(8,128)(2,1)} %sum_returned.1), calls=%async_computation.3 | async-start | bytes 4194304 | tf_op jit(solution)/shard_map/all_to_all | solution.py:397
  234.9 52.2 %collective-permute-done.20.above_ref = bf16[4,512,640]{2,1,0:T(8,128)(2,1)} collective-permute-done((bf16[4,512,640]{2,1,0:T(8,128)(2,1)}, bf16[4,512,640]{2,1,0:T(8,128)(2,1)}, u32[]{:S(2)}, u32[]{:S(2)}) %collective-permute-start.20) | collective-permute-done | bytes 2621472 | tf_op jit(solution)/shard_map/ppermute | solution.py:391
  287.1 2.9 collective-permute-done.19.below_ref
  290.0 2.9 all-to-all-done.3.sums_ref
  292.9 1.3 copy-done.4
  294.2 8.1 %add_all.1 = (f32[4,512,512]{2,1,0:T(8,128)}, f32[4,512,128]{2,1,0:T(8,128)}) custom-call(s32[14]{0:T(128)} %concatenate.14.place_ref, bf16[4,512,640]{2,1,0:T(8,128)(2,1)} %get-tuple-element.22.own_ref, bf16[4,512,640]{2,1,0:T(8,128)(2,1)} %collective-permute-done.19.below_ref, bf16[4,512,640]{2,1,0:T(8,128)(2,1)} %collective-permute-done.20.above_ref, ...), custom_call_target="tpu_custom_call" | custom-call | bytes 1024 | tf_op jit(solution)/shard_map/add_all/pallas_call | solution.py:32
  (62 shorter events, 1.3 us)
Async XLA Ops:
  0.6 71.6 %copy-start = (f32[128,512]{1,0:T(8,128)S(1)}, f32[128,512]{1,0:T(8,128)}, u32[]{:S(2)}) copy-start(f32[128,512]{1,0:T(8,128)} %param.7) | copy-start | bytes 786436
  5.5 12.0 %copy-start.3 = (bf16[4,512,512]{2,1,0:T(8,128)(2,1)S(1)}, bf16[4,512,512]{2,1,0:T(8,128)(2,1)}, u32[]{:S(2)}) copy-start(bf16[4,512,512]{2,1,0:T(8,128)(2,1)} %refs_0_.1) | copy-start | bytes 6291460
  5.5 49.6 %all-to-all-start = ((bf16[128,4,16,128]{3,2,1,0:T(8,128)(2,1)}), bf16[128,4,16,128]{3,2,1,0:T(8,128)(2,1)}, u32[]{:S(2)}, u32[]{:S(2)}) async-start(bf16[128,4,16,128]{3,2,1,0:T(8,128)(2,1)} %pack_blocks.1), calls=%async_computation | async-start | bytes 4194304 | tf_op jit(solution)/shard_map/all_to_all | solution.py:397
  17.4 4.6 %copy-start.14 = (s32[16,2]{0,1:T(2,128)S(1)}, s32[16,2]{0,1:T(2,128)}, u32[]{:S(2)}) copy-start(s32[16,2]{0,1:T(2,128)} %param.9) | copy-start | bytes 388
  18.8 34.2 %collective-permute-start.8 = (bf16[1,512,512]{2,1,0:T(8,128)(2,1)}, bf16[1,512,512]{2,1,0:T(8,128)(2,1)S(1)}, u32[]{:S(2)}, u32[]{:S(2)}) collective-permute-start(bf16[1,512,512]{2,1,0:T(8,128)(2,1)} %get-tuple-element.34), channel_id=1, source_target_pairs={{0,3},{1,0},{2,1},{3,2},{4,7},{5,4},{6,5},{7,6},{8,11},{9,8},{10,9... | collective-permute-start | bytes 1572872 | tf_op jit(solution)/shard_map/ppermute | solution.py:391
  22.1 33.0 %collective-permute-start.7 = (bf16[1,512,512]{2,1,0:T(8,128)(2,1)}, bf16[1,512,512]{2,1,0:T(8,128)(2,1)S(1)}, u32[]{:S(2)}, u32[]{:S(2)}) collective-permute-start(bf16[1,512,512]{2,1,0:T(8,128)(2,1)} %get-tuple-element.35), channel_id=1, source_target_pairs={{0,1},{1,2},{2,3},{3,0},{4,5},{5,6},{6,7},{7,4},{8,9},{9,10},{10,1... | collective-permute-start | bytes 1572872 | tf_op jit(solution)/shard_map/ppermute | solution.py:391
  22.2 1.5 collective-permute-start
  23.7 17.3 %collective-permute-start.3 = (s32[2,128]{1,0:T(2,128)S(1)}, s32[2,128]{1,0:T(2,128)S(1)}, u32[]{:S(2)}, u32[]{:S(2)}) collective-permute-start(s32[2,128]{1,0:T(2,128)S(1)} %pad_add_fusion), channel_id=1, source_target_pairs={{0,24},{4,28},{8,0},{12,4},{16,8},{20,12},{24,16},{28,20},{32,56},... | collective-permute-start | bytes 3080 | tf_op jit(solution)/shard_map/ppermute | solution.py:410
  26.2 16.4 %collective-permute-start.2 = (s32[2,128]{1,0:T(2,128)S(1)}, s32[2,128]{1,0:T(2,128)S(1)}, u32[]{:S(2)}, u32[]{:S(2)}) collective-permute-start(s32[2,128]{1,0:T(2,128)S(1)} %pad_add_fusion), channel_id=1, source_target_pairs={{0,16},{4,20},{8,24},{12,28},{16,0},{20,4},{24,8},{28,12},{32,48},... | collective-permute-start | bytes 3080 | tf_op jit(solution)/shard_map/ppermute | solution.py:410
  26.7 15.9 %collective-permute-start.1 = (s32[2,128]{1,0:T(2,128)S(1)}, s32[2,128]{1,0:T(2,128)S(1)}, u32[]{:S(2)}, u32[]{:S(2)}) collective-permute-start(s32[2,128]{1,0:T(2,128)S(1)} %pad_add_fusion), channel_id=1, source_target_pairs={{0,8},{4,12},{8,16},{12,20},{16,24},{20,28},{24,0},{28,4},{32,40},... | collective-permute-start | bytes 3080 | tf_op jit(solution)/shard_map/ppermute | solution.py:410
  42.6 3.6 %collective-permute-start.6 = (s32[8,128]{1,0:T(8,128)S(1)}, s32[8,128]{1,0:T(8,128)S(1)}, u32[]{:S(2)}, u32[]{:S(2)}) collective-permute-start(s32[8,128]{1,0:T(8,128)S(1)} %concatenate.16), channel_id=1, source_target_pairs={{0,96},{4,100},{8,104},{12,108},{16,112},{20,116},{24,120},{28,124... | collective-permute-start | bytes 12296 | tf_op jit(solution)/shard_map/ppermute | solution.py:410
  45.1 4.0 %collective-permute-start.5 = (s32[8,128]{1,0:T(8,128)S(1)}, s32[8,128]{1,0:T(8,128)S(1)}, u32[]{:S(2)}, u32[]{:S(2)}) collective-permute-start(s32[8,128]{1,0:T(8,128)S(1)} %concatenate.16), channel_id=1, source_target_pairs={{0,64},{4,68},{8,72},{12,76},{16,80},{20,84},{24,88},{28,92},{32,9... | collective-permute-start | bytes 12296 | tf_op jit(solution)/shard_map/ppermute | solution.py:410
  45.6 4.0 %collective-permute-start.4 = (s32[8,128]{1,0:T(8,128)S(1)}, s32[8,128]{1,0:T(8,128)S(1)}, u32[]{:S(2)}, u32[]{:S(2)}) collective-permute-start(s32[8,128]{1,0:T(8,128)S(1)} %concatenate.16), channel_id=1, source_target_pairs={{0,32},{4,36},{8,40},{12,44},{16,48},{20,52},{24,56},{28,60},{32,6... | collective-permute-start | bytes 12296 | tf_op jit(solution)/shard_map/ppermute | solution.py:410
  53.1 2.0 copy-start.5
  55.1 0.8 copy-start.7
  61.7 8.6 %copy-start.2 = (f32[128]{0:T(128)S(1)}, f32[128]{0:T(128)}, u32[]{:S(2)}) copy-start(f32[128]{0:T(128)} %param.6) | copy-start | bytes 1540
  61.7 9.2 %copy-start.17 = (s32[128]{0:T(128)S(1)}, s32[128]{0:T(128)}, u32[]{:S(2)}) copy-start(s32[128]{0:T(128)} %param.8) | copy-start | bytes 1540
  61.7 68.5 %all-to-all-start.1 = ((bf16[32,32,16,128]{3,2,1,0:T(8,128)(2,1)}), bf16[32,32,16,128]{3,2,1,0:T(8,128)(2,1)}, u32[]{:S(2)}, u32[]{:S(2)}) async-start(bf16[32,32,16,128]{3,2,1,0:T(8,128)(2,1)} %pick_pieces.1), calls=%async_computation.1 | async-start | bytes 8388608 | tf_op jit(solution)/shard_map/all_to_all | solution.py:394
  68.7 13.6 %collective-permute-start.10 = (bf16[1,512,512]{2,1,0:T(8,128)(2,1)}, bf16[1,512,512]{2,1,0:T(8,128)(2,1)}, u32[]{:S(2)}, u32[]{:S(2)}) collective-permute-start(bf16[1,512,512]{2,1,0:T(8,128)(2,1)} %get-tuple-element.32), channel_id=1, source_target_pairs={{0,3},{1,0},{2,1},{3,2},{4,7},{5,4},{6,5},{7,6},{8,11},{9,8},{10,9... | collective-permute-start | bytes 1572872 | tf_op jit(solution)/shard_map/ppermute | solution.py:391
  69.0 14.4 %collective-permute-start.9 = (bf16[1,512,512]{2,1,0:T(8,128)(2,1)}, bf16[1,512,512]{2,1,0:T(8,128)(2,1)}, u32[]{:S(2)}, u32[]{:S(2)}) collective-permute-start(bf16[1,512,512]{2,1,0:T(8,128)(2,1)} %get-tuple-element.33), channel_id=1, source_target_pairs={{0,1},{1,2},{2,3},{3,0},{4,5},{5,6},{6,7},{7,4},{8,9},{9,10},{10,1... | collective-permute-start | bytes 1572872 | tf_op jit(solution)/shard_map/ppermute | solution.py:391
  70.9 4.6 %copy-start.6 = (bf16[1,512,512]{2,1,0:T(8,128)(2,1)S(1)}, bf16[1,512,512]{2,1,0:T(8,128)(2,1)}, u32[]{:S(2)}) copy-start(bf16[1,512,512]{2,1,0:T(8,128)(2,1)} %copy-done.5) | copy-start | bytes 1572868
  70.9 22.6 %copy-start.8 = (bf16[1,512,512]{2,1,0:T(8,128)(2,1)S(1)}, bf16[1,512,512]{2,1,0:T(8,128)(2,1)}, u32[]{:S(2)}) copy-start(bf16[1,512,512]{2,1,0:T(8,128)(2,1)} %copy-done.7) | copy-start | bytes 1572868
  75.5 18.0 %collective-permute-start.16 = (bf16[1,512,512]{2,1,0:T(8,128)(2,1)S(1)}, bf16[1,512,512]{2,1,0:T(8,128)(2,1)S(1)}, u32[]{:S(2)}, u32[]{:S(2)}) collective-permute-start(bf16[1,512,512]{2,1,0:T(8,128)(2,1)S(1)} %copy-done.6), channel_id=1, source_target_pairs={{0,3},{1,0},{2,1},{3,2},{4,7},{5,4},{6,5},{7,6},{8,11},{9,8},{10,9... | collective-permute-start | bytes 1572872 | tf_op jit(solution)/shard_map/ppermute | solution.py:391
  83.4 46.7 %collective-permute-start.11 = (bf16[2,512,512]{2,1,0:T(8,128)(2,1)}, bf16[2,512,512]{2,1,0:T(8,128)(2,1)S(1)}, u32[]{:S(2)}, u32[]{:S(2)}) collective-permute-start(bf16[2,512,512]{2,1,0:T(8,128)(2,1)} %get-tuple-element.16), channel_id=1, source_target_pairs={{0,3},{1,0},{2,1},{3,2},{4,7},{5,4},{6,5},{7,6},{8,11},{9,8},{10,9... | collective-permute-start | bytes 3145736 | tf_op jit(solution)/shard_map/ppermute | solution.py:391
  83.7 46.4 %collective-permute-start.12 = (bf16[2,512,512]{2,1,0:T(8,128)(2,1)}, bf16[2,512,512]{2,1,0:T(8,128)(2,1)}, u32[]{:S(2)}, u32[]{:S(2)}) collective-permute-start(bf16[2,512,512]{2,1,0:T(8,128)(2,1)} %get-tuple-element.19), channel_id=1, source_target_pairs={{0,1},{1,2},{2,3},{3,0},{4,5},{5,6},{6,7},{7,4},{8,9},{9,10},{10,1... | collective-permute-start | bytes 3145736 | tf_op jit(solution)/shard_map/ppermute | solution.py:391
  85.0 45.2 %collective-permute-start.15 = (bf16[1,512,512]{2,1,0:T(8,128)(2,1)}, bf16[1,512,512]{2,1,0:T(8,128)(2,1)}, u32[]{:S(2)}, u32[]{:S(2)}) collective-permute-start(bf16[1,512,512]{2,1,0:T(8,128)(2,1)} %collective-permute-done.10.refs_2_), channel_id=1, source_target_pairs={{0,3},{1,0},{2,1},{3,2},{4,7},{5,4},{6,5},{7,6},{8,11},{9,8},{10,9... | collective-permute-start | bytes 1572872 | tf_op jit(solution)/shard_map/ppermute | solution.py:391
  86.6 43.6 %collective-permute-start.14 = (bf16[1,512,512]{2,1,0:T(8,128)(2,1)}, bf16[1,512,512]{2,1,0:T(8,128)(2,1)}, u32[]{:S(2)}, u32[]{:S(2)}) collective-permute-start(bf16[1,512,512]{2,1,0:T(8,128)(2,1)} %collective-permute-done.9.refs_5_), channel_id=1, source_target_pairs={{0,1},{1,2},{2,3},{3,0},{4,5},{5,6},{6,7},{7,4},{8,9},{9,10},{10,1... | collective-permute-start | bytes 1572872 | tf_op jit(solution)/shard_map/ppermute | solution.py:391
  93.5 0.8 copy-start.12
  93.5 36.6 %collective-permute-start.13 = (bf16[1,512,512]{2,1,0:T(8,128)(2,1)S(1)}, bf16[1,512,512]{2,1,0:T(8,128)(2,1)S(1)}, u32[]{:S(2)}, u32[]{:S(2)}) collective-permute-start(bf16[1,512,512]{2,1,0:T(8,128)(2,1)S(1)} %copy-done.8), channel_id=1, source_target_pairs={{0,1},{1,2},{2,3},{3,0},{4,5},{5,6},{6,7},{7,4},{8,9},{9,10},{10,1... | collective-permute-start | bytes 1572872 | tf_op jit(solution)/shard_map/ppermute | solution.py:391
  130.1 0.8 copy-start.13
  130.2 1.1 copy-start.11
  161.4 10.3 %copy-start.16 = (bf16[2,512,640]{2,1,0:T(8,128)(2,1)S(1)}, bf16[2,512,640]{2,1,0:T(8,128)(2,1)}, u32[]{:S(2)}) copy-start(bf16[2,512,640]{2,1,0:T(8,128)(2,1)} %get-tuple-element.25) | copy-start | bytes 3932164
  161.4 10.4 %copy-start.15 = (bf16[2,512,640]{2,1,0:T(8,128)(2,1)S(1)}, bf16[2,512,640]{2,1,0:T(8,128)(2,1)}, u32[]{:S(2)}) copy-start(bf16[2,512,640]{2,1,0:T(8,128)(2,1)} %get-tuple-element.26) | copy-start | bytes 3932164
  161.4 60.5 %all-to-all-start.2 = ((bf16[32,32,16,128]{3,2,1,0:T(8,128)(2,1)}), bf16[32,32,16,128]{3,2,1,0:T(8,128)(2,1)}, u32[]{:S(2)}, u32[]{:S(2)}) async-start(bf16[32,32,16,128]{3,2,1,0:T(8,128)(2,1)} %get-tuple-element.29), calls=%async_computation.2 | async-start | bytes 8388608 | tf_op jit(solution)/shard_map/all_to_all | solution.py:394
  171.7 31.4 %collective-permute-start.17 = (bf16[2,512,640]{2,1,0:T(8,128)(2,1)S(1)}, bf16[2,512,640]{2,1,0:T(8,128)(2,1)S(1)}, u32[]{:S(2)}, u32[]{:S(2)}) collective-permute-start(bf16[2,512,640]{2,1,0:T(8,128)(2,1)S(1)} %copy-done.16), channel_id=1, source_target_pairs={{0,1},{1,2},{2,3},{3,0},{4,5},{5,6},{6,7},{7,4},{8,9},{9,10},{10,1... | collective-permute-start | bytes 3932168 | tf_op jit(solution)/shard_map/ppermute | solution.py:391
  171.8 31.4 %collective-permute-start.18 = (bf16[2,512,640]{2,1,0:T(8,128)(2,1)S(1)}, bf16[2,512,640]{2,1,0:T(8,128)(2,1)S(1)}, u32[]{:S(2)}, u32[]{:S(2)}) collective-permute-start(bf16[2,512,640]{2,1,0:T(8,128)(2,1)S(1)} %copy-done.15), channel_id=1, source_target_pairs={{0,3},{1,0},{2,1},{3,2},{4,7},{5,4},{6,5},{7,6},{8,11},{9,8},{10,9... | collective-permute-start | bytes 3932168 | tf_op jit(solution)/shard_map/ppermute | solution.py:391
  203.1 1.1 copy-start.9
  203.1 1.5 copy-start.10
  208.4 78.7 %collective-permute-start.20 = (bf16[4,512,640]{2,1,0:T(8,128)(2,1)}, bf16[4,512,640]{2,1,0:T(8,128)(2,1)}, u32[]{:S(2)}, u32[]{:S(2)}) collective-permute-start(bf16[4,512,640]{2,1,0:T(8,128)(2,1)} %get-tuple-element.28), channel_id=1, source_target_pairs={{0,3},{1,0},{2,1},{3,2},{4,7},{5,4},{6,5},{7,6},{8,11},{9,8},{10,9... | collective-permute-start | bytes 7864328 | tf_op jit(solution)/shard_map/ppermute | solution.py:391
  210.3 79.7 %collective-permute-start.19 = (bf16[4,512,640]{2,1,0:T(8,128)(2,1)}, bf16[4,512,640]{2,1,0:T(8,128)(2,1)}, u32[]{:S(2)}, u32[]{:S(2)}) collective-permute-start(bf16[4,512,640]{2,1,0:T(8,128)(2,1)} %get-tuple-element.27.refs_0_), channel_id=1, source_target_pairs={{0,1},{1,2},{2,3},{3,0},{4,5},{5,6},{6,7},{7,4},{8,9},{9,10},{10,1... | collective-permute-start | bytes 7864328 | tf_op jit(solution)/shard_map/ppermute | solution.py:391
  228.0 64.9 %all-to-all-start.3 = ((bf16[128,4,16,128]{3,2,1,0:T(8,128)(2,1)}), bf16[128,4,16,128]{3,2,1,0:T(8,128)(2,1)S(1)}, u32[]{:S(2)}, u32[]{:S(2)}) async-start(bf16[128,4,16,128]{3,2,1,0:T(8,128)(2,1)} %sum_returned.1), calls=%async_computation.3 | async-start | bytes 4194304 | tf_op jit(solution)/shard_map/all_to_all | solution.py:397
  292.9 1.3 copy-start.4
  292.9 9.4 %copy-start.1 = (f32[128,512]{1,0:T(8,128)S(1)}, f32[128,512]{1,0:T(8,128)}, u32[]{:S(2)}) copy-start(f32[128,512]{1,0:T(8,128)} %param.7) | copy-start | bytes 786436

commit v4 on v3

--- a/solution.py
+++ b/solution.py
@@ -84,21 +84,21 @@
 def pick_pieces(place, wanted, held, fits, after):
     peers, count = wanted.shape
     orbs = held.shape[1]
+    held = held.reshape(-1, SUB, 128)
     block = peers // 4
 
     def kernel(place_ref, wanted_ref, held_ref, *refs):
         out_ref = refs[-1]
-        parts = [place_ref[NEXT + s] for s in range(fits)]
+        parts = [place_ref[NEXT + s] * orbs for s in range(fits)]
         first = pl.program_id(0) * block
 
         @pl.loop(0, block)
         def _(d):
             row = list_row(place_ref[ORB], first + d)
             for g in range(count):
-                j = wanted_ref[row, g]
-                source, k = lax.div(j, orbs) * fits, lax.rem(j, orbs)
+                spot = wanted_ref[row, g]
                 for s in range(fits):
-                    out_ref[d, g * fits + s] = held_ref[source + parts[s], k]
+                    out_ref[d, g * fits + s] = held_ref[spot + parts[s]]
 
     return call(
         kernel,
@@ -119,6 +119,7 @@
     taken = tiles * rows
     wide = virt // fits
     half = orbs // 2
+    steps = count // 2
     names = ("left", "nleft", "nright")
 
     def kernel(place_ref, left_ref, nleft_ref, nright_ref, low_ref, high_ref, pieces_ref, *refs):
@@ -137,22 +138,22 @@
                 copy.start()
             all_ref[...] = jnp.zeros_like(all_ref)
 
-        @pl.when(n < count)
-        def _():
-            g = n
+        def group(g, e):
             for m in range(peers):
                 h, turned, c = device_of(m, fits, cols)
                 for s in range(fits):
                     at = pl.multiple_of(place_ref[BACK + (turned - s) % fits] * rows + h * SUB, SUB)
-                    rows_ref[g, pl.ds(at, SUB), s * aux + c * 128 : s * aux + (c + 1) * 128] = pieces_ref[m, s]
-
-            @pl.when(n == 0)
-            def _():
-                for copy in copies:
-                    copy.wait()
-
-            rows_out_ref[0] = rows_ref[g]
-            turned_ref[...] = rows_ref[g].T
+                    rows_out_ref[e, pl.ds(at, SUB), s * aux + c * 128 : s * aux + (c + 1) * 128] = pieces_ref[m, e * fits + s]
+
+            if e == 0:
+
+                @pl.when(n == 0)
+                def _():
+                    for copy in copies:
+                        copy.wait()
+
+            rows_ref[g] = rows_out_ref[e]
+            turned_ref[e] = rows_out_ref[e].T
             row_id = lax.broadcasted_iota(jnp.int32, (WIDE, taken), 0)
             col_id = lax.broadcasted_iota(jnp.int32, (WIDE, taken), 1)
             for u in range(2):
@@ -165,7 +166,7 @@
                         total += (
                             jnp.dot(
                                 lefts_ref[s, k, at, :],
-                                turned_ref[s * aux : (s + 1) * aux, :],
+                                turned_ref[e, s * aux : (s + 1) * aux, :],
                                 preferred_element_type=F32,
                             )
                             .astype(BF16)
@@ -174,52 +175,57 @@
                     keep = (row_id < nleft_ref[p] * TILE - start) & (col_id < nright_ref[g] * rows)
                     amp = jnp.where(keep, -total / (low_ref[k, at, :] + high_ref[g]), 0.0).astype(BF16)
                     all_ref[k, at, pl.ds(pl.multiple_of(g * taken, taken), taken)] = amp
-                    amp_ref[u, :, at] = amp.T
+                    amp_ref[e, u, :, at] = amp.T
             k0, k1 = left_ref[2 * g], left_ref[2 * g + 1]
             for s in range(fits):
                 for start in range(0, aux, WIDE):
                     lanes = slice(start, start + WIDE)
                     back = (
-                        jnp.dot(amp_ref[0], lefts_ref[s, k0, :, lanes], preferred_element_type=F32)
-                        + jnp.dot(amp_ref[1], lefts_ref[s, k1, :, lanes], preferred_element_type=F32)
+                        jnp.dot(amp_ref[e, 0], lefts_ref[s, k0, :, lanes], preferred_element_type=F32)
+                        + jnp.dot(amp_ref[e, 1], lefts_ref[s, k1, :, lanes], preferred_element_type=F32)
                     ).astype(BF16)
                     for t in range(tiles):
                         turned = place_ref[NEXT + (s + t) % fits]
                         for h in range(rows // SUB):
                             for c in range(WIDE // 128):
-                                out_ref[(h * fits + turned) * cols + start // 128 + c, t] = back[
+                                out_ref[(h * fits + turned) * cols + start // 128 + c, e * tiles + t] = back[
                                     t * rows + h * SUB : t * rows + (h + 1) * SUB, c * 128 : (c + 1) * 128
                                 ]
 
+        @pl.when(n < steps)
+        def _():
+            for e in range(2):
+                group(2 * n + e, e)
+
         for low in range(2):
 
-            @pl.when((n >= count + low * half) & (n < count + (low + 1) * half))
+            @pl.when((n >= steps + low * half) & (n < steps + (low + 1) * half))
             def _(low=low):
-                k = n - count
+                k = n - steps
                 all_out_ref[0] = all_ref[k]
                 sum_part(place_ref, all_ref.at[k], rows_ref, fits // 2, far_refs[low])
 
     block = (1, virt, aux + wide)
     places = [
-        pl.BlockSpec(block, lambda n: (jnp.clip(n - count, 0, half - 1), 0, 0)),
-        pl.BlockSpec(block, lambda n: (jnp.clip(n - count - half, 0, half - 1), 0, 0)),
+        pl.BlockSpec(block, lambda n: (jnp.clip(n - steps, 0, half - 1), 0, 0)),
+        pl.BlockSpec(block, lambda n: (jnp.clip(n - steps - half, 0, half - 1), 0, 0)),
     ]
     return call(
         kernel,
-        count + orbs,
+        steps + orbs,
         [SMEM] * 4
         + [
             whole(left_levels.shape),
             whole(right_levels.shape),
-            pl.BlockSpec((peers, fits, SUB, 128), lambda n: (0, jnp.minimum(n, count - 1), 0, 0)),
+            pl.BlockSpec((peers, 2 * fits, SUB, 128), lambda n: (0, jnp.minimum(n, steps - 1), 0, 0)),
         ]
         + [ANY] * len(lefts),
         [
-            pl.BlockSpec((peers, tiles, SUB, 128), lambda n: (0, jnp.minimum(n, count - 1), 0, 0)),
+            pl.BlockSpec((peers, 2 * tiles, SUB, 128), lambda n: (0, jnp.minimum(n, steps - 1), 0, 0)),
         ]
         + [
-            pl.BlockSpec((1, virt, count * taken), lambda n: (jnp.maximum(n - count, 0), 0, 0)),
-            pl.BlockSpec((1, taken, fits * aux), lambda n: (jnp.minimum(n, count - 1), 0, 0)),
+            pl.BlockSpec((1, virt, count * taken), lambda n: (jnp.maximum(n - steps, 0), 0, 0)),
+            pl.BlockSpec((2, taken, fits * aux), lambda n: (jnp.minimum(n, steps - 1), 0, 0)),
         ]
         + places,
         [
@@ -232,8 +238,8 @@
         scratch=[
             pltpu.VMEM((fits, orbs, virt, aux), BF16),
             pltpu.VMEM((count, taken, fits * aux), BF16),
-            pltpu.VMEM((fits * aux, taken), BF16),
-            pltpu.VMEM((2, taken, virt), BF16),
+            pltpu.VMEM((2, fits * aux, taken), BF16),
+            pltpu.VMEM((2, 2, taken, virt), BF16),
             pltpu.VMEM((orbs, virt, count * taken), BF16),
             pltpu.SemaphoreType.DMA((len(lefts),)),
         ],
@@ -317,8 +323,9 @@
         def _(d):
             row = list_row(place_ref[ORB], n * block + d)
             for g in range(count):
-                spot = pl.ds(wanted_ref[row, g] * tiles, tiles)
-                total_ref[spot] += part_ref[d, g * tiles : (g + 1) * tiles].astype(F32)
+                spot = wanted_ref[row, g]
+                for t in range(tiles):
+                    total_ref[spot + t * orbs] += part_ref[d, g * tiles + t].astype(F32)
 
         @pl.when(n == steps - 1)
         def _():
@@ -327,8 +334,7 @@
             @pl.loop(0, peers)
             def _(o):
                 for q in range(fits):
-                    for k in range(orbs):
-                        out_ref[o * fits + q, k] = total_ref[(o * orbs + k) * tiles + tile[q]].astype(BF16)
+                    out_ref[o * fits + q] = total_ref[pl.ds((o * tiles + tile[q]) * orbs, orbs)].astype(BF16)
 
     out = (peers * fits, orbs, SUB, 128)
     return call(
@@ -352,7 +358,6 @@
     peers = sums.shape[0] // fits
 
     def kernel(place_ref, own_ref, below_ref, above_ref, sums_ref, gamma_ref, dens_ref):
-        k = pl.program_id(0)
         total = own_ref[0].astype(F32) + below_ref[0].astype(F32) + above_ref[0].astype(F32)
         gamma_ref[0] = total[:, 0:aux]
         dens_ref[0] = total[:, aux:width]
@@ -362,13 +367,13 @@
             lanes = slice(c * 128, (c + 1) * 128)
             for z in range(fits):
                 at = pl.ds(pl.multiple_of(tile + z * rows + h * SUB, SUB), SUB)
-                gamma_ref[0, at, lanes] += sums_ref[m * fits + z, k].astype(F32)
+                gamma_ref[0, at, lanes] += sums_ref[m * fits + z, 0].astype(F32)
 
     block = pl.BlockSpec((1, virt, width), lambda k: (k, 0, 0))
     return call(
         kernel,
         orbs,
-        [SMEM, block, block, block, whole(sums.shape)],
+        [SMEM, block, block, block, pl.BlockSpec((peers * fits, 1, SUB, 128), lambda k: (0, k, 0, 0))],
         [pl.BlockSpec((1, virt, aux), lambda k: (k, 0, 0)), pl.BlockSpec((1, virt, wide), lambda k: (k, 0, 0))],
         [sds((orbs, virt, aux), F32), sds((orbs, virt, wide), F32)],
         (place, own, below, above, sums),
@@ -396,13 +401,12 @@
     def to_all(x):
         return lax.all_to_all(x, ("orb", "fit"), split_axis=0, concat_axis=0, tiled=True)
 
-    half = orbs // 2
     one = [blocks[k : k + 1] for k in range(orbs)]
     last0, next3 = shift(one[0], 1), shift(one[3], fits - 1)
     right = pairs[::2, 1]
     groups = right.shape[0]
     held = to_all(pack_blocks(place, blocks, peers, fits))
-    wanted = jnp.pad(right[None], ((0, 0), (0, 128 - groups)))
+    wanted = jnp.pad((right // orbs * (fits * orbs) + right % orbs)[None], ((0, 0), (0, 128 - groups)))
     for count, stride in DIGITS:
         wanted = jnp.concatenate(
             [wanted]
@@ -426,13 +430,10 @@
     ).reshape(groups, 1, virt // fits)
 
     pieces = to_orb(pick_pieces(place, wanted, held, fits, after=[last0, next3]))
-    last1, next2 = shift(one[1], 1), shift(one[2], fits - 1)
+    last, next_ = shift(blocks[1:], 1), shift(blocks[:-1], fits - 1)
     far0, far3 = shift(last0, 1), shift(next3, fits - 1)
-    low, high, last1, next2 = lax.optimization_barrier((blocks[:half], blocks[half:], last1, next2))
-    last2, next0 = shift(high, 1), shift(low, fits - 1)
-    far1, far2 = shift(last1, 1), shift(next2, fits - 1)
-    lefts = [(blocks, 0, 0), (next0, 1, 0), (next2, 1, 2), (next3, 1, 3)]
-    lefts += [(last0, 3, 0), (last1, 3, 1), (last2, 3, 2)]
+    far1, far2 = shift(last[:1], 1), shift(next_[-1:], fits - 1)
+    lefts = [(blocks, 0, 0), (next_, 1, 0), (next3, 1, orbs - 1), (last0, 3, 0), (last, 3, 1)]
     lefts += [(far0, 2, 0), (far1, 2, 1), (far2, 2, 2), (far3, 2, 3)]
     back, amps, rows, *far = pair_terms(place, plan, left_levels, right_levels, pieces, lefts, fits)
     far = [shift(far[0], 1), shift(far[1], fits - 1)]

time: 303 us -> 298 us (0.983)
    ppermute x14 -> x12, waiting for transfers between devices: 118 us -> 115 us  [shift(): return lax.ppermute(x, 'fit', [(n, (n + k) % fits) for n in range(fits)])]
    ppermute x14 -> x12, starting transfers between devices: 14 us -> 14.7 us  [shift(): return lax.ppermute(x, 'fit', [(n, (n + k) % fits) for n in range(fits)])]
  transfers between devices with their start and end apart: 25 -> 23, of which waited for: 16 -> 16; matrix products, arithmetic and copies ran while one was open for 4% -> 5% of each run, Pallas kernels for 8% -> 8%
where the time goes in v4:
time: 298 us; the launch traced here: 297 us
  waiting for transfers between devices  149 us (50%)
  Pallas kernels  69.5 us (23%)
  starting transfers between devices  57.9 us (19%)
  local copies, waits for them, and re-layouts  17 us (6%)
    ppermute x12, waiting for transfers between devices, shift(): return lax.ppermute(x, 'fit', [(n, (n + k) % fits) for n in range(fits)])  115 us
    pallas_call x7, Pallas kernels, call(): pl.pallas_call(kernel, grid=(grid,), in_specs=in_specs, out_specs=out_spe...  69.5 us
    all_to_all x2, starting transfers between devices, to_all(): lax.all_to_all(x, ('orb', 'fit'), split_axis=0, concat_axis=0, tiled=True)  19.8 us
    ppermute x7, waiting for transfers between devices, on_device(): lax.ppermute(wanted, 'orb', [(n, n + ((n // stride + k) % count - n // st...  19.7 us
    all_to_all x2, starting transfers between devices, to_orb(): return lax.all_to_all(x, 'orb', split_axis=0, concat_axis=0, tiled=True)  15.5 us
    ppermute x12, starting transfers between devices, shift(): return lax.ppermute(x, 'fit', [(n, (n + k) % fits) for n in range(fits)])  14.7 us
    all_to_all x2, waiting for transfers between devices, to_orb(): return lax.all_to_all(x, 'orb', split_axis=0, concat_axis=0, tiled=True)  11.4 us
    ppermute x7, starting transfers between devices, on_device(): lax.ppermute(wanted, 'orb', [(n, n + ((n // stride + k) % count - n // st...  7.93 us
  transfers between devices with their start and end apart: 23, of which 16 were waited for; matrix products, arithmetic and copies ran while one was open for 5% of the time, Pallas kernels for 8%

profile of v4, /device:TPU:1, one launch (start us, length us, event | category | flops | bytes accessed | tf_op | source)
XLA Modules:
  0.0 297.2 jit_solution(7016832501426181196)
XLA Ops:
  0.7 0.7 concatenate.14.place_ref
  1.4 4.1 %pack_blocks.1 = bf16[128,4,16,128]{3,2,1,0:T(8,128)(2,1)} custom-call(s32[14]{0:T(128)} %concatenate.14.place_ref, bf16[4,512,512]{2,1,0:T(8,128)(2,1)} %refs_0_.1), custom_call_target="tpu_custom_call" | custom-call | bytes 1024 | tf_op jit(solution)/shard_map/pack_blocks/pallas_call | solution.py:32
  5.5 12.0 %all-to-all-start = ((bf16[128,4,16,128]{3,2,1,0:T(8,128)(2,1)}), bf16[128,4,16,128]{3,2,1,0:T(8,128)(2,1)}, u32[]{:S(2)}, u32[]{:S(2)}) async-start(bf16[128,4,16,128]{3,2,1,0:T(8,128)(2,1)} %pack_blocks.1), calls=%async_computation | async-start | bytes 4194304 | tf_op jit(solution)/shard_map/all_to_all | solution.py:402
  17.5 1.0 fusion.10
  18.5 3.3 %collective-permute-start.8 = (bf16[1,512,512]{2,1,0:T(8,128)(2,1)}, bf16[1,512,512]{2,1,0:T(8,128)(2,1)S(1)}, u32[]{:S(2)}, u32[]{:S(2)}) collective-permute-start(bf16[1,512,512]{2,1,0:T(8,128)(2,1)} %get-tuple-element.26), channel_id=1, source_target_pairs={{0,3},{1,0},{2,1},{3,2},{4,7},{5,4},{6,5},{7,6},{8,11},{9,8},{10,9... | collective-permute-start | bytes 1572872 | tf_op jit(solution)/shard_map/ppermute | solution.py:396
  21.8 0.1 slice.29
  21.9 0.7 collective-permute-start
  22.6 0.8 collective-permute-done
  23.4 2.4 collective-permute-start.3
  25.9 0.5 collective-permute-start.2
  26.4 0.6 collective-permute-start.1
  27.0 14.0 %collective-permute-done.3 = s32[2,128]{1,0:T(2,128)S(1)} collective-permute-done((s32[2,128]{1,0:T(2,128)S(1)}, s32[2,128]{1,0:T(2,128)S(1)}, u32[]{:S(2)}, u32[]{:S(2)}) %collective-permute-start.3) | collective-permute-done | bytes 1056 | tf_op jit(solution)/shard_map/ppermute | solution.py:414
  41.1 1.5 collective-permute-done.2
  42.6 2.5 collective-permute-start.6
  45.1 0.5 collective-permute-start.5
  45.6 0.6 collective-permute-start.4
  46.2 2.9 collective-permute-done.5
  49.1 0.5 collective-permute-done.4
  49.6 2.4 concatenate.17
  52.0 1.0 collective-permute-done.8.refs_1_.refs_2_
  53.0 1.8 collective-permute-done.7.refs_0_.refs_3_
  54.9 0.8 copy-done.8
  55.7 4.9 %pick_pieces.1 = bf16[32,32,16,128]{3,2,1,0:T(8,128)(2,1)} custom-call(s32[14]{0:T(128)} %concatenate.14.place_ref, s32[32,8]{1,0:T(8,128)} %bitcast.37, bf16[512,16,128]{2,1,0:T(8,128)(2,1)} %bitcast.13.held_ref, bf16[1,512,512]{2,1,0:T(8,128)(2,1)} %copy-done.8, bf16[1,512,512]{2,1,0:T(8,128)(2,1)} %copy-done.6), custom_call_target="tpu_custom_call" | custom-call | bytes 1024 | tf_op jit(solution)/shard_map/pick_pieces/pallas_call | solution.py:32
  60.6 7.1 %all-to-all-start.1 = ((bf16[32,32,16,128]{3,2,1,0:T(8,128)(2,1)}), bf16[32,32,16,128]{3,2,1,0:T(8,128)(2,1)}, u32[]{:S(2)}, u32[]{:S(2)}) async-start(bf16[32,32,16,128]{3,2,1,0:T(8,128)(2,1)} %pick_pieces.1), calls=%async_computation.1 | async-start | bytes 8388608 | tf_op jit(solution)/shard_map/all_to_all | solution.py:399
  67.7 1.9 fusion.9
  69.7 0.1 collective-permute-start.10
  69.8 2.5 collective-permute-start.9
  72.4 0.6 gather_fusion.5
  73.0 0.6 gather_fusion.1
  73.7 0.6 gather_fusion.3
  74.3 0.6 gather_fusion.4
  74.9 0.5 fusion.8
  75.5 0.6 broadcast_select_fusion.1.nright_ref
  76.2 0.1 collective-permute-start.14
  76.3 1.4 collective-permute-start.11
  77.7 29.1 %collective-permute-done.10.refs_4_ = bf16[3,512,512]{2,1,0:T(8,128)(2,1)S(1)} collective-permute-done((bf16[3,512,512]{2,1,0:T(8,128)(2,1)}, bf16[3,512,512]{2,1,0:T(8,128)(2,1)S(1)}, u32[]{:S(2)}, u32[]{:S(2)}) %collective-permute-start.10) | collective-permute-done | bytes 1572896 | tf_op jit(solution)/shard_map/ppermute | solution.py:396
  107.0 2.3 slice.51
  109.3 2.3 collective-permute-start.13
  111.6 0.6 gather_fusion.2
  112.1 0.7 gather_fusion
  112.8 0.7 reshape.214.high_ref
  113.5 0.4 copy.10
  113.8 0.5 bitcast_select_fusion.nleft_ref
  114.4 1.1 select_subtract_fusion.low_ref
  115.5 1.5 collective-permute-done.14.refs_8_
  116.9 1.2 collective-permute-done.11.refs_5_
  118.1 11.2 %collective-permute-done.12.refs_6_ = bf16[1,512,512]{2,1,0:T(8,128)(2,1)} collective-permute-done((bf16[1,512,512]{2,1,0:T(8,128)(2,1)S(1)}, bf16[1,512,512]{2,1,0:T(8,128)(2,1)}, u32[]{:S(2)}, u32[]{:S(2)}) %collective-permute-start.12) | collective-permute-done | bytes 524320 | tf_op jit(solution)/shard_map/ppermute | solution.py:396
  129.3 28.9 %pair_terms.1 = (bf16[32,32,16,128]{3,2,1,0:T(8,128)(2,1)}, bf16[4,512,1024]{2,1,0:T(8,128)(2,1)}, bf16[8,128,2048]{2,1,0:T(8,128)(2,1)}, bf16[2,512,640]{2,1,0:T(8,128)(2,1)}, bf16[2,512,640]{2,1,0:T(8,128)(2,1)}) custom-call(s32[14]{0:T(128)} %concatenate.14.place_ref, s32[16]{0:T(128)} %get-tuple-element.29.left_ref, s32[16]{0:T(128)} %bitcast_select_fusion.nleft_ref, ...), custom_call_target="tpu_custom_call" | custom-call | bytes 1024 | tf_op jit(solution)/shard_map/pair_terms/pallas_call | solution.py:32
  158.3 8.3 %all-to-all-start.2 = ((bf16[32,32,16,128]{3,2,1,0:T(8,128)(2,1)}), bf16[32,32,16,128]{3,2,1,0:T(8,128)(2,1)}, u32[]{:S(2)}, u32[]{:S(2)}) async-start(bf16[32,32,16,128]{3,2,1,0:T(8,128)(2,1)} %get-tuple-element.21), calls=%async_computation.2 | async-start | bytes 8388608 | tf_op jit(solution)/shard_map/all_to_all | solution.py:399
  166.7 2.7 collective-permute-start.16
  169.5 14.2 %near_terms.1 = (bf16[4,512,640]{2,1,0:T(8,128)(2,1)}, bf16[4,512,640]{2,1,0:T(8,128)(2,1)}, bf16[4,512,640]{2,1,0:T(8,128)(2,1)}) custom-call(s32[14]{0:T(128)} %concatenate.14.place_ref, bf16[4,512,1024]{2,1,0:T(8,128)(2,1)} %get-tuple-element.12.all_ref, bf16[8,128,2048]{2,1,0:T(8,128)(2,1)} %get-tuple-element.13.rows_ref), custom_call_target="tpu_custom_call" | custom-call | bytes 1024 | tf_op jit(solution)/shard_map/near_terms/pallas_call | solution.py:32
  183.7 14.4 %collective-permute-done.15.c_ref = bf16[2,512,640]{2,1,0:T(8,128)(2,1)S(1)} collective-permute-done((bf16[2,512,640]{2,1,0:T(8,128)(2,1)S(1)}, bf16[2,512,640]{2,1,0:T(8,128)(2,1)S(1)}, u32[]{:S(2)}, u32[]{:S(2)}) %collective-permute-start.15) | collective-permute-done | bytes 1310752 | tf_op jit(solution)/shard_map/ppermute | solution.py:396
  198.1 1.1 copy-done.10
  199.2 0.5 copy-done.11
  199.6 3.8 %merge.1 = (bf16[4,512,640]{2,1,0:T(8,128)(2,1)}, bf16[4,512,640]{2,1,0:T(8,128)(2,1)}) custom-call(bf16[4,512,640]{2,1,0:T(8,128)(2,1)} %get-tuple-element.15.a_ref, bf16[4,512,640]{2,1,0:T(8,128)(2,1)} %get-tuple-element.16.b_ref, bf16[2,512,640]{2,1,0:T(8,128)(2,1)} %copy-done.10, ...), custom_call_target="tpu_custom_call", output_to_operand_aliasing={{0}: (0, {}), {1}: (1, {})} | custom-call | bytes 1024 | tf_op jit(solution)/shard_map/merge/pallas_call | solution.py:32
  203.4 2.1 collective-permute-start.18
  205.5 11.4 %all-to-all-done.2.part_ref = bf16[32,32,16,128]{3,2,1,0:T(8,128)(2,1)} async-done(((bf16[32,32,16,128]{3,2,1,0:T(8,128)(2,1)}), bf16[32,32,16,128]{3,2,1,0:T(8,128)(2,1)}, u32[]{:S(2)}, u32[]{:S(2)}) %all-to-all-start.2) | async-done | bytes 4194336 | tf_op jit(solution)/shard_map/all_to_all | solution.py:399
  216.9 6.0 %sum_returned.1 = bf16[128,4,16,128]{3,2,1,0:T(8,128)(2,1)} custom-call(s32[14]{0:T(128)} %concatenate.14.place_ref, s32[32,8]{1,0:T(8,128)} %bitcast.38, bf16[32,32,16,128]{3,2,1,0:T(8,128)(2,1)} %all-to-all-done.2.part_ref, bf16[4,512,640]{2,1,0:T(8,128)(2,1)} %get-tuple-element.19.refs_0_), custom_call_target="tpu_custom_call" | custom-call | bytes 1024 | tf_op jit(solution)/shard_map/sum_returned/pallas_call | solution.py:32
  222.9 7.9 %all-to-all-start.3 = ((bf16[128,4,16,128]{3,2,1,0:T(8,128)(2,1)}), bf16[128,4,16,128]{3,2,1,0:T(8,128)(2,1)S(1)}, u32[]{:S(2)}, u32[]{:S(2)}) async-start(bf16[128,4,16,128]{3,2,1,0:T(8,128)(2,1)} %sum_returned.1), calls=%async_computation.3 | async-start | bytes 4194304 | tf_op jit(solution)/shard_map/all_to_all | solution.py:402
  230.8 51.3 %collective-permute-done.18.above_ref = bf16[4,512,640]{2,1,0:T(8,128)(2,1)} collective-permute-done((bf16[4,512,640]{2,1,0:T(8,128)(2,1)}, bf16[4,512,640]{2,1,0:T(8,128)(2,1)}, u32[]{:S(2)}, u32[]{:S(2)}) %collective-permute-start.18) | collective-permute-done | bytes 2621472 | tf_op jit(solution)/shard_map/ppermute | solution.py:396
  282.1 3.1 %collective-permute-done.17.below_ref = bf16[4,512,640]{2,1,0:T(8,128)(2,1)} collective-permute-done((bf16[4,512,640]{2,1,0:T(8,128)(2,1)}, bf16[4,512,640]{2,1,0:T(8,128)(2,1)}, u32[]{:S(2)}, u32[]{:S(2)}) %collective-permute-start.17) | collective-permute-done | bytes 2621472 | tf_op jit(solution)/shard_map/ppermute | solution.py:396
  285.2 2.8 all-to-all-done.3.sums_ref
  288.1 1.3 copy-done.4
  289.4 7.6 %add_all.1 = (f32[4,512,512]{2,1,0:T(8,128)}, f32[4,512,128]{2,1,0:T(8,128)}) custom-call(s32[14]{0:T(128)} %concatenate.14.place_ref, bf16[4,512,640]{2,1,0:T(8,128)(2,1)} %get-tuple-element.14.own_ref, bf16[4,512,640]{2,1,0:T(8,128)(2,1)} %collective-permute-done.17.below_ref, bf16[4,512,640]{2,1,0:T(8,128)(2,1)} %collective-permute-done.18.above_ref, ...), custom_call_target="tpu_custom_call" | custom-call | bytes 1024 | tf_op jit(solution)/shard_map/add_all/pallas_call | solution.py:32
  (57 shorter events, 0.6 us)
Async XLA Ops:
  0.6 73.7 %copy-start = (f32[128,512]{1,0:T(8,128)S(1)}, f32[128,512]{1,0:T(8,128)}, u32[]{:S(2)}) copy-start(f32[128,512]{1,0:T(8,128)} %param.7) | copy-start | bytes 786436
  5.5 12.0 %copy-start.3 = (bf16[4,512,512]{2,1,0:T(8,128)(2,1)S(1)}, bf16[4,512,512]{2,1,0:T(8,128)(2,1)}, u32[]{:S(2)}) copy-start(bf16[4,512,512]{2,1,0:T(8,128)(2,1)} %refs_0_.1) | copy-start | bytes 6291460
  5.5 49.4 %all-to-all-start = ((bf16[128,4,16,128]{3,2,1,0:T(8,128)(2,1)}), bf16[128,4,16,128]{3,2,1,0:T(8,128)(2,1)}, u32[]{:S(2)}, u32[]{:S(2)}) async-start(bf16[128,4,16,128]{3,2,1,0:T(8,128)(2,1)} %pack_blocks.1), calls=%async_computation | async-start | bytes 4194304 | tf_op jit(solution)/shard_map/all_to_all | solution.py:402
  17.4 4.3 %copy-start.12 = (s32[16,2]{0,1:T(2,128)S(1)}, s32[16,2]{0,1:T(2,128)}, u32[]{:S(2)}) copy-start(s32[16,2]{0,1:T(2,128)} %param.9) | copy-start | bytes 388
  18.5 34.5 %collective-permute-start.8 = (bf16[1,512,512]{2,1,0:T(8,128)(2,1)}, bf16[1,512,512]{2,1,0:T(8,128)(2,1)S(1)}, u32[]{:S(2)}, u32[]{:S(2)}) collective-permute-start(bf16[1,512,512]{2,1,0:T(8,128)(2,1)} %get-tuple-element.26), channel_id=1, source_target_pairs={{0,3},{1,0},{2,1},{3,2},{4,7},{5,4},{6,5},{7,6},{8,11},{9,8},{10,9... | collective-permute-start | bytes 1572872 | tf_op jit(solution)/shard_map/ppermute | solution.py:396
  21.8 33.1 %collective-permute-start.7 = (bf16[1,512,512]{2,1,0:T(8,128)(2,1)}, bf16[1,512,512]{2,1,0:T(8,128)(2,1)S(1)}, u32[]{:S(2)}, u32[]{:S(2)}) collective-permute-start(bf16[1,512,512]{2,1,0:T(8,128)(2,1)} %get-tuple-element.27), channel_id=1, source_target_pairs={{0,1},{1,2},{2,3},{3,0},{4,5},{5,6},{6,7},{7,4},{8,9},{9,10},{10,1... | collective-permute-start | bytes 1572872 | tf_op jit(solution)/shard_map/ppermute | solution.py:396
  21.9 1.5 collective-permute-start
  23.4 17.6 %collective-permute-start.3 = (s32[2,128]{1,0:T(2,128)S(1)}, s32[2,128]{1,0:T(2,128)S(1)}, u32[]{:S(2)}, u32[]{:S(2)}) collective-permute-start(s32[2,128]{1,0:T(2,128)S(1)} %pad_add_fusion), channel_id=1, source_target_pairs={{0,24},{4,28},{8,0},{12,4},{16,8},{20,12},{24,16},{28,20},{32,56},... | collective-permute-start | bytes 3080 | tf_op jit(solution)/shard_map/ppermute | solution.py:414
  25.9 16.7 %collective-permute-start.2 = (s32[2,128]{1,0:T(2,128)S(1)}, s32[2,128]{1,0:T(2,128)S(1)}, u32[]{:S(2)}, u32[]{:S(2)}) collective-permute-start(s32[2,128]{1,0:T(2,128)S(1)} %pad_add_fusion), channel_id=1, source_target_pairs={{0,16},{4,20},{8,24},{12,28},{16,0},{20,4},{24,8},{28,12},{32,48},... | collective-permute-start | bytes 3080 | tf_op jit(solution)/shard_map/ppermute | solution.py:414
  26.4 16.1 %collective-permute-start.1 = (s32[2,128]{1,0:T(2,128)S(1)}, s32[2,128]{1,0:T(2,128)S(1)}, u32[]{:S(2)}, u32[]{:S(2)}) collective-permute-start(s32[2,128]{1,0:T(2,128)S(1)} %pad_add_fusion), channel_id=1, source_target_pairs={{0,8},{4,12},{8,16},{12,20},{16,24},{20,28},{24,0},{28,4},{32,40},... | collective-permute-start | bytes 3080 | tf_op jit(solution)/shard_map/ppermute | solution.py:414
  42.6 3.6 %collective-permute-start.6 = (s32[8,128]{1,0:T(8,128)S(1)}, s32[8,128]{1,0:T(8,128)S(1)}, u32[]{:S(2)}, u32[]{:S(2)}) collective-permute-start(s32[8,128]{1,0:T(8,128)S(1)} %concatenate.16), channel_id=1, source_target_pairs={{0,96},{4,100},{8,104},{12,108},{16,112},{20,116},{24,120},{28,124... | collective-permute-start | bytes 12296 | tf_op jit(solution)/shard_map/ppermute | solution.py:414
  45.1 4.0 %collective-permute-start.5 = (s32[8,128]{1,0:T(8,128)S(1)}, s32[8,128]{1,0:T(8,128)S(1)}, u32[]{:S(2)}, u32[]{:S(2)}) collective-permute-start(s32[8,128]{1,0:T(8,128)S(1)} %concatenate.16), channel_id=1, source_target_pairs={{0,64},{4,68},{8,72},{12,76},{16,80},{20,84},{24,88},{28,92},{32,9... | collective-permute-start | bytes 12296 | tf_op jit(solution)/shard_map/ppermute | solution.py:414
  45.6 4.0 %collective-permute-start.4 = (s32[8,128]{1,0:T(8,128)S(1)}, s32[8,128]{1,0:T(8,128)S(1)}, u32[]{:S(2)}, u32[]{:S(2)}) collective-permute-start(s32[8,128]{1,0:T(8,128)S(1)} %concatenate.16), channel_id=1, source_target_pairs={{0,32},{4,36},{8,40},{12,44},{16,48},{20,52},{24,56},{28,60},{32,6... | collective-permute-start | bytes 12296 | tf_op jit(solution)/shard_map/ppermute | solution.py:414
  53.0 1.8 copy-start.6
  54.9 0.8 copy-start.8
  60.6 68.8 %all-to-all-start.1 = ((bf16[32,32,16,128]{3,2,1,0:T(8,128)(2,1)}), bf16[32,32,16,128]{3,2,1,0:T(8,128)(2,1)}, u32[]{:S(2)}, u32[]{:S(2)}) async-start(bf16[32,32,16,128]{3,2,1,0:T(8,128)(2,1)} %pick_pieces.1), calls=%async_computation.1 | async-start | bytes 8388608 | tf_op jit(solution)/shard_map/all_to_all | solution.py:399
  67.7 4.7 %copy-start.15 = (s32[128]{0:T(128)S(1)}, s32[128]{0:T(128)}, u32[]{:S(2)}) copy-start(s32[128]{0:T(128)} %param.8) | copy-start | bytes 1540
  67.7 4.7 %copy-start.2 = (f32[128]{0:T(128)S(1)}, f32[128]{0:T(128)}, u32[]{:S(2)}) copy-start(f32[128]{0:T(128)} %param.6) | copy-start | bytes 1540
  67.7 8.5 %copy-start.7 = (bf16[1,512,512]{2,1,0:T(8,128)(2,1)S(1)}, bf16[1,512,512]{2,1,0:T(8,128)(2,1)}, u32[]{:S(2)}) copy-start(bf16[1,512,512]{2,1,0:T(8,128)(2,1)} %copy-done.6) | copy-start | bytes 1572868
  67.7 8.6 %copy-start.9 = (bf16[1,512,512]{2,1,0:T(8,128)(2,1)S(1)}, bf16[1,512,512]{2,1,0:T(8,128)(2,1)}, u32[]{:S(2)}) copy-start(bf16[1,512,512]{2,1,0:T(8,128)(2,1)} %copy-done.8) | copy-start | bytes 1572868
  69.7 37.2 %collective-permute-start.10 = (bf16[3,512,512]{2,1,0:T(8,128)(2,1)}, bf16[3,512,512]{2,1,0:T(8,128)(2,1)S(1)}, u32[]{:S(2)}, u32[]{:S(2)}) collective-permute-start(bf16[3,512,512]{2,1,0:T(8,128)(2,1)} %get-tuple-element.24), channel_id=1, source_target_pairs={{0,1},{1,2},{2,3},{3,0},{4,5},{5,6},{6,7},{7,4},{8,9},{9,10},{10,1... | collective-permute-start | bytes 4718600 | tf_op jit(solution)/shard_map/ppermute | solution.py:396
  69.8 37.2 %collective-permute-start.9 = (bf16[3,512,512]{2,1,0:T(8,128)(2,1)}, bf16[3,512,512]{2,1,0:T(8,128)(2,1)}, u32[]{:S(2)}, u32[]{:S(2)}) collective-permute-start(bf16[3,512,512]{2,1,0:T(8,128)(2,1)} %get-tuple-element.25), channel_id=1, source_target_pairs={{0,3},{1,0},{2,1},{3,2},{4,7},{5,4},{6,5},{7,6},{8,11},{9,8},{10,9... | collective-permute-start | bytes 4718600 | tf_op jit(solution)/shard_map/ppermute | solution.py:396
  76.2 40.8 %collective-permute-start.14 = (bf16[1,512,512]{2,1,0:T(8,128)(2,1)S(1)}, bf16[1,512,512]{2,1,0:T(8,128)(2,1)}, u32[]{:S(2)}, u32[]{:S(2)}) collective-permute-start(bf16[1,512,512]{2,1,0:T(8,128)(2,1)S(1)} %copy-done.7), channel_id=1, source_target_pairs={{0,3},{1,0},{2,1},{3,2},{4,7},{5,4},{6,5},{7,6},{8,11},{9,8},{10,9... | collective-permute-start | bytes 1572872 | tf_op jit(solution)/shard_map/ppermute | solution.py:396
  76.3 41.8 %collective-permute-start.11 = (bf16[1,512,512]{2,1,0:T(8,128)(2,1)S(1)}, bf16[1,512,512]{2,1,0:T(8,128)(2,1)}, u32[]{:S(2)}, u32[]{:S(2)}) collective-permute-start(bf16[1,512,512]{2,1,0:T(8,128)(2,1)S(1)} %copy-done.9), channel_id=1, source_target_pairs={{0,1},{1,2},{2,3},{3,0},{4,5},{5,6},{6,7},{7,4},{8,9},{9,10},{10,1... | collective-permute-start | bytes 1572872 | tf_op jit(solution)/shard_map/ppermute | solution.py:396
  106.9 6.6 %copy-start.5 = (bf16[3,512,512]{2,1,0:T(8,128)(2,1)}, bf16[3,512,512]{2,1,0:T(8,128)(2,1)S(1)}, u32[]{:S(2)}) copy-start(bf16[3,512,512]{2,1,0:T(8,128)(2,1)S(1)} %collective-permute-done.10.refs_4_) | copy-start | bytes 4718596
  106.9 22.4 %collective-permute-start.12 = (bf16[1,512,512]{2,1,0:T(8,128)(2,1)S(1)}, bf16[1,512,512]{2,1,0:T(8,128)(2,1)}, u32[]{:S(2)}, u32[]{:S(2)}) collective-permute-start(bf16[1,512,512]{2,1,0:T(8,128)(2,1)S(1)} %slice.50), channel_id=1, source_target_pairs={{0,1},{1,2},{2,3},{3,0},{4,5},{5,6},{6,7},{7,4},{8,9},{9,10},{10,1... | collective-permute-start | bytes 1572872 | tf_op jit(solution)/shard_map/ppermute | solution.py:396
  109.3 20.1 %collective-permute-start.13 = (bf16[1,512,512]{2,1,0:T(8,128)(2,1)}, bf16[1,512,512]{2,1,0:T(8,128)(2,1)}, u32[]{:S(2)}, u32[]{:S(2)}) collective-permute-start(bf16[1,512,512]{2,1,0:T(8,128)(2,1)} %slice.51), channel_id=1, source_target_pairs={{0,3},{1,0},{2,1},{3,2},{4,7},{5,4},{6,5},{7,6},{8,11},{9,8},{10,9... | collective-permute-start | bytes 1572872 | tf_op jit(solution)/shard_map/ppermute | solution.py:396
  158.3 8.4 %copy-start.14 = (bf16[2,512,640]{2,1,0:T(8,128)(2,1)S(1)}, bf16[2,512,640]{2,1,0:T(8,128)(2,1)}, u32[]{:S(2)}) copy-start(bf16[2,512,640]{2,1,0:T(8,128)(2,1)} %get-tuple-element.17) | copy-start | bytes 3932164
  158.3 8.5 %copy-start.13 = (bf16[2,512,640]{2,1,0:T(8,128)(2,1)S(1)}, bf16[2,512,640]{2,1,0:T(8,128)(2,1)}, u32[]{:S(2)}) copy-start(bf16[2,512,640]{2,1,0:T(8,128)(2,1)} %get-tuple-element.18) | copy-start | bytes 3932164
  158.3 58.6 %all-to-all-start.2 = ((bf16[32,32,16,128]{3,2,1,0:T(8,128)(2,1)}), bf16[32,32,16,128]{3,2,1,0:T(8,128)(2,1)}, u32[]{:S(2)}, u32[]{:S(2)}) async-start(bf16[32,32,16,128]{3,2,1,0:T(8,128)(2,1)} %get-tuple-element.21), calls=%async_computation.2 | async-start | bytes 8388608 | tf_op jit(solution)/shard_map/all_to_all | solution.py:399
  166.6 31.5 %collective-permute-start.15 = (bf16[2,512,640]{2,1,0:T(8,128)(2,1)S(1)}, bf16[2,512,640]{2,1,0:T(8,128)(2,1)S(1)}, u32[]{:S(2)}, u32[]{:S(2)}) collective-permute-start(bf16[2,512,640]{2,1,0:T(8,128)(2,1)S(1)} %copy-done.14), channel_id=1, source_target_pairs={{0,1},{1,2},{2,3},{3,0},{4,5},{5,6},{6,7},{7,4},{8,9},{9,10},{10,1... | collective-permute-start | bytes 3932168 | tf_op jit(solution)/shard_map/ppermute | solution.py:396
  166.7 31.4 %collective-permute-start.16 = (bf16[2,512,640]{2,1,0:T(8,128)(2,1)S(1)}, bf16[2,512,640]{2,1,0:T(8,128)(2,1)S(1)}, u32[]{:S(2)}, u32[]{:S(2)}) collective-permute-start(bf16[2,512,640]{2,1,0:T(8,128)(2,1)S(1)} %copy-done.13), channel_id=1, source_target_pairs={{0,3},{1,0},{2,1},{3,2},{4,7},{5,4},{6,5},{7,6},{8,11},{9,8},{10,9... | collective-permute-start | bytes 3932168 | tf_op jit(solution)/shard_map/ppermute | solution.py:396
  198.1 1.1 copy-start.10
  198.1 1.5 copy-start.11
  203.4 78.7 %collective-permute-start.18 = (bf16[4,512,640]{2,1,0:T(8,128)(2,1)}, bf16[4,512,640]{2,1,0:T(8,128)(2,1)}, u32[]{:S(2)}, u32[]{:S(2)}) collective-permute-start(bf16[4,512,640]{2,1,0:T(8,128)(2,1)} %get-tuple-element.20), channel_id=1, source_target_pairs={{0,3},{1,0},{2,1},{3,2},{4,7},{5,4},{6,5},{7,6},{8,11},{9,8},{10,9... | collective-permute-start | bytes 7864328 | tf_op jit(solution)/shard_map/ppermute | solution.py:396
  205.5 79.8 %collective-permute-start.17 = (bf16[4,512,640]{2,1,0:T(8,128)(2,1)}, bf16[4,512,640]{2,1,0:T(8,128)(2,1)}, u32[]{:S(2)}, u32[]{:S(2)}) collective-permute-start(bf16[4,512,640]{2,1,0:T(8,128)(2,1)} %get-tuple-element.19.refs_0_), channel_id=1, source_target_pairs={{0,1},{1,2},{2,3},{3,0},{4,5},{5,6},{6,7},{7,4},{8,9},{9,10},{10,1... | collective-permute-start | bytes 7864328 | tf_op jit(solution)/shard_map/ppermute | solution.py:396
  222.9 65.2 %all-to-all-start.3 = ((bf16[128,4,16,128]{3,2,1,0:T(8,128)(2,1)}), bf16[128,4,16,128]{3,2,1,0:T(8,128)(2,1)S(1)}, u32[]{:S(2)}, u32[]{:S(2)}) async-start(bf16[128,4,16,128]{3,2,1,0:T(8,128)(2,1)} %sum_returned.1), calls=%async_computation.3 | async-start | bytes 4194304 | tf_op jit(solution)/shard_map/all_to_all | solution.py:402
  288.1 1.3 copy-start.4
  289.4 7.6 %copy-start.1 = (f32[128,512]{1,0:T(8,128)S(1)}, f32[128,512]{1,0:T(8,128)}, u32[]{:S(2)}) copy-start(f32[128,512]{1,0:T(8,128)} %param.7) | copy-start | bytes 786436

commit v5 on v4

--- a/solution.py
+++ b/solution.py
@@ -77,6 +77,7 @@
         pl.BlockSpec((block * fits, orbs, SUB, 128), lambda n: (n, 0, 0, 0)),
         sds((peers * fits, orbs, SUB, 128), BF16),
         (place, blocks),
+        memory=16,
         name="pack_blocks",
     )
 
@@ -301,6 +302,7 @@
         [sds(rise.shape, BF16)] * 2,
         (rise, fall, *far),
         aliases={0: 0, 1: 1},
+        memory=16,
         name="merge",
     )
 

time: 298 us -> 296 us (level)
  Pallas kernels: 69.5 us -> 66.5 us
    pallas_call x7, Pallas kernels: 69.5 us -> 66.5 us  [call(): pl.pallas_call(kernel, grid=(grid,), in_specs=in_specs, out_specs=out_spe...]
where the time goes in v5:
time: 296 us; the launch traced here: 295 us
  waiting for transfers between devices  149 us (50%)
  Pallas kernels  66.5 us (22%)
  starting transfers between devices  58.3 us (20%)
  local copies, waits for them, and re-layouts  17.8 us (6%)
    ppermute x12, waiting for transfers between devices, shift(): return lax.ppermute(x, 'fit', [(n, (n + k) % fits) for n in range(fits)])  113 us
    pallas_call x7, Pallas kernels, call(): pl.pallas_call(kernel, grid=(grid,), in_specs=in_specs, out_specs=out_spe...  66.5 us
    all_to_all x2, starting transfers between devices, to_all(): lax.all_to_all(x, ('orb', 'fit'), split_axis=0, concat_axis=0, tiled=True)  19.8 us
    ppermute x7, waiting for transfers between devices, on_device(): lax.ppermute(wanted, 'orb', [(n, n + ((n // stride + k) % count - n // st...  19.7 us
    all_to_all x2, starting transfers between devices, to_orb(): return lax.all_to_all(x, 'orb', split_axis=0, concat_axis=0, tiled=True)  15.5 us
    ppermute x12, starting transfers between devices, shift(): return lax.ppermute(x, 'fit', [(n, (n + k) % fits) for n in range(fits)])  15.1 us
    all_to_all x2, waiting for transfers between devices, to_orb(): return lax.all_to_all(x, 'orb', split_axis=0, concat_axis=0, tiled=True)  13.3 us
    ppermute x7, starting transfers between devices, on_device(): lax.ppermute(wanted, 'orb', [(n, n + ((n // stride + k) % count - n // st...  7.93 us
  transfers between devices with their start and end apart: 23, of which 16 were waited for; matrix products, arithmetic and copies ran while one was open for 5% of the time, Pallas kernels for 8%

profile of v5, /device:TPU:1, one launch (start us, length us, event | category | flops | bytes accessed | tf_op | source)
XLA Modules:
  0.0 295.4 jit_solution(5921653595341111563)
XLA Ops:
  0.8 1.6 copy-done.2
  2.4 1.8 pack_blocks.1
  4.2 1.3 copy-done.4
  5.5 12.0 %all-to-all-start = ((bf16[128,4,16,128]{3,2,1,0:T(8,128)(2,1)}), bf16[128,4,16,128]{3,2,1,0:T(8,128)(2,1)}, u32[]{:S(2)}, u32[]{:S(2)}) async-start(bf16[128,4,16,128]{3,2,1,0:T(8,128)(2,1)} %copy-done.4), calls=%async_computation | async-start | bytes 4194304 | tf_op jit(solution)/shard_map/all_to_all | solution.py:404
  17.5 1.0 fusion.10
  18.5 3.3 %collective-permute-start.8 = (bf16[1,512,512]{2,1,0:T(8,128)(2,1)}, bf16[1,512,512]{2,1,0:T(8,128)(2,1)S(1)}, u32[]{:S(2)}, u32[]{:S(2)}) collective-permute-start(bf16[1,512,512]{2,1,0:T(8,128)(2,1)} %get-tuple-element.26), channel_id=1, source_target_pairs={{0,3},{1,0},{2,1},{3,2},{4,7},{5,4},{6,5},{7,6},{8,11},{9,8},{10,9... | collective-permute-start | bytes 1572872 | tf_op jit(solution)/shard_map/ppermute | solution.py:398
  21.8 0.1 slice.29
  21.9 0.7 collective-permute-start
  22.6 0.8 collective-permute-done
  23.5 2.4 collective-permute-start.3
  25.9 0.5 collective-permute-start.2
  26.4 0.6 collective-permute-start.1
  27.0 14.0 %collective-permute-done.3 = s32[2,128]{1,0:T(2,128)S(1)} collective-permute-done((s32[2,128]{1,0:T(2,128)S(1)}, s32[2,128]{1,0:T(2,128)S(1)}, u32[]{:S(2)}, u32[]{:S(2)}) %collective-permute-start.3) | collective-permute-done | bytes 1056 | tf_op jit(solution)/shard_map/ppermute | solution.py:416
  41.1 1.5 collective-permute-done.2
  42.6 2.5 collective-permute-start.6
  45.2 0.5 collective-permute-start.5
  45.7 0.6 collective-permute-start.4
  46.3 2.9 collective-permute-done.5
  49.1 0.5 collective-permute-done.4
  49.6 2.4 concatenate.17
  52.0 1.0 collective-permute-done.8.refs_1_.refs_2_
  53.0 1.8 collective-permute-done.7.refs_0_.refs_3_
  54.9 0.8 copy-done.11
  55.7 4.9 %pick_pieces.1 = bf16[32,32,16,128]{3,2,1,0:T(8,128)(2,1)} custom-call(s32[14]{0:T(128)} %copy-done.5, s32[32,8]{1,0:T(8,128)} %bitcast.37, bf16[512,16,128]{2,1,0:T(8,128)(2,1)} %bitcast.13.held_ref, bf16[1,512,512]{2,1,0:T(8,128)(2,1)} %copy-done.11, bf16[1,512,512]{2,1,0:T(8,128)(2,1)} %copy-done.9), custom_call_target="tpu_custom_call" | custom-call | bytes 1024 | tf_op jit(solution)/shard_map/pick_pieces/pallas_call | solution.py:32
  60.6 7.1 %all-to-all-start.1 = ((bf16[32,32,16,128]{3,2,1,0:T(8,128)(2,1)}), bf16[32,32,16,128]{3,2,1,0:T(8,128)(2,1)}, u32[]{:S(2)}, u32[]{:S(2)}) async-start(bf16[32,32,16,128]{3,2,1,0:T(8,128)(2,1)} %pick_pieces.1), calls=%async_computation.1 | async-start | bytes 8388608 | tf_op jit(solution)/shard_map/all_to_all | solution.py:401
  67.7 1.9 fusion.9
  69.7 0.1 collective-permute-start.10
  69.8 2.5 collective-permute-start.9
  72.4 0.6 gather_fusion.5
  73.0 0.6 gather_fusion.1
  73.7 0.6 gather_fusion.3
  74.4 0.6 gather_fusion.4
  74.9 0.5 fusion.8
  75.6 0.5 broadcast_select_fusion.1.nright_ref
  76.1 0.1 fusion
  76.2 0.1 collective-permute-start.14
  76.3 1.4 collective-permute-start.11
  77.7 29.2 %collective-permute-done.10.refs_4_ = bf16[3,512,512]{2,1,0:T(8,128)(2,1)S(1)} collective-permute-done((bf16[3,512,512]{2,1,0:T(8,128)(2,1)}, bf16[3,512,512]{2,1,0:T(8,128)(2,1)S(1)}, u32[]{:S(2)}, u32[]{:S(2)}) %collective-permute-start.10) | collective-permute-done | bytes 1572896 | tf_op jit(solution)/shard_map/ppermute | solution.py:398
  107.0 2.3 slice.51
  109.3 2.3 collective-permute-start.13
  111.6 0.6 gather_fusion.2
  112.1 0.7 gather_fusion
  112.8 0.7 reshape.214.high_ref
  113.5 0.4 copy.10
  113.8 0.6 bitcast_select_fusion.nleft_ref
  114.4 1.1 select_subtract_fusion.low_ref
  115.5 1.4 collective-permute-done.14.refs_8_
  117.0 1.2 collective-permute-done.11.refs_5_
  118.1 11.2 %collective-permute-done.12.refs_6_ = bf16[1,512,512]{2,1,0:T(8,128)(2,1)} collective-permute-done((bf16[1,512,512]{2,1,0:T(8,128)(2,1)S(1)}, bf16[1,512,512]{2,1,0:T(8,128)(2,1)}, u32[]{:S(2)}, u32[]{:S(2)}) %collective-permute-start.12) | collective-permute-done | bytes 524320 | tf_op jit(solution)/shard_map/ppermute | solution.py:398
  129.4 28.9 %pair_terms.1 = (bf16[32,32,16,128]{3,2,1,0:T(8,128)(2,1)}, bf16[4,512,1024]{2,1,0:T(8,128)(2,1)}, bf16[8,128,2048]{2,1,0:T(8,128)(2,1)}, bf16[2,512,640]{2,1,0:T(8,128)(2,1)}, bf16[2,512,640]{2,1,0:T(8,128)(2,1)}) custom-call(s32[14]{0:T(128)} %copy-done.5, s32[16]{0:T(128)} %get-tuple-element.29.left_ref, s32[16]{0:T(128)} %bitcast_select_fusion.nleft_ref, ...), custom_call_target="tpu_custom_call" | custom-call | bytes 1024 | tf_op jit(solution)/shard_map/pair_terms/pallas_call | solution.py:32
  158.3 8.4 %all-to-all-start.2 = ((bf16[32,32,16,128]{3,2,1,0:T(8,128)(2,1)}), bf16[32,32,16,128]{3,2,1,0:T(8,128)(2,1)}, u32[]{:S(2)}, u32[]{:S(2)}) async-start(bf16[32,32,16,128]{3,2,1,0:T(8,128)(2,1)} %get-tuple-element.21), calls=%async_computation.2 | async-start | bytes 8388608 | tf_op jit(solution)/shard_map/all_to_all | solution.py:401
  166.8 2.7 collective-permute-start.16
  169.5 14.2 %near_terms.1 = (bf16[4,512,640]{2,1,0:T(8,128)(2,1)}, bf16[4,512,640]{2,1,0:T(8,128)(2,1)}, bf16[4,512,640]{2,1,0:T(8,128)(2,1)}) custom-call(s32[14]{0:T(128)} %copy-done.5, bf16[4,512,1024]{2,1,0:T(8,128)(2,1)} %get-tuple-element.12.all_ref, bf16[8,128,2048]{2,1,0:T(8,128)(2,1)} %get-tuple-element.13.rows_ref), custom_call_target="tpu_custom_call" | custom-call | bytes 1024 | tf_op jit(solution)/shard_map/near_terms/pallas_call | solution.py:32
  183.7 14.4 %collective-permute-done.15.c_ref = bf16[2,512,640]{2,1,0:T(8,128)(2,1)S(1)} collective-permute-done((bf16[2,512,640]{2,1,0:T(8,128)(2,1)S(1)}, bf16[2,512,640]{2,1,0:T(8,128)(2,1)S(1)}, u32[]{:S(2)}, u32[]{:S(2)}) %collective-permute-start.15) | collective-permute-done | bytes 1310752 | tf_op jit(solution)/shard_map/ppermute | solution.py:398
  198.1 3.0 %merge.1 = (bf16[4,512,640]{2,1,0:T(8,128)(2,1)}, bf16[4,512,640]{2,1,0:T(8,128)(2,1)}) custom-call(bf16[4,512,640]{2,1,0:T(8,128)(2,1)} %get-tuple-element.15.a_ref, bf16[4,512,640]{2,1,0:T(8,128)(2,1)} %get-tuple-element.16.b_ref, bf16[2,512,640]{2,1,0:T(8,128)(2,1)S(1)} %collective-permute-done.15.c_ref, ...), custom_call_target="tpu_custom_call", output_to_operand_aliasing={{0}: (0, {}), {1}: (1, {})} | custom-call | bytes 1024 | tf_op jit(solution)/shard_map/merge/pallas_call | solution.py:32
  201.1 2.5 collective-permute-start.18
  203.7 13.3 %all-to-all-done.2.part_ref = bf16[32,32,16,128]{3,2,1,0:T(8,128)(2,1)} async-done(((bf16[32,32,16,128]{3,2,1,0:T(8,128)(2,1)}), bf16[32,32,16,128]{3,2,1,0:T(8,128)(2,1)}, u32[]{:S(2)}, u32[]{:S(2)}) %all-to-all-start.2) | async-done | bytes 4194336 | tf_op jit(solution)/shard_map/all_to_all | solution.py:401
  216.9 6.0 %sum_returned.1 = bf16[128,4,16,128]{3,2,1,0:T(8,128)(2,1)} custom-call(s32[14]{0:T(128)} %copy-done.5, s32[32,8]{1,0:T(8,128)} %bitcast.38, bf16[32,32,16,128]{3,2,1,0:T(8,128)(2,1)} %all-to-all-done.2.part_ref, bf16[4,512,640]{2,1,0:T(8,128)(2,1)} %get-tuple-element.19.refs_0_), custom_call_target="tpu_custom_call" | custom-call | bytes 1024 | tf_op jit(solution)/shard_map/sum_returned/pallas_call | solution.py:32
  222.9 7.9 %all-to-all-start.3 = ((bf16[128,4,16,128]{3,2,1,0:T(8,128)(2,1)}), bf16[128,4,16,128]{3,2,1,0:T(8,128)(2,1)S(1)}, u32[]{:S(2)}, u32[]{:S(2)}) async-start(bf16[128,4,16,128]{3,2,1,0:T(8,128)(2,1)} %sum_returned.1), calls=%async_computation.3 | async-start | bytes 4194304 | tf_op jit(solution)/shard_map/all_to_all | solution.py:404
  230.8 49.2 %collective-permute-done.18.above_ref = bf16[4,512,640]{2,1,0:T(8,128)(2,1)} collective-permute-done((bf16[4,512,640]{2,1,0:T(8,128)(2,1)}, bf16[4,512,640]{2,1,0:T(8,128)(2,1)}, u32[]{:S(2)}, u32[]{:S(2)}) %collective-permute-start.18) | collective-permute-done | bytes 2621472 | tf_op jit(solution)/shard_map/ppermute | solution.py:398
  280.0 3.4 %collective-permute-done.17.below_ref = bf16[4,512,640]{2,1,0:T(8,128)(2,1)} collective-permute-done((bf16[4,512,640]{2,1,0:T(8,128)(2,1)}, bf16[4,512,640]{2,1,0:T(8,128)(2,1)}, u32[]{:S(2)}, u32[]{:S(2)}) %collective-permute-start.17) | collective-permute-done | bytes 2621472 | tf_op jit(solution)/shard_map/ppermute | solution.py:398
  283.4 2.8 all-to-all-done.3.sums_ref
  286.3 1.3 copy-done.7
  287.6 7.6 %add_all.1 = (f32[4,512,512]{2,1,0:T(8,128)}, f32[4,512,128]{2,1,0:T(8,128)}) custom-call(s32[14]{0:T(128)} %copy-done.5, bf16[4,512,640]{2,1,0:T(8,128)(2,1)} %get-tuple-element.14.own_ref, bf16[4,512,640]{2,1,0:T(8,128)(2,1)} %collective-permute-done.17.below_ref, bf16[4,512,640]{2,1,0:T(8,128)(2,1)} %collective-permute-done.18.above_ref, ...), custom_call_target="tpu_custom_call" | custom-call | bytes 1024 | tf_op jit(solution)/shard_map/add_all/pallas_call | solution.py:32
  (59 shorter events, 0.6 us)
Async XLA Ops:
  0.6 73.7 %copy-start = (f32[128,512]{1,0:T(8,128)S(1)}, f32[128,512]{1,0:T(8,128)}, u32[]{:S(2)}) copy-start(f32[128,512]{1,0:T(8,128)} %param.7) | copy-start | bytes 786436
  0.8 1.6 copy-start.2
  2.4 1.8 copy-start.5
  4.2 1.3 copy-start.4
  5.5 12.0 %copy-start.3 = (bf16[4,512,512]{2,1,0:T(8,128)(2,1)S(1)}, bf16[4,512,512]{2,1,0:T(8,128)(2,1)}, u32[]{:S(2)}) copy-start(bf16[4,512,512]{2,1,0:T(8,128)(2,1)} %refs_0_.1) | copy-start | bytes 6291460
  5.5 49.4 %all-to-all-start = ((bf16[128,4,16,128]{3,2,1,0:T(8,128)(2,1)}), bf16[128,4,16,128]{3,2,1,0:T(8,128)(2,1)}, u32[]{:S(2)}, u32[]{:S(2)}) async-start(bf16[128,4,16,128]{3,2,1,0:T(8,128)(2,1)} %copy-done.4), calls=%async_computation | async-start | bytes 4194304 | tf_op jit(solution)/shard_map/all_to_all | solution.py:404
  17.5 4.3 %copy-start.13 = (s32[16,2]{0,1:T(2,128)S(1)}, s32[16,2]{0,1:T(2,128)}, u32[]{:S(2)}) copy-start(s32[16,2]{0,1:T(2,128)} %param.9) | copy-start | bytes 388
  18.5 34.5 %collective-permute-start.8 = (bf16[1,512,512]{2,1,0:T(8,128)(2,1)}, bf16[1,512,512]{2,1,0:T(8,128)(2,1)S(1)}, u32[]{:S(2)}, u32[]{:S(2)}) collective-permute-start(bf16[1,512,512]{2,1,0:T(8,128)(2,1)} %get-tuple-element.26), channel_id=1, source_target_pairs={{0,3},{1,0},{2,1},{3,2},{4,7},{5,4},{6,5},{7,6},{8,11},{9,8},{10,9... | collective-permute-start | bytes 1572872 | tf_op jit(solution)/shard_map/ppermute | solution.py:398
  21.8 33.1 %collective-permute-start.7 = (bf16[1,512,512]{2,1,0:T(8,128)(2,1)}, bf16[1,512,512]{2,1,0:T(8,128)(2,1)S(1)}, u32[]{:S(2)}, u32[]{:S(2)}) collective-permute-start(bf16[1,512,512]{2,1,0:T(8,128)(2,1)} %get-tuple-element.27), channel_id=1, source_target_pairs={{0,1},{1,2},{2,3},{3,0},{4,5},{5,6},{6,7},{7,4},{8,9},{9,10},{10,1... | collective-permute-start | bytes 1572872 | tf_op jit(solution)/shard_map/ppermute | solution.py:398
  21.9 1.5 collective-permute-start
  23.5 17.6 %collective-permute-start.3 = (s32[2,128]{1,0:T(2,128)S(1)}, s32[2,128]{1,0:T(2,128)S(1)}, u32[]{:S(2)}, u32[]{:S(2)}) collective-permute-start(s32[2,128]{1,0:T(2,128)S(1)} %pad_add_fusion), channel_id=1, source_target_pairs={{0,24},{4,28},{8,0},{12,4},{16,8},{20,12},{24,16},{28,20},{32,56},... | collective-permute-start | bytes 3080 | tf_op jit(solution)/shard_map/ppermute | solution.py:416
  25.9 16.7 %collective-permute-start.2 = (s32[2,128]{1,0:T(2,128)S(1)}, s32[2,128]{1,0:T(2,128)S(1)}, u32[]{:S(2)}, u32[]{:S(2)}) collective-permute-start(s32[2,128]{1,0:T(2,128)S(1)} %pad_add_fusion), channel_id=1, source_target_pairs={{0,16},{4,20},{8,24},{12,28},{16,0},{20,4},{24,8},{28,12},{32,48},... | collective-permute-start | bytes 3080 | tf_op jit(solution)/shard_map/ppermute | solution.py:416
  26.4 16.1 %collective-permute-start.1 = (s32[2,128]{1,0:T(2,128)S(1)}, s32[2,128]{1,0:T(2,128)S(1)}, u32[]{:S(2)}, u32[]{:S(2)}) collective-permute-start(s32[2,128]{1,0:T(2,128)S(1)} %pad_add_fusion), channel_id=1, source_target_pairs={{0,8},{4,12},{8,16},{12,20},{16,24},{20,28},{24,0},{28,4},{32,40},... | collective-permute-start | bytes 3080 | tf_op jit(solution)/shard_map/ppermute | solution.py:416
  42.6 3.6 %collective-permute-start.6 = (s32[8,128]{1,0:T(8,128)S(1)}, s32[8,128]{1,0:T(8,128)S(1)}, u32[]{:S(2)}, u32[]{:S(2)}) collective-permute-start(s32[8,128]{1,0:T(8,128)S(1)} %concatenate.16), channel_id=1, source_target_pairs={{0,96},{4,100},{8,104},{12,108},{16,112},{20,116},{24,120},{28,124... | collective-permute-start | bytes 12296 | tf_op jit(solution)/shard_map/ppermute | solution.py:416
  45.2 4.0 %collective-permute-start.5 = (s32[8,128]{1,0:T(8,128)S(1)}, s32[8,128]{1,0:T(8,128)S(1)}, u32[]{:S(2)}, u32[]{:S(2)}) collective-permute-start(s32[8,128]{1,0:T(8,128)S(1)} %concatenate.16), channel_id=1, source_target_pairs={{0,64},{4,68},{8,72},{12,76},{16,80},{20,84},{24,88},{28,92},{32,9... | collective-permute-start | bytes 12296 | tf_op jit(solution)/shard_map/ppermute | solution.py:416
  45.7 4.0 %collective-permute-start.4 = (s32[8,128]{1,0:T(8,128)S(1)}, s32[8,128]{1,0:T(8,128)S(1)}, u32[]{:S(2)}, u32[]{:S(2)}) collective-permute-start(s32[8,128]{1,0:T(8,128)S(1)} %concatenate.16), channel_id=1, source_target_pairs={{0,32},{4,36},{8,40},{12,44},{16,48},{20,52},{24,56},{28,60},{32,6... | collective-permute-start | bytes 12296 | tf_op jit(solution)/shard_map/ppermute | solution.py:416
  53.0 1.9 copy-start.9
  54.9 0.8 copy-start.11
  60.6 68.8 %all-to-all-start.1 = ((bf16[32,32,16,128]{3,2,1,0:T(8,128)(2,1)}), bf16[32,32,16,128]{3,2,1,0:T(8,128)(2,1)}, u32[]{:S(2)}, u32[]{:S(2)}) async-start(bf16[32,32,16,128]{3,2,1,0:T(8,128)(2,1)} %pick_pieces.1), calls=%async_computation.1 | async-start | bytes 8388608 | tf_op jit(solution)/shard_map/all_to_all | solution.py:401
  67.7 4.7 %copy-start.16 = (s32[128]{0:T(128)S(1)}, s32[128]{0:T(128)}, u32[]{:S(2)}) copy-start(s32[128]{0:T(128)} %param.8) | copy-start | bytes 1540
  67.7 4.7 %copy-start.6 = (f32[128]{0:T(128)S(1)}, f32[128]{0:T(128)}, u32[]{:S(2)}) copy-start(f32[128]{0:T(128)} %param.6) | copy-start | bytes 1540
  67.7 8.4 %copy-start.10 = (bf16[1,512,512]{2,1,0:T(8,128)(2,1)S(1)}, bf16[1,512,512]{2,1,0:T(8,128)(2,1)}, u32[]{:S(2)}) copy-start(bf16[1,512,512]{2,1,0:T(8,128)(2,1)} %copy-done.9) | copy-start | bytes 1572868
  67.7 8.5 %copy-start.12 = (bf16[1,512,512]{2,1,0:T(8,128)(2,1)S(1)}, bf16[1,512,512]{2,1,0:T(8,128)(2,1)}, u32[]{:S(2)}) copy-start(bf16[1,512,512]{2,1,0:T(8,128)(2,1)} %copy-done.11) | copy-start | bytes 1572868
  69.7 37.2 %collective-permute-start.10 = (bf16[3,512,512]{2,1,0:T(8,128)(2,1)}, bf16[3,512,512]{2,1,0:T(8,128)(2,1)S(1)}, u32[]{:S(2)}, u32[]{:S(2)}) collective-permute-start(bf16[3,512,512]{2,1,0:T(8,128)(2,1)} %get-tuple-element.24), channel_id=1, source_target_pairs={{0,1},{1,2},{2,3},{3,0},{4,5},{5,6},{6,7},{7,4},{8,9},{9,10},{10,1... | collective-permute-start | bytes 4718600 | tf_op jit(solution)/shard_map/ppermute | solution.py:398
  69.8 37.2 %collective-permute-start.9 = (bf16[3,512,512]{2,1,0:T(8,128)(2,1)}, bf16[3,512,512]{2,1,0:T(8,128)(2,1)}, u32[]{:S(2)}, u32[]{:S(2)}) collective-permute-start(bf16[3,512,512]{2,1,0:T(8,128)(2,1)} %get-tuple-element.25), channel_id=1, source_target_pairs={{0,3},{1,0},{2,1},{3,2},{4,7},{5,4},{6,5},{7,6},{8,11},{9,8},{10,9... | collective-permute-start | bytes 4718600 | tf_op jit(solution)/shard_map/ppermute | solution.py:398
  76.2 40.8 %collective-permute-start.14 = (bf16[1,512,512]{2,1,0:T(8,128)(2,1)S(1)}, bf16[1,512,512]{2,1,0:T(8,128)(2,1)}, u32[]{:S(2)}, u32[]{:S(2)}) collective-permute-start(bf16[1,512,512]{2,1,0:T(8,128)(2,1)S(1)} %copy-done.10), channel_id=1, source_target_pairs={{0,3},{1,0},{2,1},{3,2},{4,7},{5,4},{6,5},{7,6},{8,11},{9,8},{10,9... | collective-permute-start | bytes 1572872 | tf_op jit(solution)/shard_map/ppermute | solution.py:398
  76.3 41.8 %collective-permute-start.11 = (bf16[1,512,512]{2,1,0:T(8,128)(2,1)S(1)}, bf16[1,512,512]{2,1,0:T(8,128)(2,1)}, u32[]{:S(2)}, u32[]{:S(2)}) collective-permute-start(bf16[1,512,512]{2,1,0:T(8,128)(2,1)S(1)} %copy-done.12), channel_id=1, source_target_pairs={{0,1},{1,2},{2,3},{3,0},{4,5},{5,6},{6,7},{7,4},{8,9},{9,10},{10,1... | collective-permute-start | bytes 1572872 | tf_op jit(solution)/shard_map/ppermute | solution.py:398
  106.9 6.6 %copy-start.8 = (bf16[3,512,512]{2,1,0:T(8,128)(2,1)}, bf16[3,512,512]{2,1,0:T(8,128)(2,1)S(1)}, u32[]{:S(2)}) copy-start(bf16[3,512,512]{2,1,0:T(8,128)(2,1)S(1)} %collective-permute-done.10.refs_4_) | copy-start | bytes 4718596
  106.9 22.4 %collective-permute-start.12 = (bf16[1,512,512]{2,1,0:T(8,128)(2,1)S(1)}, bf16[1,512,512]{2,1,0:T(8,128)(2,1)}, u32[]{:S(2)}, u32[]{:S(2)}) collective-permute-start(bf16[1,512,512]{2,1,0:T(8,128)(2,1)S(1)} %slice.50), channel_id=1, source_target_pairs={{0,1},{1,2},{2,3},{3,0},{4,5},{5,6},{6,7},{7,4},{8,9},{9,10},{10,1... | collective-permute-start | bytes 1572872 | tf_op jit(solution)/shard_map/ppermute | solution.py:398
  109.3 20.1 %collective-permute-start.13 = (bf16[1,512,512]{2,1,0:T(8,128)(2,1)}, bf16[1,512,512]{2,1,0:T(8,128)(2,1)}, u32[]{:S(2)}, u32[]{:S(2)}) collective-permute-start(bf16[1,512,512]{2,1,0:T(8,128)(2,1)} %slice.51), channel_id=1, source_target_pairs={{0,3},{1,0},{2,1},{3,2},{4,7},{5,4},{6,5},{7,6},{8,11},{9,8},{10,9... | collective-permute-start | bytes 1572872 | tf_op jit(solution)/shard_map/ppermute | solution.py:398
  158.3 8.4 %copy-start.15 = (bf16[2,512,640]{2,1,0:T(8,128)(2,1)S(1)}, bf16[2,512,640]{2,1,0:T(8,128)(2,1)}, u32[]{:S(2)}) copy-start(bf16[2,512,640]{2,1,0:T(8,128)(2,1)} %get-tuple-element.17) | copy-start | bytes 3932164
  158.3 8.5 %copy-start.14 = (bf16[2,512,640]{2,1,0:T(8,128)(2,1)S(1)}, bf16[2,512,640]{2,1,0:T(8,128)(2,1)}, u32[]{:S(2)}) copy-start(bf16[2,512,640]{2,1,0:T(8,128)(2,1)} %get-tuple-element.18) | copy-start | bytes 3932164
  158.3 58.6 %all-to-all-start.2 = ((bf16[32,32,16,128]{3,2,1,0:T(8,128)(2,1)}), bf16[32,32,16,128]{3,2,1,0:T(8,128)(2,1)}, u32[]{:S(2)}, u32[]{:S(2)}) async-start(bf16[32,32,16,128]{3,2,1,0:T(8,128)(2,1)} %get-tuple-element.21), calls=%async_computation.2 | async-start | bytes 8388608 | tf_op jit(solution)/shard_map/all_to_all | solution.py:401
  166.7 31.4 %collective-permute-start.15 = (bf16[2,512,640]{2,1,0:T(8,128)(2,1)S(1)}, bf16[2,512,640]{2,1,0:T(8,128)(2,1)S(1)}, u32[]{:S(2)}, u32[]{:S(2)}) collective-permute-start(bf16[2,512,640]{2,1,0:T(8,128)(2,1)S(1)} %copy-done.15), channel_id=1, source_target_pairs={{0,1},{1,2},{2,3},{3,0},{4,5},{5,6},{6,7},{7,4},{8,9},{9,10},{10,1... | collective-permute-start | bytes 3932168 | tf_op jit(solution)/shard_map/ppermute | solution.py:398
  166.8 31.4 %collective-permute-start.16 = (bf16[2,512,640]{2,1,0:T(8,128)(2,1)S(1)}, bf16[2,512,640]{2,1,0:T(8,128)(2,1)S(1)}, u32[]{:S(2)}, u32[]{:S(2)}) collective-permute-start(bf16[2,512,640]{2,1,0:T(8,128)(2,1)S(1)} %copy-done.14), channel_id=1, source_target_pairs={{0,3},{1,0},{2,1},{3,2},{4,7},{5,4},{6,5},{7,6},{8,11},{9,8},{10,9... | collective-permute-start | bytes 3932168 | tf_op jit(solution)/shard_map/ppermute | solution.py:398
  201.1 78.8 %collective-permute-start.18 = (bf16[4,512,640]{2,1,0:T(8,128)(2,1)}, bf16[4,512,640]{2,1,0:T(8,128)(2,1)}, u32[]{:S(2)}, u32[]{:S(2)}) collective-permute-start(bf16[4,512,640]{2,1,0:T(8,128)(2,1)} %get-tuple-element.20), channel_id=1, source_target_pairs={{0,3},{1,0},{2,1},{3,2},{4,7},{5,4},{6,5},{7,6},{8,11},{9,8},{10,9... | collective-permute-start | bytes 7864328 | tf_op jit(solution)/shard_map/ppermute | solution.py:398
  203.7 79.8 %collective-permute-start.17 = (bf16[4,512,640]{2,1,0:T(8,128)(2,1)}, bf16[4,512,640]{2,1,0:T(8,128)(2,1)}, u32[]{:S(2)}, u32[]{:S(2)}) collective-permute-start(bf16[4,512,640]{2,1,0:T(8,128)(2,1)} %get-tuple-element.19.refs_0_), channel_id=1, source_target_pairs={{0,1},{1,2},{2,3},{3,0},{4,5},{5,6},{6,7},{7,4},{8,9},{9,10},{10,1... | collective-permute-start | bytes 7864328 | tf_op jit(solution)/shard_map/ppermute | solution.py:398
  222.9 63.3 %all-to-all-start.3 = ((bf16[128,4,16,128]{3,2,1,0:T(8,128)(2,1)}), bf16[128,4,16,128]{3,2,1,0:T(8,128)(2,1)S(1)}, u32[]{:S(2)}, u32[]{:S(2)}) async-start(bf16[128,4,16,128]{3,2,1,0:T(8,128)(2,1)} %sum_returned.1), calls=%async_computation.3 | async-start | bytes 4194304 | tf_op jit(solution)/shard_map/all_to_all | solution.py:404
  286.3 1.3 copy-start.7
  287.6 7.6 %copy-start.1 = (f32[128,512]{1,0:T(8,128)S(1)}, f32[128,512]{1,0:T(8,128)}, u32[]{:S(2)}) copy-start(f32[128,512]{1,0:T(8,128)} %param.7) | copy-start | bytes 786436

commit v6 on v5

--- a/solution.py
+++ b/solution.py
@@ -432,10 +432,12 @@
     ).reshape(groups, 1, virt // fits)
 
     pieces = to_orb(pick_pieces(place, wanted, held, fits, after=[last0, next3]))
-    last, next_ = shift(blocks[1:], 1), shift(blocks[:-1], fits - 1)
+    last1, next2 = shift(one[1], 1), shift(one[2], fits - 1)
+    last2, next0 = shift(blocks[2:], 1), shift(blocks[:2], fits - 1)
     far0, far3 = shift(last0, 1), shift(next3, fits - 1)
-    far1, far2 = shift(last[:1], 1), shift(next_[-1:], fits - 1)
-    lefts = [(blocks, 0, 0), (next_, 1, 0), (next3, 1, orbs - 1), (last0, 3, 0), (last, 3, 1)]
+    far1, far2 = shift(last1, 1), shift(next2, fits - 1)
+    lefts = [(blocks, 0, 0), (next0, 1, 0), (next2, 1, 2), (next3, 1, 3)]
+    lefts += [(last0, 3, 0), (last1, 3, 1), (last2, 3, 2)]
     lefts += [(far0, 2, 0), (far1, 2, 1), (far2, 2, 2), (far3, 2, 3)]
     back, amps, rows, *far = pair_terms(place, plan, left_levels, right_levels, pieces, lefts, fits)
     far = [shift(far[0], 1), shift(far[1], fits - 1)]

time: 296 us -> 297 us (level)
    ppermute x12 -> x14, starting transfers between devices: 15.1 us -> 16.5 us  [shift(): return lax.ppermute(x, 'fit', [(n, (n + k) % fits) for n in range(fits)])]
    unnamed x34 -> x36, local copies, waits for them, and re-layouts: 5.06 us -> 6.03 us
    ppermute x12 -> x14, waiting for transfers between devices: 113 us -> 114 us  [shift(): return lax.ppermute(x, 'fit', [(n, (n + k) % fits) for n in range(fits)])]
  transfers between devices with their start and end apart: 23 -> 25, of which waited for: 16 -> 15; matrix products, arithmetic and copies ran while one was open for 5% -> 4% of each run, Pallas kernels for 8% -> 8%
where the time goes in v6:
time: 297 us; the launch traced here: 296 us
  waiting for transfers between devices  149 us (50%)
  Pallas kernels  66.4 us (22%)
  starting transfers between devices  60.2 us (20%)
  local copies, waits for them, and re-layouts  16.2 us (5%)
  other arithmetic  3.01 us (1%)
    ppermute x14, waiting for transfers between devices, shift(): return lax.ppermute(x, 'fit', [(n, (n + k) % fits) for n in range(fits)])  114 us
    pallas_call x7, Pallas kernels, call(): pl.pallas_call(kernel, grid=(grid,), in_specs=in_specs, out_specs=out_spe...  66.4 us
    ppermute x7, waiting for transfers between devices, on_device(): lax.ppermute(wanted, 'orb', [(n, n + ((n // stride + k) % count - n // st...  19.4 us
    all_to_all x2, starting transfers between devices, to_all(): lax.all_to_all(x, ('orb', 'fit'), split_axis=0, concat_axis=0, tiled=True)  18.9 us
    all_to_all x2, starting transfers between devices, to_orb(): return lax.all_to_all(x, 'orb', split_axis=0, concat_axis=0, tiled=True)  16.9 us
    ppermute x14, starting transfers between devices, shift(): return lax.ppermute(x, 'fit', [(n, (n + k) % fits) for n in range(fits)])  16.5 us
    all_to_all x2, waiting for transfers between devices, to_orb(): return lax.all_to_all(x, 'orb', split_axis=0, concat_axis=0, tiled=True)  13.4 us
    ppermute x7, starting transfers between devices, on_device(): lax.ppermute(wanted, 'orb', [(n, n + ((n // stride + k) % count - n // st...  7.93 us
  transfers between devices with their start and end apart: 25, of which 15 were waited for; matrix products, arithmetic and copies ran while one was open for 4% of the time, Pallas kernels for 8%

profile of v6, /device:TPU:1, one launch (start us, length us, event | category | flops | bytes accessed | tf_op | source)
XLA Modules:
  0.0 296.3 jit_solution(2183614741949987272)
XLA Ops:
  0.7 0.1 concatenate.14.place_ref
  0.8 1.6 copy-done.2
  2.4 1.8 pack_blocks.1
  4.2 1.3 copy-done.4
  5.5 12.0 %all-to-all-start = ((bf16[128,4,16,128]{3,2,1,0:T(8,128)(2,1)}), bf16[128,4,16,128]{3,2,1,0:T(8,128)(2,1)}, u32[]{:S(2)}, u32[]{:S(2)}) async-start(bf16[128,4,16,128]{3,2,1,0:T(8,128)(2,1)} %copy-done.4), calls=%async_computation | async-start | bytes 4194304 | tf_op jit(solution)/shard_map/all_to_all | solution.py:404
  17.5 1.3 fusion.10
  18.8 3.3 %collective-permute-start.8 = (bf16[1,512,512]{2,1,0:T(8,128)(2,1)}, bf16[1,512,512]{2,1,0:T(8,128)(2,1)S(1)}, u32[]{:S(2)}, u32[]{:S(2)}) collective-permute-start(bf16[1,512,512]{2,1,0:T(8,128)(2,1)} %get-tuple-element.28), channel_id=1, source_target_pairs={{0,3},{1,0},{2,1},{3,2},{4,7},{5,4},{6,5},{7,6},{8,11},{9,8},{10,9... | collective-permute-start | bytes 1572872 | tf_op jit(solution)/shard_map/ppermute | solution.py:398
  22.1 0.1 slice.29
  22.2 0.7 collective-permute-start
  22.9 0.8 collective-permute-done
  23.8 2.4 collective-permute-start.3
  26.2 0.5 collective-permute-start.2
  26.8 0.6 collective-permute-start.1
  27.4 13.7 %collective-permute-done.3 = s32[2,128]{1,0:T(2,128)S(1)} collective-permute-done((s32[2,128]{1,0:T(2,128)S(1)}, s32[2,128]{1,0:T(2,128)S(1)}, u32[]{:S(2)}, u32[]{:S(2)}) %collective-permute-start.3) | collective-permute-done | bytes 1056 | tf_op jit(solution)/shard_map/ppermute | solution.py:416
  41.1 1.5 collective-permute-done.2
  42.6 2.5 collective-permute-start.6
  45.2 0.5 collective-permute-start.5
  45.7 0.6 collective-permute-start.4
  46.2 2.9 collective-permute-done.5
  49.1 0.5 collective-permute-done.4
  49.6 2.4 concatenate.17
  52.0 1.1 collective-permute-done.8.refs_1_.refs_3_
  53.1 2.0 collective-permute-done.7.refs_0_.refs_4_
  55.1 0.8 copy-done.10
  55.9 4.9 %pick_pieces.1 = bf16[32,32,16,128]{3,2,1,0:T(8,128)(2,1)} custom-call(s32[14]{0:T(128)} %copy-done.5, s32[32,8]{1,0:T(8,128)} %bitcast.37, bf16[512,16,128]{2,1,0:T(8,128)(2,1)} %bitcast.13.held_ref, bf16[1,512,512]{2,1,0:T(8,128)(2,1)} %copy-done.10, bf16[1,512,512]{2,1,0:T(8,128)(2,1)} %copy-done.8), custom_call_target="tpu_custom_call" | custom-call | bytes 1024 | tf_op jit(solution)/shard_map/pick_pieces/pallas_call | solution.py:32
  60.8 6.9 %all-to-all-start.1 = ((bf16[32,32,16,128]{3,2,1,0:T(8,128)(2,1)}), bf16[32,32,16,128]{3,2,1,0:T(8,128)(2,1)}, u32[]{:S(2)}, u32[]{:S(2)}) async-start(bf16[32,32,16,128]{3,2,1,0:T(8,128)(2,1)} %pick_pieces.1), calls=%async_computation.1 | async-start | bytes 8388608 | tf_op jit(solution)/shard_map/all_to_all | solution.py:401
  67.7 0.2 collective-permute-start.11
  67.9 2.6 collective-permute-start.10
  70.5 1.5 fusion.9
  71.9 2.7 collective-permute-start.9
  74.6 0.6 gather_fusion.5
  75.3 0.6 gather_fusion.1
  76.0 0.6 gather_fusion.3
  76.6 0.6 gather_fusion.4
  77.2 0.1 constant_dynamic-slice_fusion
  77.3 0.6 broadcast_select_fusion.1.nright_ref
  77.9 0.5 fusion.8
  78.4 4.2 %collective-permute-done.11.refs_5_ = bf16[1,512,512]{2,1,0:T(8,128)(2,1)} collective-permute-done((bf16[1,512,512]{2,1,0:T(8,128)(2,1)}, bf16[1,512,512]{2,1,0:T(8,128)(2,1)}, u32[]{:S(2)}, u32[]{:S(2)}) %collective-permute-start.11) | collective-permute-done | bytes 524320 | tf_op jit(solution)/shard_map/ppermute | solution.py:398
  82.6 0.1 fusion
  82.7 2.7 collective-permute-start.16
  85.4 30.7 %collective-permute-done.14.refs_8_ = bf16[1,512,512]{2,1,0:T(8,128)(2,1)S(1)} collective-permute-done((bf16[1,512,512]{2,1,0:T(8,128)(2,1)}, bf16[1,512,512]{2,1,0:T(8,128)(2,1)S(1)}, u32[]{:S(2)}, u32[]{:S(2)}) %collective-permute-start.14) | collective-permute-done | bytes 524320 | tf_op jit(solution)/shard_map/ppermute | solution.py:398
  116.1 0.6 gather_fusion.2
  116.7 0.7 gather_fusion
  117.4 0.7 reshape.214.high_ref
  118.0 0.4 copy.10
  118.4 0.6 bitcast_select_fusion.nleft_ref
  119.0 1.1 select_subtract_fusion.low_ref
  120.1 7.9 %collective-permute-done.15.refs_9_ = bf16[1,512,512]{2,1,0:T(8,128)(2,1)} collective-permute-done((bf16[1,512,512]{2,1,0:T(8,128)(2,1)}, bf16[1,512,512]{2,1,0:T(8,128)(2,1)}, u32[]{:S(2)}, u32[]{:S(2)}) %collective-permute-start.15) | collective-permute-done | bytes 524320 | tf_op jit(solution)/shard_map/ppermute | solution.py:398
  128.0 1.0 copy-done.12
  129.0 28.9 %pair_terms.1 = (bf16[32,32,16,128]{3,2,1,0:T(8,128)(2,1)}, bf16[4,512,1024]{2,1,0:T(8,128)(2,1)}, bf16[8,128,2048]{2,1,0:T(8,128)(2,1)}, bf16[2,512,640]{2,1,0:T(8,128)(2,1)}, bf16[2,512,640]{2,1,0:T(8,128)(2,1)}) custom-call(s32[14]{0:T(128)} %copy-done.5, s32[16]{0:T(128)} %get-tuple-element.31.left_ref, s32[16]{0:T(128)} %bitcast_select_fusion.nleft_ref, ...), custom_call_target="tpu_custom_call" | custom-call | bytes 1024 | tf_op jit(solution)/shard_map/pair_terms/pallas_call | solution.py:32
  157.9 10.0 %all-to-all-start.2 = ((bf16[32,32,16,128]{3,2,1,0:T(8,128)(2,1)}), bf16[32,32,16,128]{3,2,1,0:T(8,128)(2,1)}, u32[]{:S(2)}, u32[]{:S(2)}) async-start(bf16[32,32,16,128]{3,2,1,0:T(8,128)(2,1)} %get-tuple-element.21), calls=%async_computation.2 | async-start | bytes 8388608 | tf_op jit(solution)/shard_map/all_to_all | solution.py:401
  168.0 2.7 collective-permute-start.18
  170.6 14.2 %near_terms.1 = (bf16[4,512,640]{2,1,0:T(8,128)(2,1)}, bf16[4,512,640]{2,1,0:T(8,128)(2,1)}, bf16[4,512,640]{2,1,0:T(8,128)(2,1)}) custom-call(s32[14]{0:T(128)} %copy-done.5, bf16[4,512,1024]{2,1,0:T(8,128)(2,1)} %get-tuple-element.12.all_ref, bf16[8,128,2048]{2,1,0:T(8,128)(2,1)} %get-tuple-element.13.rows_ref), custom_call_target="tpu_custom_call" | custom-call | bytes 1024 | tf_op jit(solution)/shard_map/near_terms/pallas_call | solution.py:32
  184.8 14.5 %collective-permute-done.17.c_ref = bf16[2,512,640]{2,1,0:T(8,128)(2,1)S(1)} collective-permute-done((bf16[2,512,640]{2,1,0:T(8,128)(2,1)S(1)}, bf16[2,512,640]{2,1,0:T(8,128)(2,1)S(1)}, u32[]{:S(2)}, u32[]{:S(2)}) %collective-permute-start.17) | collective-permute-done | bytes 1310752 | tf_op jit(solution)/shard_map/ppermute | solution.py:398
  199.3 3.0 %merge.1 = (bf16[4,512,640]{2,1,0:T(8,128)(2,1)}, bf16[4,512,640]{2,1,0:T(8,128)(2,1)}) custom-call(bf16[4,512,640]{2,1,0:T(8,128)(2,1)} %get-tuple-element.15.a_ref, bf16[4,512,640]{2,1,0:T(8,128)(2,1)} %get-tuple-element.16.b_ref, bf16[2,512,640]{2,1,0:T(8,128)(2,1)S(1)} %collective-permute-done.17.c_ref, ...), custom_call_target="tpu_custom_call", output_to_operand_aliasing={{0}: (0, {}), {1}: (1, {})} | custom-call | bytes 1024 | tf_op jit(solution)/shard_map/merge/pallas_call | solution.py:32
  202.3 2.3 collective-permute-start.20
  204.7 13.4 %all-to-all-done.2.part_ref = bf16[32,32,16,128]{3,2,1,0:T(8,128)(2,1)} async-done(((bf16[32,32,16,128]{3,2,1,0:T(8,128)(2,1)}), bf16[32,32,16,128]{3,2,1,0:T(8,128)(2,1)}, u32[]{:S(2)}, u32[]{:S(2)}) %all-to-all-start.2) | async-done | bytes 4194336 | tf_op jit(solution)/shard_map/all_to_all | solution.py:401
  218.2 6.0 %sum_returned.1 = bf16[128,4,16,128]{3,2,1,0:T(8,128)(2,1)} custom-call(s32[14]{0:T(128)} %copy-done.5, s32[32,8]{1,0:T(8,128)} %bitcast.38, bf16[32,32,16,128]{3,2,1,0:T(8,128)(2,1)} %all-to-all-done.2.part_ref, bf16[4,512,640]{2,1,0:T(8,128)(2,1)} %get-tuple-element.19.refs_0_), custom_call_target="tpu_custom_call" | custom-call | bytes 1024 | tf_op jit(solution)/shard_map/sum_returned/pallas_call | solution.py:32
  224.2 7.0 %all-to-all-start.3 = ((bf16[128,4,16,128]{3,2,1,0:T(8,128)(2,1)}), bf16[128,4,16,128]{3,2,1,0:T(8,128)(2,1)S(1)}, u32[]{:S(2)}, u32[]{:S(2)}) async-start(bf16[128,4,16,128]{3,2,1,0:T(8,128)(2,1)} %sum_returned.1), calls=%async_computation.3 | async-start | bytes 4194304 | tf_op jit(solution)/shard_map/all_to_all | solution.py:404
  231.1 49.9 %collective-permute-done.20.above_ref = bf16[4,512,640]{2,1,0:T(8,128)(2,1)} collective-permute-done((bf16[4,512,640]{2,1,0:T(8,128)(2,1)}, bf16[4,512,640]{2,1,0:T(8,128)(2,1)}, u32[]{:S(2)}, u32[]{:S(2)}) %collective-permute-start.20) | collective-permute-done | bytes 2621472 | tf_op jit(solution)/shard_map/ppermute | solution.py:398
  281.1 3.3 %collective-permute-done.19.below_ref = bf16[4,512,640]{2,1,0:T(8,128)(2,1)} collective-permute-done((bf16[4,512,640]{2,1,0:T(8,128)(2,1)}, bf16[4,512,640]{2,1,0:T(8,128)(2,1)}, u32[]{:S(2)}, u32[]{:S(2)}) %collective-permute-start.19) | collective-permute-done | bytes 2621472 | tf_op jit(solution)/shard_map/ppermute | solution.py:398
  284.4 2.9 all-to-all-done.3.sums_ref
  287.3 1.3 copy-done.7
  288.6 7.6 %add_all.1 = (f32[4,512,512]{2,1,0:T(8,128)}, f32[4,512,128]{2,1,0:T(8,128)}) custom-call(s32[14]{0:T(128)} %copy-done.5, bf16[4,512,640]{2,1,0:T(8,128)(2,1)} %get-tuple-element.14.own_ref, bf16[4,512,640]{2,1,0:T(8,128)(2,1)} %collective-permute-done.19.below_ref, bf16[4,512,640]{2,1,0:T(8,128)(2,1)} %collective-permute-done.20.above_ref, ...), custom_call_target="tpu_custom_call" | custom-call | bytes 1024 | tf_op jit(solution)/shard_map/add_all/pallas_call | solution.py:32
  (63 shorter events, 0.3 us)
Async XLA Ops:
  0.6 76.0 %copy-start = (f32[128,512]{1,0:T(8,128)S(1)}, f32[128,512]{1,0:T(8,128)}, u32[]{:S(2)}) copy-start(f32[128,512]{1,0:T(8,128)} %param.7) | copy-start | bytes 786436
  0.8 1.6 copy-start.2
  2.4 3.1 %copy-start.5 = (s32[14]{0:T(128)}, s32[14]{0:T(128)S(1)}, u32[]{:S(2)}) copy-start(s32[14]{0:T(128)S(1)} %concatenate.14.place_ref) | copy-start | bytes 172
  4.2 1.3 copy-start.4
  5.5 12.0 %copy-start.3 = (bf16[4,512,512]{2,1,0:T(8,128)(2,1)S(1)}, bf16[4,512,512]{2,1,0:T(8,128)(2,1)}, u32[]{:S(2)}) copy-start(bf16[4,512,512]{2,1,0:T(8,128)(2,1)} %refs_0_.1) | copy-start | bytes 6291460
  5.5 49.6 %all-to-all-start = ((bf16[128,4,16,128]{3,2,1,0:T(8,128)(2,1)}), bf16[128,4,16,128]{3,2,1,0:T(8,128)(2,1)}, u32[]{:S(2)}, u32[]{:S(2)}) async-start(bf16[128,4,16,128]{3,2,1,0:T(8,128)(2,1)} %copy-done.4), calls=%async_computation | async-start | bytes 4194304 | tf_op jit(solution)/shard_map/all_to_all | solution.py:404
  17.5 4.6 %copy-start.14 = (s32[16,2]{0,1:T(2,128)S(1)}, s32[16,2]{0,1:T(2,128)}, u32[]{:S(2)}) copy-start(s32[16,2]{0,1:T(2,128)} %param.9) | copy-start | bytes 388
  18.8 34.3 %collective-permute-start.8 = (bf16[1,512,512]{2,1,0:T(8,128)(2,1)}, bf16[1,512,512]{2,1,0:T(8,128)(2,1)S(1)}, u32[]{:S(2)}, u32[]{:S(2)}) collective-permute-start(bf16[1,512,512]{2,1,0:T(8,128)(2,1)} %get-tuple-element.28), channel_id=1, source_target_pairs={{0,3},{1,0},{2,1},{3,2},{4,7},{5,4},{6,5},{7,6},{8,11},{9,8},{10,9... | collective-permute-start | bytes 1572872 | tf_op jit(solution)/shard_map/ppermute | solution.py:398
  22.1 33.0 %collective-permute-start.7 = (bf16[1,512,512]{2,1,0:T(8,128)(2,1)}, bf16[1,512,512]{2,1,0:T(8,128)(2,1)S(1)}, u32[]{:S(2)}, u32[]{:S(2)}) collective-permute-start(bf16[1,512,512]{2,1,0:T(8,128)(2,1)} %get-tuple-element.29), channel_id=1, source_target_pairs={{0,1},{1,2},{2,3},{3,0},{4,5},{5,6},{6,7},{7,4},{8,9},{9,10},{10,1... | collective-permute-start | bytes 1572872 | tf_op jit(solution)/shard_map/ppermute | solution.py:398
  22.2 1.5 collective-permute-start
  23.8 17.3 %collective-permute-start.3 = (s32[2,128]{1,0:T(2,128)S(1)}, s32[2,128]{1,0:T(2,128)S(1)}, u32[]{:S(2)}, u32[]{:S(2)}) collective-permute-start(s32[2,128]{1,0:T(2,128)S(1)} %pad_add_fusion), channel_id=1, source_target_pairs={{0,24},{4,28},{8,0},{12,4},{16,8},{20,12},{24,16},{28,20},{32,56},... | collective-permute-start | bytes 3080 | tf_op jit(solution)/shard_map/ppermute | solution.py:416
  26.2 16.4 %collective-permute-start.2 = (s32[2,128]{1,0:T(2,128)S(1)}, s32[2,128]{1,0:T(2,128)S(1)}, u32[]{:S(2)}, u32[]{:S(2)}) collective-permute-start(s32[2,128]{1,0:T(2,128)S(1)} %pad_add_fusion), channel_id=1, source_target_pairs={{0,16},{4,20},{8,24},{12,28},{16,0},{20,4},{24,8},{28,12},{32,48},... | collective-permute-start | bytes 3080 | tf_op jit(solution)/shard_map/ppermute | solution.py:416
  26.8 15.8 %collective-permute-start.1 = (s32[2,128]{1,0:T(2,128)S(1)}, s32[2,128]{1,0:T(2,128)S(1)}, u32[]{:S(2)}, u32[]{:S(2)}) collective-permute-start(s32[2,128]{1,0:T(2,128)S(1)} %pad_add_fusion), channel_id=1, source_target_pairs={{0,8},{4,12},{8,16},{12,20},{16,24},{20,28},{24,0},{28,4},{32,40},... | collective-permute-start | bytes 3080 | tf_op jit(solution)/shard_map/ppermute | solution.py:416
  42.6 3.6 %collective-permute-start.6 = (s32[8,128]{1,0:T(8,128)S(1)}, s32[8,128]{1,0:T(8,128)S(1)}, u32[]{:S(2)}, u32[]{:S(2)}) collective-permute-start(s32[8,128]{1,0:T(8,128)S(1)} %concatenate.16), channel_id=1, source_target_pairs={{0,96},{4,100},{8,104},{12,108},{16,112},{20,116},{24,120},{28,124... | collective-permute-start | bytes 12296 | tf_op jit(solution)/shard_map/ppermute | solution.py:416
  45.2 4.0 %collective-permute-start.5 = (s32[8,128]{1,0:T(8,128)S(1)}, s32[8,128]{1,0:T(8,128)S(1)}, u32[]{:S(2)}, u32[]{:S(2)}) collective-permute-start(s32[8,128]{1,0:T(8,128)S(1)} %concatenate.16), channel_id=1, source_target_pairs={{0,64},{4,68},{8,72},{12,76},{16,80},{20,84},{24,88},{28,92},{32,9... | collective-permute-start | bytes 12296 | tf_op jit(solution)/shard_map/ppermute | solution.py:416
  45.7 4.0 %collective-permute-start.4 = (s32[8,128]{1,0:T(8,128)S(1)}, s32[8,128]{1,0:T(8,128)S(1)}, u32[]{:S(2)}, u32[]{:S(2)}) collective-permute-start(s32[8,128]{1,0:T(8,128)S(1)} %concatenate.16), channel_id=1, source_target_pairs={{0,32},{4,36},{8,40},{12,44},{16,48},{20,52},{24,56},{28,60},{32,6... | collective-permute-start | bytes 12296 | tf_op jit(solution)/shard_map/ppermute | solution.py:416
  53.1 2.0 copy-start.8
  55.1 0.8 copy-start.10
  60.8 67.2 %all-to-all-start.1 = ((bf16[32,32,16,128]{3,2,1,0:T(8,128)(2,1)}), bf16[32,32,16,128]{3,2,1,0:T(8,128)(2,1)}, u32[]{:S(2)}, u32[]{:S(2)}) async-start(bf16[32,32,16,128]{3,2,1,0:T(8,128)(2,1)} %pick_pieces.1), calls=%async_computation.1 | async-start | bytes 8388608 | tf_op jit(solution)/shard_map/all_to_all | solution.py:401
  67.7 6.9 %copy-start.6 = (f32[128]{0:T(128)S(1)}, f32[128]{0:T(128)}, u32[]{:S(2)}) copy-start(f32[128]{0:T(128)} %param.6) | copy-start | bytes 1540
  67.7 7.6 %copy-start.17 = (s32[128]{0:T(128)S(1)}, s32[128]{0:T(128)}, u32[]{:S(2)}) copy-start(s32[128]{0:T(128)} %param.8) | copy-start | bytes 1540
  67.7 14.8 %collective-permute-start.11 = (bf16[1,512,512]{2,1,0:T(8,128)(2,1)}, bf16[1,512,512]{2,1,0:T(8,128)(2,1)}, u32[]{:S(2)}, u32[]{:S(2)}) collective-permute-start(bf16[1,512,512]{2,1,0:T(8,128)(2,1)} %get-tuple-element.26), channel_id=1, source_target_pairs={{0,1},{1,2},{2,3},{3,0},{4,5},{5,6},{6,7},{7,4},{8,9},{9,10},{10,1... | collective-permute-start | bytes 1572872 | tf_op jit(solution)/shard_map/ppermute | solution.py:398
  67.9 14.7 %copy-start.9 = (bf16[1,512,512]{2,1,0:T(8,128)(2,1)S(1)}, bf16[1,512,512]{2,1,0:T(8,128)(2,1)}, u32[]{:S(2)}) copy-start(bf16[1,512,512]{2,1,0:T(8,128)(2,1)} %copy-done.8) | copy-start | bytes 1572868
  67.9 17.5 %copy-start.11 = (bf16[1,512,512]{2,1,0:T(8,128)(2,1)S(1)}, bf16[1,512,512]{2,1,0:T(8,128)(2,1)}, u32[]{:S(2)}) copy-start(bf16[1,512,512]{2,1,0:T(8,128)(2,1)} %copy-done.10) | copy-start | bytes 1572868
  67.9 17.5 %collective-permute-start.10 = (bf16[1,512,512]{2,1,0:T(8,128)(2,1)}, bf16[1,512,512]{2,1,0:T(8,128)(2,1)}, u32[]{:S(2)}, u32[]{:S(2)}) collective-permute-start(bf16[1,512,512]{2,1,0:T(8,128)(2,1)} %get-tuple-element.27), channel_id=1, source_target_pairs={{0,3},{1,0},{2,1},{3,2},{4,7},{5,4},{6,5},{7,6},{8,11},{9,8},{10,9... | collective-permute-start | bytes 1572872 | tf_op jit(solution)/shard_map/ppermute | solution.py:398
  71.9 56.1 %collective-permute-start.12 = (bf16[2,512,512]{2,1,0:T(8,128)(2,1)}, bf16[2,512,512]{2,1,0:T(8,128)(2,1)S(1)}, u32[]{:S(2)}, u32[]{:S(2)}) collective-permute-start(bf16[2,512,512]{2,1,0:T(8,128)(2,1)} %get-tuple-element.24), channel_id=1, source_target_pairs={{0,1},{1,2},{2,3},{3,0},{4,5},{5,6},{6,7},{7,4},{8,9},{9,10},{10,1... | collective-permute-start | bytes 3145736 | tf_op jit(solution)/shard_map/ppermute | solution.py:398
  71.9 56.1 %collective-permute-start.9 = (bf16[2,512,512]{2,1,0:T(8,128)(2,1)}, bf16[2,512,512]{2,1,0:T(8,128)(2,1)}, u32[]{:S(2)}, u32[]{:S(2)}) collective-permute-start(bf16[2,512,512]{2,1,0:T(8,128)(2,1)} %get-tuple-element.25), channel_id=1, source_target_pairs={{0,3},{1,0},{2,1},{3,2},{4,7},{5,4},{6,5},{7,6},{8,11},{9,8},{10,9... | collective-permute-start | bytes 3145736 | tf_op jit(solution)/shard_map/ppermute | solution.py:398
  82.5 33.6 %collective-permute-start.14 = (bf16[1,512,512]{2,1,0:T(8,128)(2,1)}, bf16[1,512,512]{2,1,0:T(8,128)(2,1)S(1)}, u32[]{:S(2)}, u32[]{:S(2)}) collective-permute-start(bf16[1,512,512]{2,1,0:T(8,128)(2,1)} %collective-permute-done.11.refs_5_), channel_id=1, source_target_pairs={{0,1},{1,2},{2,3},{3,0},{4,5},{5,6},{6,7},{7,4},{8,9},{9,10},{10,1... | collective-permute-start | bytes 1572872 | tf_op jit(solution)/shard_map/ppermute | solution.py:398
  82.7 45.3 %collective-permute-start.16 = (bf16[1,512,512]{2,1,0:T(8,128)(2,1)S(1)}, bf16[1,512,512]{2,1,0:T(8,128)(2,1)}, u32[]{:S(2)}, u32[]{:S(2)}) collective-permute-start(bf16[1,512,512]{2,1,0:T(8,128)(2,1)S(1)} %copy-done.9), channel_id=1, source_target_pairs={{0,3},{1,0},{2,1},{3,2},{4,7},{5,4},{6,5},{7,6},{8,11},{9,8},{10,9... | collective-permute-start | bytes 1572872 | tf_op jit(solution)/shard_map/ppermute | solution.py:398
  85.4 42.6 %collective-permute-start.13 = (bf16[1,512,512]{2,1,0:T(8,128)(2,1)S(1)}, bf16[1,512,512]{2,1,0:T(8,128)(2,1)}, u32[]{:S(2)}, u32[]{:S(2)}) collective-permute-start(bf16[1,512,512]{2,1,0:T(8,128)(2,1)S(1)} %copy-done.11), channel_id=1, source_target_pairs={{0,1},{1,2},{2,3},{3,0},{4,5},{5,6},{6,7},{7,4},{8,9},{9,10},{10,1... | collective-permute-start | bytes 1572872 | tf_op jit(solution)/shard_map/ppermute | solution.py:398
  116.1 1.9 copy-start.13
  116.1 11.9 %collective-permute-start.15 = (bf16[1,512,512]{2,1,0:T(8,128)(2,1)}, bf16[1,512,512]{2,1,0:T(8,128)(2,1)}, u32[]{:S(2)}, u32[]{:S(2)}) collective-permute-start(bf16[1,512,512]{2,1,0:T(8,128)(2,1)} %collective-permute-done.10.refs_2_), channel_id=1, source_target_pairs={{0,3},{1,0},{2,1},{3,2},{4,7},{5,4},{6,5},{7,6},{8,11},{9,8},{10,9... | collective-permute-start | bytes 1572872 | tf_op jit(solution)/shard_map/ppermute | solution.py:398
  128.0 1.0 copy-start.12
  157.9 10.0 %copy-start.16 = (bf16[2,512,640]{2,1,0:T(8,128)(2,1)S(1)}, bf16[2,512,640]{2,1,0:T(8,128)(2,1)}, u32[]{:S(2)}) copy-start(bf16[2,512,640]{2,1,0:T(8,128)(2,1)} %get-tuple-element.17) | copy-start | bytes 3932164
  157.9 10.1 %copy-start.15 = (bf16[2,512,640]{2,1,0:T(8,128)(2,1)S(1)}, bf16[2,512,640]{2,1,0:T(8,128)(2,1)}, u32[]{:S(2)}) copy-start(bf16[2,512,640]{2,1,0:T(8,128)(2,1)} %get-tuple-element.18) | copy-start | bytes 3932164
  157.9 60.2 %all-to-all-start.2 = ((bf16[32,32,16,128]{3,2,1,0:T(8,128)(2,1)}), bf16[32,32,16,128]{3,2,1,0:T(8,128)(2,1)}, u32[]{:S(2)}, u32[]{:S(2)}) async-start(bf16[32,32,16,128]{3,2,1,0:T(8,128)(2,1)} %get-tuple-element.21), calls=%async_computation.2 | async-start | bytes 8388608 | tf_op jit(solution)/shard_map/all_to_all | solution.py:401
  167.9 31.4 %collective-permute-start.17 = (bf16[2,512,640]{2,1,0:T(8,128)(2,1)S(1)}, bf16[2,512,640]{2,1,0:T(8,128)(2,1)S(1)}, u32[]{:S(2)}, u32[]{:S(2)}) collective-permute-start(bf16[2,512,640]{2,1,0:T(8,128)(2,1)S(1)} %copy-done.16), channel_id=1, source_target_pairs={{0,1},{1,2},{2,3},{3,0},{4,5},{5,6},{6,7},{7,4},{8,9},{9,10},{10,1... | collective-permute-start | bytes 3932168 | tf_op jit(solution)/shard_map/ppermute | solution.py:398
  168.0 31.4 %collective-permute-start.18 = (bf16[2,512,640]{2,1,0:T(8,128)(2,1)S(1)}, bf16[2,512,640]{2,1,0:T(8,128)(2,1)S(1)}, u32[]{:S(2)}, u32[]{:S(2)}) collective-permute-start(bf16[2,512,640]{2,1,0:T(8,128)(2,1)S(1)} %copy-done.15), channel_id=1, source_target_pairs={{0,3},{1,0},{2,1},{3,2},{4,7},{5,4},{6,5},{7,6},{8,11},{9,8},{10,9... | collective-permute-start | bytes 3932168 | tf_op jit(solution)/shard_map/ppermute | solution.py:398
  202.3 78.7 %collective-permute-start.20 = (bf16[4,512,640]{2,1,0:T(8,128)(2,1)}, bf16[4,512,640]{2,1,0:T(8,128)(2,1)}, u32[]{:S(2)}, u32[]{:S(2)}) collective-permute-start(bf16[4,512,640]{2,1,0:T(8,128)(2,1)} %get-tuple-element.20), channel_id=1, source_target_pairs={{0,3},{1,0},{2,1},{3,2},{4,7},{5,4},{6,5},{7,6},{8,11},{9,8},{10,9... | collective-permute-start | bytes 7864328 | tf_op jit(solution)/shard_map/ppermute | solution.py:398
  204.7 79.7 %collective-permute-start.19 = (bf16[4,512,640]{2,1,0:T(8,128)(2,1)}, bf16[4,512,640]{2,1,0:T(8,128)(2,1)}, u32[]{:S(2)}, u32[]{:S(2)}) collective-permute-start(bf16[4,512,640]{2,1,0:T(8,128)(2,1)} %get-tuple-element.19.refs_0_), channel_id=1, source_target_pairs={{0,1},{1,2},{2,3},{3,0},{4,5},{5,6},{6,7},{7,4},{8,9},{9,10},{10,1... | collective-permute-start | bytes 7864328 | tf_op jit(solution)/shard_map/ppermute | solution.py:398
  224.2 63.2 %all-to-all-start.3 = ((bf16[128,4,16,128]{3,2,1,0:T(8,128)(2,1)}), bf16[128,4,16,128]{3,2,1,0:T(8,128)(2,1)S(1)}, u32[]{:S(2)}, u32[]{:S(2)}) async-start(bf16[128,4,16,128]{3,2,1,0:T(8,128)(2,1)} %sum_returned.1), calls=%async_computation.3 | async-start | bytes 4194304 | tf_op jit(solution)/shard_map/all_to_all | solution.py:404
  287.3 1.3 copy-start.7
  287.3 8.9 %copy-start.1 = (f32[128,512]{1,0:T(8,128)S(1)}, f32[128,512]{1,0:T(8,128)}, u32[]{:S(2)}) copy-start(f32[128,512]{1,0:T(8,128)} %param.7) | copy-start | bytes 786436
